TPU v7x, 32 devices: a whole 2x2x4 slice. The times are simulated.
32 devices in a mesh: section: 4 (over y, core), expert: 8 (over z, x).
Axes of the slice: x: 2, y: 2, z: 4, core: 2. Of those that a mesh axis runs over, the one named last changes fastest.
Arguments:
- tokens: bfloat16 [4, 512, 2560], P('section', 'expert'), may hold values from -6 to 6
- norm_gain: float32 [4, 2560], P('section'), may hold values from 0.25 to 1.75
- w_gate: bfloat16 [4, 8, 2560, 192], P('section', 'expert'), may hold values from -0.125 to 0.125
- w_up: bfloat16 [4, 8, 2560, 192], P('section', 'expert'), may hold values from -0.125 to 0.125
- w_down: bfloat16 [4, 8, 192, 2560], P('section', 'expert'), may hold values from -0.21875 to 0.21875
- routes: int32 [4, 2, 512, 1], P('section', None, 'expert'), may hold values from 0 to 1; in each aligned block of 64 rows (0 to 63, 64 to 127, ..., all dimensions but the last counted through in order) at most 34 rows name the same one
- mix_weights: float32 [4, 2, 512, 1], P('section', None, 'expert'), may hold values from 0.1 to 1
- cotangent: bfloat16 [4, 512, 2560], P('section', 'expert'), may hold values from -6 to 6
Outputs:
- final: bfloat16 [4, 512, 2560], P('section', 'expert')
- input_grads: bfloat16 [4, 512, 2560], P('section', 'expert')
Inputs may be any that keep to these rules, and one draw needn't show every extreme that they name: `routes`: the 1 ids of a token differ. In the rows of one device (aligned blocks of 64 tokens of one layer and step) no id is named by more than 34 tokens, a bound that some block reaches.
All inputs are finite; a program needn't handle non-finite values.
Results may differ from a plain program's by a relative error of at most 0.011.
Values may be sent and summed in bfloat16 or wider, within the bound.
No kernel may reach another device: no remote copies, remote signals or barrier semaphores. Data moves between devices by JAX's collectives and lax.ppermute only.
A program may use at most 64 MiB of HBM per device.

v0:
```python
import functools

import jax
import jax.numpy as jnp
from jax import lax
from jax.experimental import pallas as pl
from jax.experimental.pallas import tpu as pltpu
from jax.sharding import PartitionSpec as P

SPLIT = 4
EPSILON = 1e-06
BF = jnp.bfloat16
F32 = jnp.float32
ROWS = 16
LANES = 128


def dot(left, right, dims=((1,), (0,))):
    return lax.dot_general(left, right, (dims, ((), ())), preferred_element_type=F32)


NT = ((1,), (1,))


def iota(shape, axis):
    return lax.broadcasted_iota(jnp.int32, shape, axis)


class Box:
    def __init__(self, capacity, width):
        self.capacity, self.width = capacity, width
        self.groups, self.extra = capacity // ROWS, capacity % ROWS
        self.cuts = ROWS // self.extra if self.extra else 1
        self.wide = -(-width // (LANES * self.cuts)) * LANES if self.extra else 0
        self.lanes = self.groups * width + self.wide
        self.pieces = -(-width // self.wide) if self.extra else 0

    def group(self, g):
        return pl.ds(g * self.width, self.width)

    def tail(self):
        return pl.ds(self.groups * self.width, self.wide)

    def piece(self, i):
        return i * self.wide, min(self.wide, self.width - i * self.wide)


def shift(value, sections=0, experts=0, flip=0):
    n_sec, n_own = lax.axis_size("section"), lax.axis_size("expert")
    n_exp = n_own // SPLIT
    if sections % n_sec == 0 and experts % n_exp == 0 and flip == 0:
        return value
    pairs = []
    for sec in range(n_sec):
        for own in range(n_own):
            exp, sl = own // SPLIT, own % SPLIT
            to = ((exp + experts) % n_exp) * SPLIT + (sl ^ flip)
            pairs.append((sec * n_own + own, ((sec + sections) % n_sec) * n_own + to))
    return lax.ppermute(value, ("section", "expert"), pairs)


def call(body, outs, *operands, scratch=(), flops=0, after=()):
    moved = sum(a.size * a.dtype.itemsize for a in operands)
    moved += sum(o.size * o.dtype.itemsize for o in outs)
    vmem = pl.BlockSpec(memory_space=pltpu.VMEM)
    read = len(operands)

    def reading(*refs):
        body(*refs[:read], *refs[read + len(after) :])

    return pl.pallas_call(
        reading,
        out_shape=list(outs),
        in_specs=[vmem] * read + [pl.BlockSpec(memory_space=pl.ANY)] * len(after),
        out_specs=[vmem] * len(outs),
        scratch_shapes=list(scratch),
        compiler_params=pltpu.CompilerParams(vmem_limit_bytes=40 * 2**20),
        cost_estimate=pl.CostEstimate(flops=flops, bytes_accessed=moved, transcendentals=0),
    )(*operands, *after)


def column_of(row):
    n = row.shape[1]
    eye = iota((n, n), 0) == iota((n, n), 1)
    return jnp.sum(jnp.where(eye, row, 0.0), axis=1, keepdims=True)


def slots_of(rel, experts, capacity):
    n = rel.shape[1]
    same = jnp.broadcast_to(column_of(rel), (n, n)) == jnp.broadcast_to(rel, (n, n))
    before = iota((n, n), 0) < iota((n, n), 1)
    rank = jnp.sum(jnp.where(same & before, 1.0, 0.0), axis=0, keepdims=True)
    return rel * capacity + rank


def terms(value):
    high = value.astype(BF).astype(F32)
    middle = (value - high).astype(BF).astype(F32)
    return high, middle, value - high - middle


def notes_of(slots, mix, gain, n, width):
    r = iota((ROWS, n), 0)
    left = jnp.where(r == 0, slots, 0.0)
    for at, term in enumerate(terms(mix)):
        left = jnp.where(r == 1 + at, term, left)
    r = iota((ROWS, width), 0)
    wide = jnp.concatenate([left, jnp.zeros((ROWS, width - n), F32)], axis=1)
    for at, term in enumerate(terms(gain)):
        wide = jnp.where(r == 4 + at, term, wide)
    return wide.astype(BF)


def slots_in(notes, n):
    return notes[:, :n].astype(F32)[0:1]


def mix_in(notes, n):
    left = notes[:, :n].astype(F32)
    return column_of(left[1:2] + left[2:3] + left[3:4])


def gain_in(notes):
    wide = notes.astype(F32)
    return wide[4:5] + wide[5:6] + wide[6:7]


def pack_rows(box, slots, values, out_refs):
    n = values.shape[0]
    line = jnp.broadcast_to(slots.astype(jnp.int32), (ROWS, n))
    r = iota((ROWS, n), 0)
    for j, out in enumerate(out_refs):
        first = j * box.capacity
        for g in range(box.groups):
            sel = jnp.where(line == first + g * ROWS + r, 1.0, 0.0).astype(BF)
            out[:, box.group(g)] = dot(sel, values).astype(BF)
        if box.extra:
            total = jnp.zeros((ROWS, box.wide), F32)
            for i in range(box.pieces):
                at, size = box.piece(i)
                hit = (line == first + box.groups * ROWS + r // box.cuts) & (r % box.cuts == i)
                hit &= r // box.cuts < box.extra
                got = dot(jnp.where(hit, 1.0, 0.0).astype(BF), values[:, at : at + size])
                if size < box.wide:
                    got = jnp.concatenate([got, jnp.zeros((ROWS, box.wide - size), F32)], axis=1)
                total = total + got
            out[:, box.tail()] = total.astype(BF)


def pick_rows(box, slots, boxes, n, picked):
    count = len(boxes)
    slots = column_of(slots)
    if box.groups:
        stack = jnp.concatenate(
            [b[:, g * box.width : (g + 1) * box.width] for b in boxes for g in range(box.groups)],
            axis=0,
        )
        tall = count * box.groups * ROWS
        c = iota((n, tall), 1)
        slot = c // (box.groups * ROWS) * box.capacity + c % (box.groups * ROWS)
        sel = jnp.where(slots.astype(jnp.int32) == slot, 1.0, 0.0).astype(BF)
        picked[...] = dot(sel, stack)
    else:
        picked[...] = jnp.zeros(picked.shape, F32)
    if box.extra:
        tails = jnp.concatenate([b[:, box.groups * box.width :] for b in boxes], axis=0)
        c = iota((n, count * ROWS), 1)
        r = c % ROWS
        slot = c // ROWS * box.capacity + box.groups * ROWS + r // box.cuts
        mine = (slots.astype(jnp.int32) == slot) & (r // box.cuts < box.extra)
        for i in range(box.pieces):
            at, size = box.piece(i)
            sel = jnp.where(mine & (r % box.cuts == i), 1.0, 0.0).astype(BF)
            picked[:, at : at + size] += dot(sel, tails[:, :size])


def heights(box, count):
    extra = -(-count * box.extra // ROWS) * ROWS
    return count * box.groups * ROWS, extra


def unpack(box, refs, stack, tails, at=0):
    count = 0
    for ref in refs:
        for p in range(ref.shape[0] // ROWS):
            for g in range(box.groups):
                stack[at : at + ROWS, :] = ref[p * ROWS : (p + 1) * ROWS, box.group(g)]
                at += ROWS
            if box.extra:
                tails[count * ROWS : (count + 1) * ROWS, :] = ref[
                    p * ROWS : (p + 1) * ROWS, box.tail()
                ]
            count += 1
    if box.extra:
        extra = heights(box, count)[1]
        r = iota((extra, count * ROWS), 0)
        c = iota((extra, count * ROWS), 1)
        mine = (r // box.extra == c // ROWS) & (r % box.extra == c % ROWS // box.cuts)
        for i in range(box.pieces):
            start, size = box.piece(i)
            sel = jnp.where(mine & (c % ROWS % box.cuts == i), 1.0, 0.0).astype(BF)
            stack[at : at + extra, start : start + size] = dot(sel, tails[:, :size]).astype(BF)


def repack(box, rows, refs):
    rows = rows.astype(BF)
    at = 0
    count = 0
    for ref in refs:
        for p in range(ref.shape[0] // ROWS):
            for g in range(box.groups):
                ref[p * ROWS : (p + 1) * ROWS, box.group(g)] = rows[at : at + ROWS]
                at += ROWS
            count += 1
    if box.extra:
        extra = heights(box, count)[1]
        r = iota((count * ROWS, extra), 0)
        c = iota((count * ROWS, extra), 1)
        mine = (c // box.extra == r // ROWS) & (c % box.extra == r % ROWS // box.cuts)
        total = jnp.zeros((count * ROWS, box.wide), F32)
        for i in range(box.pieces):
            start, size = box.piece(i)
            sel = jnp.where(mine & (r % ROWS % box.cuts == i), 1.0, 0.0).astype(BF)
            got = dot(sel, rows[at:, start : start + size])
            if size < box.wide:
                pad = jnp.zeros((count * ROWS, box.wide - size), F32)
                got = jnp.concatenate([got, pad], axis=1)
            total = total + got
        total = total.astype(BF)
        count = 0
        for ref in refs:
            tall = ref.shape[0]
            ref[:, box.tail()] = total[count : count + tall]
            count += tall


def inv_rms(wide):
    return lax.rsqrt(jnp.mean(wide * wide, axis=-1, keepdims=True) + EPSILON)


def total_of(refs):
    return sum(ref[...].astype(F32) for ref in refs).astype(BF)


def start_kernel(box, experts, tokens, cot, gain, ids, mix, ahead, notes0, notes1, *boxes):
    n, width = tokens.shape
    mine = lax.axis_index("expert") // SPLIT
    for k, notes in enumerate((notes0, notes1)):
        rel = ids[k : k + 1, :] - mine
        rel = jnp.where(rel < 0, rel + experts, rel).astype(F32)
        slots = slots_of(rel, experts, box.capacity)
        notes[...] = notes_of(slots, mix[k : k + 1, :], gain[...], n, width)
    ahead[:n] = tokens[...]
    ahead[n:] = notes0[...]
    wide = tokens[...].astype(F32)
    normed = (wide * inv_rms(wide) * gain[...]).astype(BF)
    crossing = boxes[2:]
    firsts = [boxes[0]] + [ref.at[:ROWS] for ref in crossing]
    pack_rows(box, slots_in(notes0[...], n), normed, firsts)
    seconds = [boxes[1]] + [ref.at[ROWS:] for ref in crossing]
    pack_rows(box, slots_in(notes1[...], n), cot[...], seconds)


def combine(box, notes, n, own, back, picked):
    sums = [total_of(own)] + [ref[...] for ref in back]
    pick_rows(box, slots_in(notes, n), sums, n, picked)
    return mix_in(notes, n) * picked[...]


def split_refs(refs, experts, outs):
    ins = refs[:-outs]
    return ins[experts - 1 :], ins[: experts - 1], refs[-outs:]


def middle_kernel(box, experts, arrived, cot, notes1, gain, *refs):
    boxes, picked = refs[-1 - experts : -1], refs[-1]
    own, back, (after, behind) = split_refs(refs[: -1 - experts], experts, 2)
    n = cot.shape[0]
    update = combine(box, arrived[n:], n, own, back, picked)
    later = (arrived[:n].astype(F32) + update).astype(BF)
    after[...] = later
    behind[:n] = later
    behind[n : 2 * n] = cot[...]
    behind[2 * n :] = notes1[...]
    wide = later.astype(F32)
    normed = (wide * inv_rms(wide) * gain[...]).astype(BF)
    pack_rows(box, slots_in(notes1[...], n), normed, boxes)


def final_kernel(box, experts, hidden, notes, *refs):
    picked = refs[-1]
    own, back, (out,) = split_refs(refs[:-1], experts, 1)
    n = hidden.shape[0]
    update = combine(box, notes[...], n, own, back, picked)
    out[...] = (hidden[...].astype(F32) + update).astype(BF)


def norm_back(hidden, gain, grad):
    wide = hidden.astype(F32)
    inv = inv_rms(wide)
    scaled = grad * gain
    along = jnp.mean(scaled * wide, axis=-1, keepdims=True)
    return inv * scaled - wide * (inv * inv * inv * along)


def turn_kernel(box, experts, arrived, notes0, *refs):
    boxes, picked = refs[-1 - experts : -1], refs[-1]
    own, back, (out,) = split_refs(refs[: -1 - experts], experts, 1)
    n = out.shape[0]
    notes = arrived[2 * n :]
    d_normed = combine(box, notes, n, own, back, picked)
    change = norm_back(arrived[:n], gain_in(notes), d_normed)
    now = (arrived[n : 2 * n].astype(F32) + change).astype(BF)
    out[...] = now
    pack_rows(box, slots_in(notes0[...], n), now, boxes)


def last_kernel(box, experts, grad, hidden, notes0, gain, *refs):
    picked = refs[-1]
    own, back, (out,) = split_refs(refs[:-1], experts, 1)
    n = hidden.shape[0]
    d_normed = combine(box, notes0[...], n, own, back, picked)
    change = norm_back(hidden[...], gain[...], d_normed)
    out[...] = (grad[...].astype(F32) + change).astype(BF)


def spans(tall):
    return pl.ds(0, 2 * tall), pl.ds(tall, 2 * tall)


def gate_up(rows, pack):
    return dot(rows, pack[: 2 * (pack.shape[0] // 3)], NT)


def parts_of(both):
    units = both.shape[1] // 2
    return both[:, :units], both[:, units:]


def down_rows(both, pack):
    g, u = parts_of(both)
    return dot((jax.nn.silu(g) * u).astype(BF), pack[2 * g.shape[1] :])


def inner_of(rows, pack):
    return dot(rows, pack[2 * (pack.shape[0] // 3) :], NT)


def part_rows(d_inner, both, pack):
    g, u = parts_of(both)
    r = jax.nn.sigmoid(g)
    d_gate = d_inner * u * r * (1.0 + g * (1.0 - r))
    d_up = d_inner * g * r
    return dot(jnp.concatenate([d_gate, d_up], axis=1).astype(BF), pack[: both.shape[1]])


def read_rows(box, rows, stack, tails):
    tall = stack.shape[0] // 3
    for at, ref in enumerate(rows):
        unpack(box, [ref], stack, tails, at * tall)
    return [stack[span, :] for span in spans(tall)]


def write_rows(box, top, bottom, outs):
    tall = top.shape[0] // 2
    for ref, value in zip(outs, (top[:tall], top[tall:] + bottom[:tall], bottom[tall:])):
        repack(box, value, [ref])


def forward_kernel(box, packs, saved, rows, outs, kept, stack, tails):
    sides = read_rows(box, rows, stack, tails)
    total = []
    for side, values in enumerate(sides):
        total.append(0.0)
        for at in (2 * side, 2 * side + 1):
            both = gate_up(values, packs[at])
            kept[at][...] = both
            total[side] = total[side] + down_rows(both, packs[at])
    write_rows(box, *total, outs)


def inner_kernel(box, packs, saved, rows, outs, kept, stack, tails):
    for side, values in enumerate(read_rows(box, rows, stack, tails)):
        for at in (2 * side, 2 * side + 1):
            kept[at][...] = inner_of(values, packs[at])


def gate_back_kernel(box, packs, saved, rows, outs, kept, stack, tails):
    sides = read_rows(box, rows, stack, tails)
    total = []
    for side, values in enumerate(sides):
        total.append(0.0)
        for at in (2 * side, 2 * side + 1):
            both = gate_up(values, packs[at])
            kept[at][...] = both
            total[side] = total[side] + part_rows(saved[at][...], both, packs[at])
    write_rows(box, *total, outs)


def back_kernel(box, packs, saved, rows, outs, kept, stack, tails):
    sides = read_rows(box, rows, stack, tails)
    total = []
    for side, values in enumerate(sides):
        total.append(0.0)
        for at in (2 * side, 2 * side + 1):
            d_inner = inner_of(values, packs[at])
            total[side] = total[side] + part_rows(d_inner, saved[at][...], packs[at])
    write_rows(box, *total, outs)


def down_kernel(box, packs, saved, rows, outs, kept, stack, tails):
    total = []
    for side in range(2):
        at = 2 * side
        total.append(sum(down_rows(saved[i][...], packs[i]) for i in (at, at + 1)))
    write_rows(box, *total, outs)


def expert_call(kernel, box, packs, rows, saved=(), outs=True, kept=0, reads=True, after=(), window=None):
    width = packs[0].shape[1]
    first, size = window or (0, rows[0].shape[0])
    count = size // ROWS
    tall = sum(heights(box, count))
    boxes = jax.ShapeDtypeStruct((count * ROWS, box.lanes), BF)
    results = [boxes] * len(rows) if outs else []
    if kept:
        units = [pack.shape[0] // 3 for pack in packs]
        results += [jax.ShapeDtypeStruct((2 * tall, kept * u), F32) for u in units]
    inputs = list(packs) + list(saved) + (list(rows) if reads else [])
    n_in, n_p, n_s, n_out = len(inputs), len(packs), len(saved), len(rows) if outs else 0

    def body(*refs):
        results_refs = refs[n_in:-2]
        kernel(
            box,
            refs[:n_p],
            refs[n_p : n_p + n_s],
            [ref.at[pl.ds(first, size)] for ref in refs[n_p + n_s : n_in]],
            results_refs[:n_out],
            results_refs[n_out:],
            refs[-2],
            refs[-1],
        )

    scratch = [
        pltpu.VMEM((3 * tall, width), BF),
        pltpu.VMEM((count * ROWS, max(box.wide, LANES)), BF),
    ]
    flops = sum(2 * 2 * tall * pack.size for pack in packs)
    results = call(body, results, *inputs, scratch=scratch, flops=flops, after=after)
    return results[:n_out], results[n_out:]


def local(tokens, norm_gain, w_gate, w_up, w_down, routes, mix_weights, cotangent):
    experts = lax.axis_size("expert") // SPLIT
    n, width = tokens.shape[1:]
    capacity = n // experts + max(1, n // (16 * experts))
    box = Box(capacity, width)
    gain = norm_gain
    gate_w, up_w, down_w = w_gate[0, 0].T, w_up[0, 0].T, w_down[0, 0]
    boxed = jax.ShapeDtypeStruct((ROWS, box.lanes), BF)
    picked = pltpu.VMEM((n, width), F32)
    bind = functools.partial

    def joined(arrays):
        return arrays[0] if len(arrays) == 1 else jnp.concatenate(arrays, axis=0)

    fence = lax.optimization_barrier

    def crossing_of(boxes):
        return joined([shift(boxes[j - 1], experts=j) for j in range(1, experts)])

    def around(boxes):
        return [shift(boxes, flip=2), boxes, shift(boxes, flip=1)]

    def add(*values):
        return sum(v.astype(F32) for v in values).astype(BF)

    def sums(parts):
        return add(parts[1], shift(parts[0], flip=2), shift(parts[2], flip=1))

    def home(total, sections):
        return [
            shift(total[(j - 1) * ROWS : j * ROWS], sections=sections, experts=-j)
            for j in range(1, experts)
        ]

    def own_home(parts, sections):
        return [
            shift(parts[0], sections=sections, flip=2),
            shift(parts[2], sections=sections, flip=1),
            shift(parts[1], sections=sections),
        ]

    def give_back(cross, own, sections):
        total, own = fence((sums(cross), own))
        return home(total, sections) + own_home(own, sections)

    units = w_gate.shape[3]
    cut = -(-units * 7 // 12 // ROWS) * ROWS
    top = jnp.concatenate([gate_w[:cut], up_w[:cut], down_w[:cut]], axis=0)
    bottom = jnp.concatenate([gate_w[cut:], up_w[cut:], down_w[cut:]], axis=0)
    packs = [top, shift(top, flip=1), bottom, shift(bottom, flip=2)]

    def rows_of(count):
        return jax.ShapeDtypeStruct((count, width), BF)

    both = jax.ShapeDtypeStruct((2 * ROWS, box.lanes), BF)
    ahead, notes0, notes1, own_tok, own_cot, *crossing = call(
        bind(start_kernel, box, experts),
        [rows_of(n + ROWS), rows_of(ROWS), rows_of(ROWS), boxed, boxed] + [both] * (experts - 1),
        tokens[0],
        cotangent[0],
        gain,
        routes[0, :, :, 0],
        mix_weights[0, :, :, 0],
        after=[top, bottom],
    )
    crossed = [shift(crossing[j - 1], experts=j) for j in range(1, experts)]
    own0 = around(own_tok)
    packs, crossed, own0 = fence((packs, crossed, own0))
    cross0 = around(joined([c[:ROWS] for c in crossed]))
    cots = around(joined([own_cot] + [c[ROWS:] for c in crossed]))

    own_out, own_kept0 = expert_call(forward_kernel, box, packs, own0, kept=2)
    cross_out, cross_kept0 = expert_call(
        forward_kernel, box, packs, cross0, kept=2, after=own_out[:1]
    )
    cross_out, cots, ahead = fence((cross_out, cots, ahead))
    arrived0 = shift(ahead, sections=1)
    got = give_back(cross_out, own_out, 1)
    h1, behind, own1, *boxes1 = call(
        bind(middle_kernel, box, experts),
        [rows_of(n), rows_of(2 * n + ROWS)] + [boxed] * experts,
        arrived0,
        cotangent[0],
        notes1,
        gain,
        *got,
        scratch=[picked],
    )
    cross1, own_z, own_x = fence(
        (crossing_of(boxes1), shift(own1, flip=2), shift(own1, flip=1))
    )
    cross1, own1 = around(cross1), [own_z, own1, own_x]
    inner = bind(expert_call, inner_kernel, box, packs, cots, outs=False, kept=1)
    own_di = inner(window=(0, ROWS))[1]
    cross_di = inner(window=(ROWS, (experts - 1) * ROWS))[1]

    gate_back = bind(expert_call, gate_back_kernel, box, packs, kept=2)
    own_grad, own_kept1 = gate_back(own1, own_di)
    cross_grad, cross_kept1 = gate_back(cross1, cross_di, after=own_grad[:1])
    down = bind(expert_call, down_kernel, box, packs, reads=False)
    cross_fin = down(cross1, cross_kept1)[0]
    arrived1 = shift(behind, sections=-1)
    total = sums(cross_grad)
    back_grad = home(total, -1)
    own_grad, fin_sums = fence((own_grad, sums(cross_fin)))
    got = back_grad + own_home(own_grad, -1)
    fin_back = home(fin_sums, 0)
    own_fin = down(own1, own_kept1)[0]
    g1, own_g, *boxes_g = call(
        bind(turn_kernel, box, experts),
        [rows_of(n)] + [boxed] * experts,
        arrived1,
        notes0,
        *got,
        scratch=[picked],
    )

    cross_g, own_g, fin_back = fence((crossing_of(boxes_g), own_g, fin_back))
    cross_g, own_g = around(cross_g), around(own_g)
    back = bind(expert_call, back_kernel, box, packs)
    cross_grad = back(cross_g, cross_kept0)[0]
    own_grad = back(own_g, own_kept0, after=cross_grad[:1])[0]
    total, own_grad, own_fin = fence((sums(cross_grad), own_grad, own_fin))
    got = home(total, 0) + own_home(own_grad, 0)
    fin_own = own_home(own_fin, 0)
    (g0,) = call(
        bind(last_kernel, box, experts),
        [rows_of(n)],
        g1,
        tokens[0],
        notes0,
        gain,
        *got,
        scratch=[picked],
    )
    (final,) = call(
        bind(final_kernel, box, experts),
        [rows_of(n)],
        h1,
        notes1,
        *fin_back,
        *fin_own,
        scratch=[picked],
    )
    return (final[None], g0[None])


def solution(mesh):
    in_specs = (
        P("section", "expert", None),
        P("section", None),
        P("section", "expert", None, None),
        P("section", "expert", None, None),
        P("section", "expert", None, None),
        P("section", None, "expert", None),
        P("section", None, "expert", None),
        P("section", "expert", None),
    )
    out_specs = (P("section", "expert", None), P("section", "expert", None))
    return jax.shard_map(local, mesh=mesh, in_specs=in_specs, out_specs=out_specs, check_vma=False)
```

profile of v0, /device:TPU:0, one launch (start us, length us, event | category | flops | bytes accessed | tf_op | source)
XLA Modules:
  0.0 171.0 jit_solution(7394896899641874927)
XLA Ops:
  0.6 1.2 slice.40
  1.8 1.1 slice.41
  3.1 3.0 %collective-permute-start = (bf16[336,2560]{1,0:T(8,128)(2,1)S(1)}, bf16[336,2560]{1,0:T(8,128)(2,1)S(1)}, u32[]{:S(2)}, u32[]{:S(2)}) collective-permute-start(bf16[336,2560]{1,0:T(8,128)(2,1)S(1)} %pad_maximum_fusion.refs_5_.refs_0_), channel_id=1, source_target_pairs={{0,1},{1,0},{2,3},{3,2},{4,5},{5,4},{6,7},{7,6},{8,9},{9,8},{10,11... | collective-permute-start | bytes 5160968 | tf_op jit(solution)/shard_map/ppermute | solution.py:59
  6.1 1.0 slice.42
  7.2 1.1 slice.43
  8.4 1.6 collective-permute-start.1
  10.9 2.6 %collective-permute-start.2 = (bf16[32,5504]{1,0:T(8,128)(2,1)S(1)}, bf16[32,5504]{1,0:T(8,128)(2,1)S(1)}, u32[]{:S(2)}, u32[]{:S(2)}) collective-permute-start(bf16[32,5504]{1,0:T(8,128)(2,1)S(1)} %get-tuple-element.99), channel_id=1, source_target_pairs={{0,4},{1,5},{2,6},{3,7},{4,0},{5,1},{6,2},{7,3},{8,12},{9,13},{10,... | collective-permute-start | bytes 1056776 | tf_op jit(solution)/shard_map/ppermute | solution.py:59
  14.5 32.9 %collective-permute-done.4.refs_6_ = bf16[16,5504]{1,0:T(8,128)(2,1)S(1)} collective-permute-done((bf16[16,5504]{1,0:T(8,128)(2,1)S(1)}, bf16[16,5504]{1,0:T(8,128)(2,1)S(1)}, u32[]{:S(2)}, u32[]{:S(2)}) %collective-permute-start.4) | collective-permute-done | bytes 176160 | tf_op jit(solution)/shard_map/ppermute | solution.py:59
  48.4 1.0 collective-permute-start.8
  49.3 1.6 collective-permute-start.7
  50.9 1.1 collective-permute-start.6
  52.5 2.5 %shard_map.96 = (bf16[16,5504]{1,0:T(8,128)(2,1)S(1)}, bf16[16,5504]{1,0:T(8,128)(2,1)S(1)}, bf16[16,5504]{1,0:T(8,128)(2,1)S(1)}, f32[96,224]{1,0:T(8,128)S(1)}...) custom-call(bf16[336,2560]{1,0:T(8,128)(2,1)S(1)} %pad_maximum_fusion.refs_5_.refs_0_, ...), custom_call_target="tpu_custom_call" | custom-call | flops 566231040 | bytes 7249920 | tf_op jit(solution)/shard_map/pallas_call | solution.py:71
  55.0 6.0 %collective-permute-done.6.refs_6_ = bf16[16,5504]{1,0:T(8,128)(2,1)S(1)} collective-permute-done((bf16[16,5504]{1,0:T(8,128)(2,1)S(1)}, bf16[16,5504]{1,0:T(8,128)(2,1)S(1)}, u32[]{:S(2)}, u32[]{:S(2)}) %collective-permute-start.6) | collective-permute-done | bytes 176160 | tf_op jit(solution)/shard_map/ppermute | solution.py:59
  61.9 2.5 %shard_map.97 = (bf16[16,5504]{1,0:T(8,128)(2,1)S(1)}, bf16[16,5504]{1,0:T(8,128)(2,1)S(1)}, bf16[16,5504]{1,0:T(8,128)(2,1)S(1)}, f32[96,224]{1,0:T(8,128)S(1)}...) custom-call(bf16[336,2560]{1,0:T(8,128)(2,1)S(1)} %pad_maximum_fusion.refs_5_.refs_0_, ...), custom_call_target="tpu_custom_call" | custom-call | flops 566231040 | bytes 7249920 | tf_op jit(solution)/shard_map/pallas_call | solution.py:71
  64.5 1.6 collective-permute-start.10
  66.9 3.1 %collective-permute-done.10 = bf16[16,5504]{1,0:T(8,128)(2,1)S(1)} collective-permute-done((bf16[16,5504]{1,0:T(8,128)(2,1)S(1)}, bf16[16,5504]{1,0:T(8,128)(2,1)S(1)}, u32[]{:S(2)}, u32[]{:S(2)}) %collective-permute-start.10) | collective-permute-done | bytes 176160 | tf_op jit(solution)/shard_map/ppermute | solution.py:59
  70.0 1.6 collective-permute-done.11
  71.7 3.7 %collective-permute-start.13 = (bf16[16,5504]{1,0:T(8,128)(2,1)S(1)}, bf16[16,5504]{1,0:T(8,128)(2,1)S(1)}, u32[]{:S(2)}, u32[]{:S(2)}) collective-permute-start(bf16[16,5504]{1,0:T(8,128)(2,1)S(1)} %get-tuple-element.123.refs_7_), channel_id=1, source_target_pairs={{0,10},{1,11},{2,8},{3,9},{4,14},{5,15},{6,12},{7,13},{8,18},{9,19... | collective-permute-start | bytes 528392 | tf_op jit(solution)/shard_map/ppermute | solution.py:59
  76.3 7.7 %collective-permute-done.12.refs_4_ = bf16[16,5504]{1,0:T(8,128)(2,1)S(1)} collective-permute-done((bf16[16,5504]{1,0:T(8,128)(2,1)S(1)}, bf16[16,5504]{1,0:T(8,128)(2,1)S(1)}, u32[]{:S(2)}, u32[]{:S(2)}) %collective-permute-start.12) | collective-permute-done | bytes 176160 | tf_op jit(solution)/shard_map/ppermute | solution.py:59
  85.3 2.3 %collective-permute-start.17 = (bf16[16,5504]{1,0:T(8,128)(2,1)S(1)}, bf16[16,5504]{1,0:T(8,128)(2,1)S(1)}, u32[]{:S(2)}, u32[]{:S(2)}) collective-permute-start(bf16[16,5504]{1,0:T(8,128)(2,1)S(1)} %get-tuple-element.136), channel_id=1, source_target_pairs={{0,4},{1,5},{2,6},{3,7},{4,0},{5,1},{6,2},{7,3},{8,12},{9,13},{10,... | collective-permute-start | bytes 528392 | tf_op jit(solution)/shard_map/ppermute | solution.py:59
  89.0 7.3 %collective-permute-done.17.refs_9_ = bf16[16,5504]{1,0:T(8,128)(2,1)S(1)} collective-permute-done((bf16[16,5504]{1,0:T(8,128)(2,1)S(1)}, bf16[16,5504]{1,0:T(8,128)(2,1)S(1)}, u32[]{:S(2)}, u32[]{:S(2)}) %collective-permute-start.17) | collective-permute-done | bytes 176160 | tf_op jit(solution)/shard_map/ppermute | solution.py:59
  99.4 2.6 %shard_map.101 = (bf16[16,5504]{1,0:T(8,128)(2,1)S(1)}, bf16[16,5504]{1,0:T(8,128)(2,1)S(1)}, bf16[16,5504]{1,0:T(8,128)(2,1)S(1)}, f32[96,224]{1,0:T(8,128)S(1)...) custom-call(bf16[336,2560]{1,0:T(8,128)(2,1)S(1)} %pad_maximum_fusion.refs_5_.refs_0_, ...), custom_call_target="tpu_custom_call" | custom-call | flops 566231040 | bytes 7397376 | tf_op jit(solution)/shard_map/pallas_call | solution.py:71
  103.1 2.6 %shard_map.102 = (bf16[16,5504]{1,0:T(8,128)(2,1)S(1)}, bf16[16,5504]{1,0:T(8,128)(2,1)S(1)}, bf16[16,5504]{1,0:T(8,128)(2,1)S(1)}, f32[96,224]{1,0:T(8,128)S(1)...) custom-call(bf16[336,2560]{1,0:T(8,128)(2,1)S(1)} %pad_maximum_fusion.refs_5_.refs_0_, ...), custom_call_target="tpu_custom_call" | custom-call | flops 566231040 | bytes 7397376 | tf_op jit(solution)/shard_map/pallas_call | solution.py:71
  105.8 1.1 collective-permute-start.22
  106.8 1.1 collective-permute-start.23
  108.8 1.2 collective-permute-start.25
  111.3 1.0 collective-permute-done.23
  112.4 4.3 %collective-permute-done.25 = bf16[16,5504]{1,0:T(8,128)(2,1)S(1)} collective-permute-done((bf16[16,5504]{1,0:T(8,128)(2,1)S(1)}, bf16[16,5504]{1,0:T(8,128)(2,1)S(1)}, u32[]{:S(2)}, u32[]{:S(2)}) %collective-permute-start.25) | collective-permute-done | bytes 176160 | tf_op jit(solution)/shard_map/ppermute | solution.py:59
  116.9 1.3 collective-permute-start.28
  118.7 3.9 %collective-permute-done.24.refs_2_ = bf16[16,5504]{1,0:T(8,128)(2,1)S(1)} collective-permute-done((bf16[16,5504]{1,0:T(8,128)(2,1)S(1)}, bf16[16,5504]{1,0:T(8,128)(2,1)S(1)}, u32[]{:S(2)}, u32[]{:S(2)}) %collective-permute-start.24) | collective-permute-done | bytes 176160 | tf_op jit(solution)/shard_map/ppermute | solution.py:59
  122.6 3.1 %collective-permute-done.27.refs_3_ = bf16[16,5504]{1,0:T(8,128)(2,1)S(1)} collective-permute-done((bf16[16,5504]{1,0:T(8,128)(2,1)S(1)}, bf16[16,5504]{1,0:T(8,128)(2,1)S(1)}, u32[]{:S(2)}, u32[]{:S(2)}) %collective-permute-start.27) | collective-permute-done | bytes 176160 | tf_op jit(solution)/shard_map/ppermute | solution.py:59
  125.7 1.0 shard_map.104
  126.8 10.0 %collective-permute-done.31.refs_2_ = bf16[16,5504]{1,0:T(8,128)(2,1)S(1)} collective-permute-done((bf16[16,5504]{1,0:T(8,128)(2,1)S(1)}, bf16[16,5504]{1,0:T(8,128)(2,1)S(1)}, u32[]{:S(2)}, u32[]{:S(2)}) %collective-permute-start.31) | collective-permute-done | bytes 176160 | tf_op jit(solution)/shard_map/ppermute | solution.py:59
  136.8 3.7 %collective-permute-done.30.refs_9_ = bf16[16,5504]{1,0:T(8,128)(2,1)S(1)} collective-permute-done((bf16[16,5504]{1,0:T(8,128)(2,1)S(1)}, bf16[16,5504]{1,0:T(8,128)(2,1)S(1)}, u32[]{:S(2)}, u32[]{:S(2)}) %collective-permute-start.30) | collective-permute-done | bytes 176160 | tf_op jit(solution)/shard_map/ppermute | solution.py:59
  140.5 1.3 collective-permute-start.33
  142.6 2.0 %collective-permute-start.36 = (bf16[16,5504]{1,0:T(8,128)(2,1)S(1)}, bf16[16,5504]{1,0:T(8,128)(2,1)S(1)}, u32[]{:S(2)}, u32[]{:S(2)}) collective-permute-start(bf16[16,5504]{1,0:T(8,128)(2,1)S(1)} %get-tuple-element.177.refs_9_), channel_id=1, source_target_pairs={{0,2},{1,3},{2,0},{3,1},{4,6},{5,7},{6,4},{7,5},{8,10},{9,11},{10,... | collective-permute-start | bytes 528392 | tf_op jit(solution)/shard_map/ppermute | solution.py:59
  144.6 3.3 %collective-permute-done.33.refs_10_ = bf16[16,5504]{1,0:T(8,128)(2,1)S(1)} collective-permute-done((bf16[16,5504]{1,0:T(8,128)(2,1)S(1)}, bf16[16,5504]{1,0:T(8,128)(2,1)S(1)}, u32[]{:S(2)}, u32[]{:S(2)}) %collective-permute-start.33) | collective-permute-done | bytes 176160 | tf_op jit(solution)/shard_map/ppermute | solution.py:59
  147.9 1.3 collective-permute-done.32.refs_8_
  149.2 2.0 %shard_map.105 = (bf16[16,5504]{1,0:T(8,128)(2,1)S(1)}, bf16[16,5504]{1,0:T(8,128)(2,1)S(1)}, bf16[16,5504]{1,0:T(8,128)(2,1)S(1)}) custom-call(bf16[336,2560]{1,0:T(8,128)(2,1)S(1)} %pad_maximum_fusion.refs_5_.refs_0_, bf16[336,2560]{1,0:T(8,128)(2,1)S(1)} %collective-permute-done.refs_1_, bf16[240,2560]{1,0:T(8,128)(2,1)S(1)} %pad_maximum_fusion.1.refs_6_.refs_2_, ...), custom_call_target="tpu_custom_call" | custom-call | flops 566231040 | bytes 7249920 | tf_op jit(solution)/shard_map/pallas_call | solution.py:71
  152.9 2.0 %shard_map.106 = (bf16[16,5504]{1,0:T(8,128)(2,1)S(1)}, bf16[16,5504]{1,0:T(8,128)(2,1)S(1)}, bf16[16,5504]{1,0:T(8,128)(2,1)S(1)}) custom-call(bf16[336,2560]{1,0:T(8,128)(2,1)S(1)} %pad_maximum_fusion.refs_5_.refs_0_, bf16[336,2560]{1,0:T(8,128)(2,1)S(1)} %collective-permute-done.refs_1_, bf16[240,2560]{1,0:T(8,128)(2,1)S(1)} %pad_maximum_fusion.1.refs_6_.refs_2_, ...), custom_call_target="tpu_custom_call" | custom-call | flops 566231040 | bytes 7249920 | tf_op jit(solution)/shard_map/pallas_call | solution.py:71
  154.9 1.8 %collective-permute-done.35 = bf16[16,5504]{1,0:T(8,128)(2,1)S(1)} collective-permute-done((bf16[16,5504]{1,0:T(8,128)(2,1)S(1)}, bf16[16,5504]{1,0:T(8,128)(2,1)S(1)}, u32[]{:S(2)}, u32[]{:S(2)}) %collective-permute-start.35) | collective-permute-done | bytes 176160 | tf_op jit(solution)/shard_map/ppermute | solution.py:59
  156.7 1.8 %collective-permute-done.34 = bf16[16,5504]{1,0:T(8,128)(2,1)S(1)} collective-permute-done((bf16[16,5504]{1,0:T(8,128)(2,1)S(1)}, bf16[16,5504]{1,0:T(8,128)(2,1)S(1)}, u32[]{:S(2)}, u32[]{:S(2)}) %collective-permute-start.34) | collective-permute-done | bytes 176160 | tf_op jit(solution)/shard_map/ppermute | solution.py:59
  158.6 2.7 %collective-permute-start.39 = (bf16[16,5504]{1,0:T(8,128)(2,1)S(1)}, bf16[16,5504]{1,0:T(8,128)(2,1)S(1)}, u32[]{:S(2)}, u32[]{:S(2)}) collective-permute-start(bf16[16,5504]{1,0:T(8,128)(2,1)S(1)} %get-tuple-element.189), channel_id=1, source_target_pairs={{0,1},{1,0},{2,3},{3,2},{4,5},{5,4},{6,7},{7,6},{8,9},{9,8},{10,11... | collective-permute-start | bytes 528392 | tf_op jit(solution)/shard_map/ppermute | solution.py:59
  161.3 2.5 %collective-permute-start.40 = (bf16[16,5504]{1,0:T(8,128)(2,1)S(1)}, bf16[16,5504]{1,0:T(8,128)(2,1)S(1)}, u32[]{:S(2)}, u32[]{:S(2)}) collective-permute-start(bf16[16,5504]{1,0:T(8,128)(2,1)S(1)} %add_convert_fusion), channel_id=1, source_target_pairs={{0,4},{1,5},{2,6},{3,7},{4,0},{5,1},{6,2},{7,3},{8,12},{9,13},{10,... | collective-permute-start | bytes 528392 | tf_op jit(solution)/shard_map/ppermute | solution.py:59
  164.0 1.0 collective-permute-done.38.refs_3_
  165.0 1.1 shard_map.108
  166.1 3.5 %collective-permute-done.40.refs_4_ = bf16[16,5504]{1,0:T(8,128)(2,1)S(1)} collective-permute-done((bf16[16,5504]{1,0:T(8,128)(2,1)S(1)}, bf16[16,5504]{1,0:T(8,128)(2,1)S(1)}, u32[]{:S(2)}, u32[]{:S(2)}) %collective-permute-start.40) | collective-permute-done | bytes 176160 | tf_op jit(solution)/shard_map/ppermute | solution.py:59
  169.7 1.3 shard_map.109
  (79 shorter events, 18.9 us)
Async XLA Ops:
  3.1 45.2 %collective-permute-start = (bf16[336,2560]{1,0:T(8,128)(2,1)S(1)}, bf16[336,2560]{1,0:T(8,128)(2,1)S(1)}, u32[]{:S(2)}, u32[]{:S(2)}) collective-permute-start(bf16[336,2560]{1,0:T(8,128)(2,1)S(1)} %pad_maximum_fusion.refs_5_.refs_0_), channel_id=1, source_target_pairs={{0,1},{1,0},{2,3},{3,2},{4,5},{5,4},{6,7},{7,6},{8,9},{9,8},{10,11... | collective-permute-start | bytes 5160968 | tf_op jit(solution)/shard_map/ppermute | solution.py:59
  7.2 2.9 %copy-start = (bf16[1,64,2560]{2,1,0:T(8,128)(2,1)S(1)}, bf16[1,64,2560]{2,1,0:T(8,128)(2,1)}, u32[]{:S(2)}) copy-start(bf16[1,64,2560]{2,1,0:T(8,128)(2,1)} %param.15) | copy-start | bytes 983044
  7.2 2.9 %copy-start.1 = (bf16[1,64,2560]{2,1,0:T(8,128)(2,1)S(1)}, bf16[1,64,2560]{2,1,0:T(8,128)(2,1)}, u32[]{:S(2)}) copy-start(bf16[1,64,2560]{2,1,0:T(8,128)(2,1)} %param.8) | copy-start | bytes 983044
  7.2 2.9 %copy-start.2 = (f32[1,2560]{1,0:T(1,128)S(1)}, f32[1,2560]{1,0:T(1,128)}, u32[]{:S(2)}) copy-start(f32[1,2560]{1,0:T(1,128)} %refs_3_.3) | copy-start | bytes 30724
  7.2 2.9 %copy-start.3 = (s32[1,2,64,1]{2,3,1,0:T(1,128)S(1)}, s32[1,2,64,1]{2,3,1,0:T(1,128)}, u32[]{:S(2)}) copy-start(s32[1,2,64,1]{2,3,1,0:T(1,128)} %param.13) | copy-start | bytes 1540
  7.2 2.8 %copy-start.4 = (f32[1,2,64,1]{2,3,1,0:T(1,128)S(1)}, f32[1,2,64,1]{2,3,1,0:T(1,128)}, u32[]{:S(2)}) copy-start(f32[1,2,64,1]{2,3,1,0:T(1,128)} %param.14) | copy-start | bytes 1540
  8.4 39.9 %collective-permute-start.1 = (bf16[240,2560]{1,0:T(8,128)(2,1)S(1)}, bf16[240,2560]{1,0:T(8,128)(2,1)S(1)}, u32[]{:S(2)}, u32[]{:S(2)}) collective-permute-start(bf16[240,2560]{1,0:T(8,128)(2,1)S(1)} %pad_maximum_fusion.1.refs_6_.refs_2_), channel_id=1, source_target_pairs={{0,2},{1,3},{2,0},{3,1},{4,6},{5,7},{6,4},{7,5},{8,10},{9,11},{10,... | collective-permute-start | bytes 3686408 | tf_op jit(solution)/shard_map/ppermute | solution.py:59
  10.9 37.4 %collective-permute-start.2 = (bf16[32,5504]{1,0:T(8,128)(2,1)S(1)}, bf16[32,5504]{1,0:T(8,128)(2,1)S(1)}, u32[]{:S(2)}, u32[]{:S(2)}) collective-permute-start(bf16[32,5504]{1,0:T(8,128)(2,1)S(1)} %get-tuple-element.99), channel_id=1, source_target_pairs={{0,4},{1,5},{2,6},{3,7},{4,0},{5,1},{6,2},{7,3},{8,12},{9,13},{10,... | collective-permute-start | bytes 1056776 | tf_op jit(solution)/shard_map/ppermute | solution.py:59
  13.6 33.9 %collective-permute-start.4 = (bf16[16,5504]{1,0:T(8,128)(2,1)S(1)}, bf16[16,5504]{1,0:T(8,128)(2,1)S(1)}, u32[]{:S(2)}, u32[]{:S(2)}) collective-permute-start(bf16[16,5504]{1,0:T(8,128)(2,1)S(1)} %get-tuple-element.107.refs_5_), channel_id=1, source_target_pairs={{0,1},{1,0},{2,3},{3,2},{4,5},{5,4},{6,7},{7,6},{8,9},{9,8},{10,11... | collective-permute-start | bytes 528392 | tf_op jit(solution)/shard_map/ppermute | solution.py:59
  14.1 34.2 %collective-permute-start.3 = (bf16[16,5504]{1,0:T(8,128)(2,1)S(1)}, bf16[16,5504]{1,0:T(8,128)(2,1)S(1)}, u32[]{:S(2)}, u32[]{:S(2)}) collective-permute-start(bf16[16,5504]{1,0:T(8,128)(2,1)S(1)} %get-tuple-element.107.refs_5_), channel_id=1, source_target_pairs={{0,2},{1,3},{2,0},{3,1},{4,6},{5,7},{6,4},{7,5},{8,10},{9,11},{10,... | collective-permute-start | bytes 528392 | tf_op jit(solution)/shard_map/ppermute | solution.py:59
  48.4 16.1 %collective-permute-start.8 = (bf16[32,5504]{1,0:T(8,128)(2,1)S(1)}, bf16[32,5504]{1,0:T(8,128)(2,1)S(1)}, u32[]{:S(2)}, u32[]{:S(2)}) collective-permute-start(bf16[32,5504]{1,0:T(8,128)(2,1)S(1)} %pad_maximum_fusion.2.refs_5_), channel_id=1, source_target_pairs={{0,1},{1,0},{2,3},{3,2},{4,5},{5,4},{6,7},{7,6},{8,9},{9,8},{10,11... | collective-permute-start | bytes 1056776 | tf_op jit(solution)/shard_map/ppermute | solution.py:59
  49.3 15.1 %collective-permute-start.7 = (bf16[32,5504]{1,0:T(8,128)(2,1)S(1)}, bf16[32,5504]{1,0:T(8,128)(2,1)S(1)}, u32[]{:S(2)}, u32[]{:S(2)}) collective-permute-start(bf16[32,5504]{1,0:T(8,128)(2,1)S(1)} %pad_maximum_fusion.2.refs_5_), channel_id=1, source_target_pairs={{0,2},{1,3},{2,0},{3,1},{4,6},{5,7},{6,4},{7,5},{8,10},{9,11},{10,... | collective-permute-start | bytes 1056776 | tf_op jit(solution)/shard_map/ppermute | solution.py:59
  50.9 10.1 %collective-permute-start.6 = (bf16[16,5504]{1,0:T(8,128)(2,1)S(1)}, bf16[16,5504]{1,0:T(8,128)(2,1)S(1)}, u32[]{:S(2)}, u32[]{:S(2)}) collective-permute-start(bf16[16,5504]{1,0:T(8,128)(2,1)S(1)} %get-tuple-element.197.refs_5_), channel_id=1, source_target_pairs={{0,1},{1,0},{2,3},{3,2},{4,5},{5,4},{6,7},{7,6},{8,9},{9,8},{10,11... | collective-permute-start | bytes 528392 | tf_op jit(solution)/shard_map/ppermute | solution.py:59
  52.0 9.9 %collective-permute-start.5 = (bf16[16,5504]{1,0:T(8,128)(2,1)S(1)}, bf16[16,5504]{1,0:T(8,128)(2,1)S(1)}, u32[]{:S(2)}, u32[]{:S(2)}) collective-permute-start(bf16[16,5504]{1,0:T(8,128)(2,1)S(1)} %get-tuple-element.197.refs_5_), channel_id=1, source_target_pairs={{0,2},{1,3},{2,0},{3,1},{4,6},{5,7},{6,4},{7,5},{8,10},{9,11},{10,... | collective-permute-start | bytes 528392 | tf_op jit(solution)/shard_map/ppermute | solution.py:59
  64.5 5.5 %collective-permute-start.10 = (bf16[16,5504]{1,0:T(8,128)(2,1)S(1)}, bf16[16,5504]{1,0:T(8,128)(2,1)S(1)}, u32[]{:S(2)}, u32[]{:S(2)}) collective-permute-start(bf16[16,5504]{1,0:T(8,128)(2,1)S(1)} %get-tuple-element.118), channel_id=1, source_target_pairs={{0,2},{1,3},{2,0},{3,1},{4,6},{5,7},{6,4},{7,5},{8,10},{9,11},{10,... | collective-permute-start | bytes 528392 | tf_op jit(solution)/shard_map/ppermute | solution.py:59
  66.1 5.5 %collective-permute-start.11 = (bf16[16,5504]{1,0:T(8,128)(2,1)S(1)}, bf16[16,5504]{1,0:T(8,128)(2,1)S(1)}, u32[]{:S(2)}, u32[]{:S(2)}) collective-permute-start(bf16[16,5504]{1,0:T(8,128)(2,1)S(1)} %get-tuple-element.119), channel_id=1, source_target_pairs={{0,1},{1,0},{2,3},{3,2},{4,5},{5,4},{6,7},{7,6},{8,9},{9,8},{10,11... | collective-permute-start | bytes 528392 | tf_op jit(solution)/shard_map/ppermute | solution.py:59
  66.9 17.4 %collective-permute-start.9 = (bf16[80,2560]{1,0:T(8,128)(2,1)S(1)}, bf16[80,2560]{1,0:T(8,128)(2,1)S(1)}, u32[]{:S(2)}, u32[]{:S(2)}) collective-permute-start(bf16[80,2560]{1,0:T(8,128)(2,1)S(1)} %get-tuple-element.115), channel_id=1, source_target_pairs={{0,8},{1,9},{2,10},{3,11},{4,12},{5,13},{6,14},{7,15},{8,16},{9,17... | collective-permute-start | bytes 1228808 | tf_op jit(solution)/shard_map/ppermute | solution.py:59
  71.6 12.3 %collective-permute-start.12 = (bf16[16,5504]{1,0:T(8,128)(2,1)S(1)}, bf16[16,5504]{1,0:T(8,128)(2,1)S(1)}, u32[]{:S(2)}, u32[]{:S(2)}) collective-permute-start(bf16[16,5504]{1,0:T(8,128)(2,1)S(1)} %add_convert_fusion.3), channel_id=1, source_target_pairs={{0,12},{1,13},{2,14},{3,15},{4,8},{5,9},{6,10},{7,11},{8,20},{9,21... | collective-permute-start | bytes 528392 | tf_op jit(solution)/shard_map/ppermute | solution.py:59
  71.7 12.3 %collective-permute-start.13 = (bf16[16,5504]{1,0:T(8,128)(2,1)S(1)}, bf16[16,5504]{1,0:T(8,128)(2,1)S(1)}, u32[]{:S(2)}, u32[]{:S(2)}) collective-permute-start(bf16[16,5504]{1,0:T(8,128)(2,1)S(1)} %get-tuple-element.123.refs_7_), channel_id=1, source_target_pairs={{0,10},{1,11},{2,8},{3,9},{4,14},{5,15},{6,12},{7,13},{8,18},{9,19... | collective-permute-start | bytes 528392 | tf_op jit(solution)/shard_map/ppermute | solution.py:59
  75.4 8.6 %collective-permute-start.14 = (bf16[16,5504]{1,0:T(8,128)(2,1)S(1)}, bf16[16,5504]{1,0:T(8,128)(2,1)S(1)}, u32[]{:S(2)}, u32[]{:S(2)}) collective-permute-start(bf16[16,5504]{1,0:T(8,128)(2,1)S(1)} %get-tuple-element.124), channel_id=1, source_target_pairs={{0,9},{1,8},{2,11},{3,10},{4,13},{5,12},{6,15},{7,14},{8,17},{9,16... | collective-permute-start | bytes 528392 | tf_op jit(solution)/shard_map/ppermute | solution.py:59
  75.8 8.6 %collective-permute-start.15 = (bf16[16,5504]{1,0:T(8,128)(2,1)S(1)}, bf16[16,5504]{1,0:T(8,128)(2,1)S(1)}, u32[]{:S(2)}, u32[]{:S(2)}) collective-permute-start(bf16[16,5504]{1,0:T(8,128)(2,1)S(1)} %get-tuple-element.125), channel_id=1, source_target_pairs={{0,8},{1,9},{2,10},{3,11},{4,12},{5,13},{6,14},{7,15},{8,16},{9,17... | collective-permute-start | bytes 528392 | tf_op jit(solution)/shard_map/ppermute | solution.py:59
  85.3 11.0 %collective-permute-start.17 = (bf16[16,5504]{1,0:T(8,128)(2,1)S(1)}, bf16[16,5504]{1,0:T(8,128)(2,1)S(1)}, u32[]{:S(2)}, u32[]{:S(2)}) collective-permute-start(bf16[16,5504]{1,0:T(8,128)(2,1)S(1)} %get-tuple-element.136), channel_id=1, source_target_pairs={{0,4},{1,5},{2,6},{3,7},{4,0},{5,1},{6,2},{7,3},{8,12},{9,13},{10,... | collective-permute-start | bytes 528392 | tf_op jit(solution)/shard_map/ppermute | solution.py:59
  87.6 8.7 %collective-permute-start.19 = (bf16[16,5504]{1,0:T(8,128)(2,1)S(1)}, bf16[16,5504]{1,0:T(8,128)(2,1)S(1)}, u32[]{:S(2)}, u32[]{:S(2)}) collective-permute-start(bf16[16,5504]{1,0:T(8,128)(2,1)S(1)} %get-tuple-element.137.refs_9_), channel_id=1, source_target_pairs={{0,1},{1,0},{2,3},{3,2},{4,5},{5,4},{6,7},{7,6},{8,9},{9,8},{10,11... | collective-permute-start | bytes 528392 | tf_op jit(solution)/shard_map/ppermute | solution.py:59
  88.4 8.3 %collective-permute-start.18 = (bf16[16,5504]{1,0:T(8,128)(2,1)S(1)}, bf16[16,5504]{1,0:T(8,128)(2,1)S(1)}, u32[]{:S(2)}, u32[]{:S(2)}) collective-permute-start(bf16[16,5504]{1,0:T(8,128)(2,1)S(1)} %get-tuple-element.137.refs_9_), channel_id=1, source_target_pairs={{0,2},{1,3},{2,0},{3,1},{4,6},{5,7},{6,4},{7,5},{8,10},{9,11},{10,... | collective-permute-start | bytes 528392 | tf_op jit(solution)/shard_map/ppermute | solution.py:59
  96.7 5.9 %collective-permute-start.21 = (bf16[16,5504]{1,0:T(8,128)(2,1)S(1)}, bf16[16,5504]{1,0:T(8,128)(2,1)S(1)}, u32[]{:S(2)}, u32[]{:S(2)}) collective-permute-start(bf16[16,5504]{1,0:T(8,128)(2,1)S(1)} %collective-permute-done.17.refs_9_), channel_id=1, source_target_pairs={{0,1},{1,0},{2,3},{3,2},{4,5},{5,4},{6,7},{7,6},{8,9},{9,8},{10,11... | collective-permute-start | bytes 528392 | tf_op jit(solution)/shard_map/ppermute | solution.py:59
  97.7 5.5 %collective-permute-start.20 = (bf16[16,5504]{1,0:T(8,128)(2,1)S(1)}, bf16[16,5504]{1,0:T(8,128)(2,1)S(1)}, u32[]{:S(2)}, u32[]{:S(2)}) collective-permute-start(bf16[16,5504]{1,0:T(8,128)(2,1)S(1)} %collective-permute-done.17.refs_9_), channel_id=1, source_target_pairs={{0,2},{1,3},{2,0},{3,1},{4,6},{5,7},{6,4},{7,5},{8,10},{9,11},{10,... | collective-permute-start | bytes 528392 | tf_op jit(solution)/shard_map/ppermute | solution.py:59
  105.8 5.5 %collective-permute-start.22 = (bf16[16,5504]{1,0:T(8,128)(2,1)S(1)}, bf16[16,5504]{1,0:T(8,128)(2,1)S(1)}, u32[]{:S(2)}, u32[]{:S(2)}) collective-permute-start(bf16[16,5504]{1,0:T(8,128)(2,1)S(1)} %get-tuple-element.147), channel_id=1, source_target_pairs={{0,2},{1,3},{2,0},{3,1},{4,6},{5,7},{6,4},{7,5},{8,10},{9,11},{10,... | collective-permute-start | bytes 528392 | tf_op jit(solution)/shard_map/ppermute | solution.py:59
  106.8 5.5 %collective-permute-start.23 = (bf16[16,5504]{1,0:T(8,128)(2,1)S(1)}, bf16[16,5504]{1,0:T(8,128)(2,1)S(1)}, u32[]{:S(2)}, u32[]{:S(2)}) collective-permute-start(bf16[16,5504]{1,0:T(8,128)(2,1)S(1)} %get-tuple-element.148), channel_id=1, source_target_pairs={{0,1},{1,0},{2,3},{3,2},{4,5},{5,4},{6,7},{7,6},{8,9},{9,8},{10,11... | collective-permute-start | bytes 528392 | tf_op jit(solution)/shard_map/ppermute | solution.py:59
  107.9 17.7 %collective-permute-start.16 = (bf16[144,2560]{1,0:T(8,128)(2,1)S(1)}, bf16[144,2560]{1,0:T(8,128)(2,1)S(1)}, u32[]{:S(2)}, u32[]{:S(2)}) collective-permute-start(bf16[144,2560]{1,0:T(8,128)(2,1)S(1)} %get-tuple-element.127), channel_id=1, source_target_pairs={{0,24},{1,25},{2,26},{3,27},{4,28},{5,29},{6,30},{7,31},{8,0},{9,1... | collective-permute-start | bytes 2211848 | tf_op jit(solution)/shard_map/ppermute | solution.py:59
  108.8 8.0 %collective-permute-start.25 = (bf16[16,5504]{1,0:T(8,128)(2,1)S(1)}, bf16[16,5504]{1,0:T(8,128)(2,1)S(1)}, u32[]{:S(2)}, u32[]{:S(2)}) collective-permute-start(bf16[16,5504]{1,0:T(8,128)(2,1)S(1)} %get-tuple-element.156), channel_id=1, source_target_pairs={{0,2},{1,3},{2,0},{3,1},{4,6},{5,7},{6,4},{7,5},{8,10},{9,11},{10,... | collective-permute-start | bytes 528392 | tf_op jit(solution)/shard_map/ppermute | solution.py:59
  110.0 6.8 %collective-permute-start.26 = (bf16[16,5504]{1,0:T(8,128)(2,1)S(1)}, bf16[16,5504]{1,0:T(8,128)(2,1)S(1)}, u32[]{:S(2)}, u32[]{:S(2)}) collective-permute-start(bf16[16,5504]{1,0:T(8,128)(2,1)S(1)} %get-tuple-element.157), channel_id=1, source_target_pairs={{0,1},{1,0},{2,3},{3,2},{4,5},{5,4},{6,7},{7,6},{8,9},{9,8},{10,11... | collective-permute-start | bytes 528392 | tf_op jit(solution)/shard_map/ppermute | solution.py:59
  112.3 10.2 %collective-permute-start.24 = (bf16[16,5504]{1,0:T(8,128)(2,1)S(1)}, bf16[16,5504]{1,0:T(8,128)(2,1)S(1)}, u32[]{:S(2)}, u32[]{:S(2)}) collective-permute-start(bf16[16,5504]{1,0:T(8,128)(2,1)S(1)} %add_convert_fusion.2), channel_id=1, source_target_pairs={{0,28},{1,29},{2,30},{3,31},{4,24},{5,25},{6,26},{7,27},{8,4},{9,5... | collective-permute-start | bytes 528392 | tf_op jit(solution)/shard_map/ppermute | solution.py:59
  116.8 8.8 %collective-permute-start.27 = (bf16[16,5504]{1,0:T(8,128)(2,1)S(1)}, bf16[16,5504]{1,0:T(8,128)(2,1)S(1)}, u32[]{:S(2)}, u32[]{:S(2)}) collective-permute-start(bf16[16,5504]{1,0:T(8,128)(2,1)S(1)} %get-tuple-element.158.refs_11_), channel_id=1, source_target_pairs={{0,26},{1,27},{2,24},{3,25},{4,30},{5,31},{6,28},{7,29},{8,2},{9,3... | collective-permute-start | bytes 528392 | tf_op jit(solution)/shard_map/ppermute | solution.py:59
  116.9 8.8 %collective-permute-start.28 = (bf16[16,5504]{1,0:T(8,128)(2,1)S(1)}, bf16[16,5504]{1,0:T(8,128)(2,1)S(1)}, u32[]{:S(2)}, u32[]{:S(2)}) collective-permute-start(bf16[16,5504]{1,0:T(8,128)(2,1)S(1)} %get-tuple-element.159), channel_id=1, source_target_pairs={{0,25},{1,24},{2,27},{3,26},{4,29},{5,28},{6,31},{7,30},{8,1},{9,0... | collective-permute-start | bytes 528392 | tf_op jit(solution)/shard_map/ppermute | solution.py:59
  118.2 7.4 %collective-permute-start.29 = (bf16[16,5504]{1,0:T(8,128)(2,1)S(1)}, bf16[16,5504]{1,0:T(8,128)(2,1)S(1)}, u32[]{:S(2)}, u32[]{:S(2)}) collective-permute-start(bf16[16,5504]{1,0:T(8,128)(2,1)S(1)} %get-tuple-element.160), channel_id=1, source_target_pairs={{0,24},{1,25},{2,26},{3,27},{4,28},{5,29},{6,30},{7,31},{8,0},{9,1... | collective-permute-start | bytes 528392 | tf_op jit(solution)/shard_map/ppermute | solution.py:59
  122.6 14.3 %collective-permute-start.31 = (bf16[16,5504]{1,0:T(8,128)(2,1)S(1)}, bf16[16,5504]{1,0:T(8,128)(2,1)S(1)}, u32[]{:S(2)}, u32[]{:S(2)}) collective-permute-start(bf16[16,5504]{1,0:T(8,128)(2,1)S(1)} %add_convert_fusion.1), channel_id=1, source_target_pairs={{0,4},{1,5},{2,6},{3,7},{4,0},{5,1},{6,2},{7,3},{8,12},{9,13},{10,... | collective-permute-start | bytes 528392 | tf_op jit(solution)/shard_map/ppermute | solution.py:59
  126.7 13.9 %collective-permute-start.30 = (bf16[16,5504]{1,0:T(8,128)(2,1)S(1)}, bf16[16,5504]{1,0:T(8,128)(2,1)S(1)}, u32[]{:S(2)}, u32[]{:S(2)}) collective-permute-start(bf16[16,5504]{1,0:T(8,128)(2,1)S(1)} %get-tuple-element.161), channel_id=1, source_target_pairs={{0,4},{1,5},{2,6},{3,7},{4,0},{5,1},{6,2},{7,3},{8,12},{9,13},{10,... | collective-permute-start | bytes 528392 | tf_op jit(solution)/shard_map/ppermute | solution.py:59
  140.5 7.3 %collective-permute-start.33 = (bf16[16,5504]{1,0:T(8,128)(2,1)S(1)}, bf16[16,5504]{1,0:T(8,128)(2,1)S(1)}, u32[]{:S(2)}, u32[]{:S(2)}) collective-permute-start(bf16[16,5504]{1,0:T(8,128)(2,1)S(1)} %collective-permute-done.30.refs_9_), channel_id=1, source_target_pairs={{0,1},{1,0},{2,3},{3,2},{4,5},{5,4},{6,7},{7,6},{8,9},{9,8},{10,11... | collective-permute-start | bytes 528392 | tf_op jit(solution)/shard_map/ppermute | solution.py:59
  141.8 7.3 %collective-permute-start.32 = (bf16[16,5504]{1,0:T(8,128)(2,1)S(1)}, bf16[16,5504]{1,0:T(8,128)(2,1)S(1)}, u32[]{:S(2)}, u32[]{:S(2)}) collective-permute-start(bf16[16,5504]{1,0:T(8,128)(2,1)S(1)} %collective-permute-done.30.refs_9_), channel_id=1, source_target_pairs={{0,2},{1,3},{2,0},{3,1},{4,6},{5,7},{6,4},{7,5},{8,10},{9,11},{10,... | collective-permute-start | bytes 528392 | tf_op jit(solution)/shard_map/ppermute | solution.py:59
  141.8 11.0 %collective-permute-start.37 = (bf16[16,5504]{1,0:T(8,128)(2,1)S(1)}, bf16[16,5504]{1,0:T(8,128)(2,1)S(1)}, u32[]{:S(2)}, u32[]{:S(2)}) collective-permute-start(bf16[16,5504]{1,0:T(8,128)(2,1)S(1)} %get-tuple-element.177.refs_9_), channel_id=1, source_target_pairs={{0,1},{1,0},{2,3},{3,2},{4,5},{5,4},{6,7},{7,6},{8,9},{9,8},{10,11... | collective-permute-start | bytes 528392 | tf_op jit(solution)/shard_map/ppermute | solution.py:59
  142.6 10.3 %collective-permute-start.36 = (bf16[16,5504]{1,0:T(8,128)(2,1)S(1)}, bf16[16,5504]{1,0:T(8,128)(2,1)S(1)}, u32[]{:S(2)}, u32[]{:S(2)}) collective-permute-start(bf16[16,5504]{1,0:T(8,128)(2,1)S(1)} %get-tuple-element.177.refs_9_), channel_id=1, source_target_pairs={{0,2},{1,3},{2,0},{3,1},{4,6},{5,7},{6,4},{7,5},{8,10},{9,11},{10,... | collective-permute-start | bytes 528392 | tf_op jit(solution)/shard_map/ppermute | solution.py:59
  151.2 5.5 %collective-permute-start.35 = (bf16[16,5504]{1,0:T(8,128)(2,1)S(1)}, bf16[16,5504]{1,0:T(8,128)(2,1)S(1)}, u32[]{:S(2)}, u32[]{:S(2)}) collective-permute-start(bf16[16,5504]{1,0:T(8,128)(2,1)S(1)} %get-tuple-element.172), channel_id=1, source_target_pairs={{0,1},{1,0},{2,3},{3,2},{4,5},{5,4},{6,7},{7,6},{8,9},{9,8},{10,11... | collective-permute-start | bytes 528392 | tf_op jit(solution)/shard_map/ppermute | solution.py:59
  152.0 6.4 %collective-permute-start.34 = (bf16[16,5504]{1,0:T(8,128)(2,1)S(1)}, bf16[16,5504]{1,0:T(8,128)(2,1)S(1)}, u32[]{:S(2)}, u32[]{:S(2)}) collective-permute-start(bf16[16,5504]{1,0:T(8,128)(2,1)S(1)} %get-tuple-element.171.refs_11_), channel_id=1, source_target_pairs={{0,2},{1,3},{2,0},{3,1},{4,6},{5,7},{6,4},{7,5},{8,10},{9,11},{10,... | collective-permute-start | bytes 528392 | tf_op jit(solution)/shard_map/ppermute | solution.py:59
  158.5 6.5 %collective-permute-start.38 = (bf16[16,5504]{1,0:T(8,128)(2,1)S(1)}, bf16[16,5504]{1,0:T(8,128)(2,1)S(1)}, u32[]{:S(2)}, u32[]{:S(2)}) collective-permute-start(bf16[16,5504]{1,0:T(8,128)(2,1)S(1)} %get-tuple-element.188), channel_id=1, source_target_pairs={{0,2},{1,3},{2,0},{3,1},{4,6},{5,7},{6,4},{7,5},{8,10},{9,11},{10,... | collective-permute-start | bytes 528392 | tf_op jit(solution)/shard_map/ppermute | solution.py:59
  158.6 6.4 %collective-permute-start.39 = (bf16[16,5504]{1,0:T(8,128)(2,1)S(1)}, bf16[16,5504]{1,0:T(8,128)(2,1)S(1)}, u32[]{:S(2)}, u32[]{:S(2)}) collective-permute-start(bf16[16,5504]{1,0:T(8,128)(2,1)S(1)} %get-tuple-element.189), channel_id=1, source_target_pairs={{0,1},{1,0},{2,3},{3,2},{4,5},{5,4},{6,7},{7,6},{8,9},{9,8},{10,11... | collective-permute-start | bytes 528392 | tf_op jit(solution)/shard_map/ppermute | solution.py:59
  161.3 8.3 %collective-permute-start.40 = (bf16[16,5504]{1,0:T(8,128)(2,1)S(1)}, bf16[16,5504]{1,0:T(8,128)(2,1)S(1)}, u32[]{:S(2)}, u32[]{:S(2)}) collective-permute-start(bf16[16,5504]{1,0:T(8,128)(2,1)S(1)} %add_convert_fusion), channel_id=1, source_target_pairs={{0,4},{1,5},{2,6},{3,7},{4,0},{5,1},{6,2},{7,3},{8,12},{9,13},{10,... | collective-permute-start | bytes 528392 | tf_op jit(solution)/shard_map/ppermute | solution.py:59
  163.8 5.9 %collective-permute-start.41 = (bf16[16,5504]{1,0:T(8,128)(2,1)S(1)}, bf16[16,5504]{1,0:T(8,128)(2,1)S(1)}, u32[]{:S(2)}, u32[]{:S(2)}) collective-permute-start(bf16[16,5504]{1,0:T(8,128)(2,1)S(1)} %get-tuple-element.193), channel_id=1, source_target_pairs={{0,2},{1,3},{2,0},{3,1},{4,6},{5,7},{6,4},{7,5},{8,10},{9,11},{10,... | collective-permute-start | bytes 528392 | tf_op jit(solution)/shard_map/ppermute | solution.py:59
  163.9 5.8 %collective-permute-start.42 = (bf16[16,5504]{1,0:T(8,128)(2,1)S(1)}, bf16[16,5504]{1,0:T(8,128)(2,1)S(1)}, u32[]{:S(2)}, u32[]{:S(2)}) collective-permute-start(bf16[16,5504]{1,0:T(8,128)(2,1)S(1)} %get-tuple-element.194), channel_id=1, source_target_pairs={{0,1},{1,0},{2,3},{3,2},{4,5},{5,4},{6,7},{7,6},{8,9},{9,8},{10,11... | collective-permute-start | bytes 528392 | tf_op jit(solution)/shard_map/ppermute | solution.py:59
  (1 other events, 2.3 us)
where the time goes:
time: 171 us
  waiting for transfers between devices  101 us (59%)
  starting transfers between devices  40.6 us (24%)
  Pallas kernels  23 us (13%)
  local copies, waits for them, and re-layouts  4.53 us (3%)
    ppermute x43, waiting for transfers between devices, shift(): return lax.ppermute(value, ('section', 'expert'), pairs)  101 us
    ppermute x43, starting transfers between devices, shift(): return lax.ppermute(value, ('section', 'expert'), pairs)  40.6 us
    pallas_call x15, Pallas kernels, call(): pl.pallas_call(reading, out_shape=list(outs), in_specs=[vmem] * read + [p...  23 us
  transfers between devices with their start and end apart: 43, of which 25 were waited for; matrix products, arithmetic and copies ran while one was open for 1% of the time, Pallas kernels for 11%

commit v1 on v0

--- a/solution.py
+++ b/solution.py
@@ -520,7 +520,9 @@
     own0 = around(own_tok)
     packs, crossed, own0 = fence((packs, crossed, own0))
     cross0 = around(joined([c[:ROWS] for c in crossed]))
-    cots = around(joined([own_cot] + [c[ROWS:] for c in crossed]))
+    cots = joined([own_cot] + [c[ROWS:] for c in crossed])
+    cross0, cots = fence((cross0, cots))
+    cots = around(cots)
 
     own_out, own_kept0 = expert_call(forward_kernel, box, packs, own0, kept=2)
     cross_out, cross_kept0 = expert_call(
@@ -553,11 +555,8 @@
     down = bind(expert_call, down_kernel, box, packs, reads=False)
     cross_fin = down(cross1, cross_kept1)[0]
     arrived1 = shift(behind, sections=-1)
-    total = sums(cross_grad)
-    back_grad = home(total, -1)
-    own_grad, fin_sums = fence((own_grad, sums(cross_fin)))
-    got = back_grad + own_home(own_grad, -1)
-    fin_back = home(fin_sums, 0)
+    got = give_back(cross_grad, own_grad, -1)
+    got[: experts - 1], fin_sums = fence((got[: experts - 1], sums(cross_fin)))
     own_fin = down(own1, own_kept1)[0]
     g1, own_g, *boxes_g = call(
         bind(turn_kernel, box, experts),
@@ -568,12 +567,16 @@
         scratch=[picked],
     )
 
-    cross_g, own_g, fin_back = fence((crossing_of(boxes_g), own_g, fin_back))
-    cross_g, own_g = around(cross_g), around(own_g)
+    cross_g, own_z, own_x = fence(
+        (crossing_of(boxes_g), shift(own_g, flip=2), shift(own_g, flip=1))
+    )
+    cross_g, own_g = around(cross_g), [own_z, own_g, own_x]
+    cross_g, fin_sums = fence((cross_g, fin_sums))
+    fin_back = home(fin_sums, 0)
     back = bind(expert_call, back_kernel, box, packs)
-    cross_grad = back(cross_g, cross_kept0)[0]
-    own_grad = back(own_g, own_kept0, after=cross_grad[:1])[0]
-    total, own_grad, own_fin = fence((sums(cross_grad), own_grad, own_fin))
+    own_grad = back(own_g, own_kept0)[0]
+    cross_grad = back(cross_g, cross_kept0, after=own_grad[:1])[0]
+    total, own_grad, own_fin, fin_back = fence((sums(cross_grad), own_grad, own_fin, fin_back))
     got = home(total, 0) + own_home(own_grad, 0)
     fin_own = own_home(own_fin, 0)
     (g0,) = call(

time: 171 us -> 172 us (level)
  starting transfers between devices: 40.6 us -> 42.6 us
    ppermute x43, starting transfers between devices: 40.6 us -> 42.6 us  [shift(): return lax.ppermute(value, ('section', 'expert'), pairs)]
  transfers between devices with their start and end apart: 43 -> 43, of which waited for: 25 -> 28; matrix products, arithmetic and copies ran while one was open for 1% -> 1% of each run, Pallas kernels for 11% -> 9%
where the time goes in v1:
time: 172 us
  waiting for transfers between devices  101 us (59%)
  starting transfers between devices  42.6 us (25%)
  Pallas kernels  23 us (13%)
  local copies, waits for them, and re-layouts  4.53 us (3%)
    ppermute x43, waiting for transfers between devices, shift(): return lax.ppermute(value, ('section', 'expert'), pairs)  101 us
    ppermute x43, starting transfers between devices, shift(): return lax.ppermute(value, ('section', 'expert'), pairs)  42.6 us
    pallas_call x15, Pallas kernels, call(): pl.pallas_call(reading, out_shape=list(outs), in_specs=[vmem] * read + [p...  23 us
  transfers between devices with their start and end apart: 43, of which 28 were waited for; matrix products, arithmetic and copies ran while one was open for 1% of the time, Pallas kernels for 9%

profile of v1, /device:TPU:0, one launch (start us, length us, event | category | flops | bytes accessed | tf_op | source)
XLA Modules:
  0.0 172.1 jit_solution(8257715195889312231)
XLA Ops:
  0.6 1.2 slice.40
  1.8 1.1 slice.41
  3.1 3.0 %collective-permute-start = (bf16[336,2560]{1,0:T(8,128)(2,1)S(1)}, bf16[336,2560]{1,0:T(8,128)(2,1)S(1)}, u32[]{:S(2)}, u32[]{:S(2)}) collective-permute-start(bf16[336,2560]{1,0:T(8,128)(2,1)S(1)} %pad_maximum_fusion.refs_5_.refs_0_), channel_id=1, source_target_pairs={{0,1},{1,0},{2,3},{3,2},{4,5},{5,4},{6,7},{7,6},{8,9},{9,8},{10,11... | collective-permute-start | bytes 5160968 | tf_op jit(solution)/shard_map/ppermute | solution.py:59
  6.1 1.0 slice.42
  7.2 1.1 slice.43
  8.4 1.6 collective-permute-start.1
  10.9 2.6 %collective-permute-start.2 = (bf16[32,5504]{1,0:T(8,128)(2,1)S(1)}, bf16[32,5504]{1,0:T(8,128)(2,1)S(1)}, u32[]{:S(2)}, u32[]{:S(2)}) collective-permute-start(bf16[32,5504]{1,0:T(8,128)(2,1)S(1)} %get-tuple-element.110), channel_id=1, source_target_pairs={{0,4},{1,5},{2,6},{3,7},{4,0},{5,1},{6,2},{7,3},{8,12},{9,13},{10,... | collective-permute-start | bytes 1056776 | tf_op jit(solution)/shard_map/ppermute | solution.py:59
  14.5 32.9 %collective-permute-done.4.refs_6_ = bf16[16,5504]{1,0:T(8,128)(2,1)S(1)} collective-permute-done((bf16[16,5504]{1,0:T(8,128)(2,1)S(1)}, bf16[16,5504]{1,0:T(8,128)(2,1)S(1)}, u32[]{:S(2)}, u32[]{:S(2)}) %collective-permute-start.4) | collective-permute-done | bytes 176160 | tf_op jit(solution)/shard_map/ppermute | solution.py:59
  49.3 1.6 collective-permute-start.5
  50.9 2.9 %collective-permute-done.6.refs_6_ = bf16[16,5504]{1,0:T(8,128)(2,1)S(1)} collective-permute-done((bf16[16,5504]{1,0:T(8,128)(2,1)S(1)}, bf16[16,5504]{1,0:T(8,128)(2,1)S(1)}, u32[]{:S(2)}, u32[]{:S(2)}) %collective-permute-start.6) | collective-permute-done | bytes 176160 | tf_op jit(solution)/shard_map/ppermute | solution.py:59
  54.8 1.1 collective-permute-start.8
  55.9 1.6 collective-permute-start.7
  57.5 2.5 %shard_map.96 = (bf16[16,5504]{1,0:T(8,128)(2,1)S(1)}, bf16[16,5504]{1,0:T(8,128)(2,1)S(1)}, bf16[16,5504]{1,0:T(8,128)(2,1)S(1)}, f32[96,224]{1,0:T(8,128)S(1)}...) custom-call(bf16[336,2560]{1,0:T(8,128)(2,1)S(1)} %pad_maximum_fusion.refs_5_.refs_0_, ...), custom_call_target="tpu_custom_call" | custom-call | flops 566231040 | bytes 7249920 | tf_op jit(solution)/shard_map/pallas_call | solution.py:71
  60.0 2.5 %shard_map.97 = (bf16[16,5504]{1,0:T(8,128)(2,1)S(1)}, bf16[16,5504]{1,0:T(8,128)(2,1)S(1)}, bf16[16,5504]{1,0:T(8,128)(2,1)S(1)}, f32[96,224]{1,0:T(8,128)S(1)}...) custom-call(bf16[336,2560]{1,0:T(8,128)(2,1)S(1)} %pad_maximum_fusion.refs_5_.refs_0_, ...), custom_call_target="tpu_custom_call" | custom-call | flops 566231040 | bytes 7249920 | tf_op jit(solution)/shard_map/pallas_call | solution.py:71
  62.7 1.5 collective-permute-done.7.refs_4_
  64.2 1.6 collective-permute-start.10
  66.8 2.9 %collective-permute-done.10 = bf16[16,5504]{1,0:T(8,128)(2,1)S(1)} collective-permute-done((bf16[16,5504]{1,0:T(8,128)(2,1)S(1)}, bf16[16,5504]{1,0:T(8,128)(2,1)S(1)}, u32[]{:S(2)}, u32[]{:S(2)}) %collective-permute-start.10) | collective-permute-done | bytes 176160 | tf_op jit(solution)/shard_map/ppermute | solution.py:59
  69.7 1.6 collective-permute-done.11
  71.4 3.7 %collective-permute-start.13 = (bf16[16,5504]{1,0:T(8,128)(2,1)S(1)}, bf16[16,5504]{1,0:T(8,128)(2,1)S(1)}, u32[]{:S(2)}, u32[]{:S(2)}) collective-permute-start(bf16[16,5504]{1,0:T(8,128)(2,1)S(1)} %get-tuple-element.138.refs_7_), channel_id=1, source_target_pairs={{0,10},{1,11},{2,8},{3,9},{4,14},{5,15},{6,12},{7,13},{8,18},{9,19... | collective-permute-start | bytes 528392 | tf_op jit(solution)/shard_map/ppermute | solution.py:59
  76.1 7.5 %collective-permute-done.12.refs_4_ = bf16[16,5504]{1,0:T(8,128)(2,1)S(1)} collective-permute-done((bf16[16,5504]{1,0:T(8,128)(2,1)S(1)}, bf16[16,5504]{1,0:T(8,128)(2,1)S(1)}, u32[]{:S(2)}, u32[]{:S(2)}) %collective-permute-start.12) | collective-permute-done | bytes 176160 | tf_op jit(solution)/shard_map/ppermute | solution.py:59
  85.1 2.2 %collective-permute-start.17 = (bf16[16,5504]{1,0:T(8,128)(2,1)S(1)}, bf16[16,5504]{1,0:T(8,128)(2,1)S(1)}, u32[]{:S(2)}, u32[]{:S(2)}) collective-permute-start(bf16[16,5504]{1,0:T(8,128)(2,1)S(1)} %get-tuple-element.155), channel_id=1, source_target_pairs={{0,4},{1,5},{2,6},{3,7},{4,0},{5,1},{6,2},{7,3},{8,12},{9,13},{10,... | collective-permute-start | bytes 528392 | tf_op jit(solution)/shard_map/ppermute | solution.py:59
  88.8 7.2 %collective-permute-done.17.refs_9_ = bf16[16,5504]{1,0:T(8,128)(2,1)S(1)} collective-permute-done((bf16[16,5504]{1,0:T(8,128)(2,1)S(1)}, bf16[16,5504]{1,0:T(8,128)(2,1)S(1)}, u32[]{:S(2)}, u32[]{:S(2)}) %collective-permute-start.17) | collective-permute-done | bytes 176160 | tf_op jit(solution)/shard_map/ppermute | solution.py:59
  96.5 1.0 collective-permute-start.21
  99.2 2.6 %shard_map.101 = (bf16[16,5504]{1,0:T(8,128)(2,1)S(1)}, bf16[16,5504]{1,0:T(8,128)(2,1)S(1)}, bf16[16,5504]{1,0:T(8,128)(2,1)S(1)}, f32[96,224]{1,0:T(8,128)S(1)...) custom-call(bf16[336,2560]{1,0:T(8,128)(2,1)S(1)} %pad_maximum_fusion.refs_5_.refs_0_, ...), custom_call_target="tpu_custom_call" | custom-call | flops 566231040 | bytes 7397376 | tf_op jit(solution)/shard_map/pallas_call | solution.py:71
  102.9 2.6 %shard_map.102 = (bf16[16,5504]{1,0:T(8,128)(2,1)S(1)}, bf16[16,5504]{1,0:T(8,128)(2,1)S(1)}, bf16[16,5504]{1,0:T(8,128)(2,1)S(1)}, f32[96,224]{1,0:T(8,128)S(1)...) custom-call(bf16[336,2560]{1,0:T(8,128)(2,1)S(1)} %pad_maximum_fusion.refs_5_.refs_0_, ...), custom_call_target="tpu_custom_call" | custom-call | flops 566231040 | bytes 7397376 | tf_op jit(solution)/shard_map/pallas_call | solution.py:71
  105.6 1.1 collective-permute-start.22
  106.7 1.0 collective-permute-start.23
  108.6 1.1 collective-permute-start.25
  111.1 1.0 collective-permute-done.23
  112.2 1.7 %collective-permute-start.27 = (bf16[16,5504]{1,0:T(8,128)(2,1)S(1)}, bf16[16,5504]{1,0:T(8,128)(2,1)S(1)}, u32[]{:S(2)}, u32[]{:S(2)}) collective-permute-start(bf16[16,5504]{1,0:T(8,128)(2,1)S(1)} %get-tuple-element.179.refs_11_), channel_id=1, source_target_pairs={{0,26},{1,27},{2,24},{3,25},{4,30},{5,31},{6,28},{7,29},{8,2},{9,3... | collective-permute-start | bytes 528392 | tf_op jit(solution)/shard_map/ppermute | solution.py:59
  114.0 2.8 %collective-permute-done.25 = bf16[16,5504]{1,0:T(8,128)(2,1)S(1)} collective-permute-done((bf16[16,5504]{1,0:T(8,128)(2,1)S(1)}, bf16[16,5504]{1,0:T(8,128)(2,1)S(1)}, u32[]{:S(2)}, u32[]{:S(2)}) %collective-permute-start.25) | collective-permute-done | bytes 176160 | tf_op jit(solution)/shard_map/ppermute | solution.py:59
  116.9 5.5 %collective-permute-done.24.refs_2_ = bf16[16,5504]{1,0:T(8,128)(2,1)S(1)} collective-permute-done((bf16[16,5504]{1,0:T(8,128)(2,1)S(1)}, bf16[16,5504]{1,0:T(8,128)(2,1)S(1)}, u32[]{:S(2)}, u32[]{:S(2)}) %collective-permute-start.24) | collective-permute-done | bytes 176160 | tf_op jit(solution)/shard_map/ppermute | solution.py:59
  123.1 1.1 collective-permute-done.29.refs_5_
  124.2 1.0 shard_map.104
  126.9 1.0 collective-permute-start.31
  127.9 9.3 %collective-permute-done.30.refs_9_ = bf16[16,5504]{1,0:T(8,128)(2,1)S(1)} collective-permute-done((bf16[16,5504]{1,0:T(8,128)(2,1)S(1)}, bf16[16,5504]{1,0:T(8,128)(2,1)S(1)}, u32[]{:S(2)}, u32[]{:S(2)}) %collective-permute-start.30) | collective-permute-done | bytes 176160 | tf_op jit(solution)/shard_map/ppermute | solution.py:59
  137.3 1.0 collective-permute-start.34
  138.3 2.0 %shard_map.105 = (bf16[16,5504]{1,0:T(8,128)(2,1)S(1)}, bf16[16,5504]{1,0:T(8,128)(2,1)S(1)}, bf16[16,5504]{1,0:T(8,128)(2,1)S(1)}) custom-call(bf16[336,2560]{1,0:T(8,128)(2,1)S(1)} %pad_maximum_fusion.refs_5_.refs_0_, bf16[336,2560]{1,0:T(8,128)(2,1)S(1)} %collective-permute-done.refs_1_, bf16[240,2560]{1,0:T(8,128)(2,1)S(1)} %pad_maximum_fusion.1.refs_6_.refs_2_, ...), custom_call_target="tpu_custom_call" | custom-call | flops 566231040 | bytes 7249920 | tf_op jit(solution)/shard_map/pallas_call | solution.py:71
  140.3 3.3 %collective-permute-done.34.refs_10_ = bf16[16,5504]{1,0:T(8,128)(2,1)S(1)} collective-permute-done((bf16[16,5504]{1,0:T(8,128)(2,1)S(1)}, bf16[16,5504]{1,0:T(8,128)(2,1)S(1)}, u32[]{:S(2)}, u32[]{:S(2)}) %collective-permute-start.34) | collective-permute-done | bytes 176160 | tf_op jit(solution)/shard_map/ppermute | solution.py:59
  144.4 2.0 %shard_map.106 = (bf16[16,5504]{1,0:T(8,128)(2,1)S(1)}, bf16[16,5504]{1,0:T(8,128)(2,1)S(1)}, bf16[16,5504]{1,0:T(8,128)(2,1)S(1)}) custom-call(bf16[336,2560]{1,0:T(8,128)(2,1)S(1)} %pad_maximum_fusion.refs_5_.refs_0_, bf16[336,2560]{1,0:T(8,128)(2,1)S(1)} %collective-permute-done.refs_1_, bf16[240,2560]{1,0:T(8,128)(2,1)S(1)} %pad_maximum_fusion.1.refs_6_.refs_2_, ...), custom_call_target="tpu_custom_call" | custom-call | flops 566231040 | bytes 7249920 | tf_op jit(solution)/shard_map/pallas_call | solution.py:71
  148.6 1.9 %collective-permute-start.37 = (bf16[16,5504]{1,0:T(8,128)(2,1)S(1)}, bf16[16,5504]{1,0:T(8,128)(2,1)S(1)}, u32[]{:S(2)}, u32[]{:S(2)}) collective-permute-start(bf16[16,5504]{1,0:T(8,128)(2,1)S(1)} %add_convert_fusion.1), channel_id=1, source_target_pairs={{0,4},{1,5},{2,6},{3,7},{4,0},{5,1},{6,2},{7,3},{8,12},{9,13},{10,... | collective-permute-start | bytes 528392 | tf_op jit(solution)/shard_map/ppermute | solution.py:59
  150.5 3.0 %collective-permute-done.35 = bf16[16,5504]{1,0:T(8,128)(2,1)S(1)} collective-permute-done((bf16[16,5504]{1,0:T(8,128)(2,1)S(1)}, bf16[16,5504]{1,0:T(8,128)(2,1)S(1)}, u32[]{:S(2)}, u32[]{:S(2)}) %collective-permute-start.35) | collective-permute-done | bytes 176160 | tf_op jit(solution)/shard_map/ppermute | solution.py:59
  153.6 4.6 %collective-permute-done.37.refs_2_ = bf16[16,5504]{1,0:T(8,128)(2,1)S(1)} collective-permute-done((bf16[16,5504]{1,0:T(8,128)(2,1)S(1)}, bf16[16,5504]{1,0:T(8,128)(2,1)S(1)}, u32[]{:S(2)}, u32[]{:S(2)}) %collective-permute-start.37) | collective-permute-done | bytes 176160 | tf_op jit(solution)/shard_map/ppermute | solution.py:59
  158.2 1.1 collective-permute-start.39
  159.4 2.2 %collective-permute-start.40 = (bf16[16,5504]{1,0:T(8,128)(2,1)S(1)}, bf16[16,5504]{1,0:T(8,128)(2,1)S(1)}, u32[]{:S(2)}, u32[]{:S(2)}) collective-permute-start(bf16[16,5504]{1,0:T(8,128)(2,1)S(1)} %add_convert_fusion), channel_id=1, source_target_pairs={{0,4},{1,5},{2,6},{3,7},{4,0},{5,1},{6,2},{7,3},{8,12},{9,13},{10,... | collective-permute-start | bytes 528392 | tf_op jit(solution)/shard_map/ppermute | solution.py:59
  162.4 6.4 %collective-permute-done.38.refs_3_ = bf16[16,5504]{1,0:T(8,128)(2,1)S(1)} collective-permute-done((bf16[16,5504]{1,0:T(8,128)(2,1)S(1)}, bf16[16,5504]{1,0:T(8,128)(2,1)S(1)}, u32[]{:S(2)}, u32[]{:S(2)}) %collective-permute-start.38) | collective-permute-done | bytes 176160 | tf_op jit(solution)/shard_map/ppermute | solution.py:59
  168.9 1.1 shard_map.108
  170.8 1.3 shard_map.109
  (79 shorter events, 23.2 us)
Async XLA Ops:
  3.1 45.2 %collective-permute-start = (bf16[336,2560]{1,0:T(8,128)(2,1)S(1)}, bf16[336,2560]{1,0:T(8,128)(2,1)S(1)}, u32[]{:S(2)}, u32[]{:S(2)}) collective-permute-start(bf16[336,2560]{1,0:T(8,128)(2,1)S(1)} %pad_maximum_fusion.refs_5_.refs_0_), channel_id=1, source_target_pairs={{0,1},{1,0},{2,3},{3,2},{4,5},{5,4},{6,7},{7,6},{8,9},{9,8},{10,11... | collective-permute-start | bytes 5160968 | tf_op jit(solution)/shard_map/ppermute | solution.py:59
  7.2 2.9 %copy-start = (bf16[1,64,2560]{2,1,0:T(8,128)(2,1)S(1)}, bf16[1,64,2560]{2,1,0:T(8,128)(2,1)}, u32[]{:S(2)}) copy-start(bf16[1,64,2560]{2,1,0:T(8,128)(2,1)} %param.15) | copy-start | bytes 983044
  7.2 2.9 %copy-start.1 = (bf16[1,64,2560]{2,1,0:T(8,128)(2,1)S(1)}, bf16[1,64,2560]{2,1,0:T(8,128)(2,1)}, u32[]{:S(2)}) copy-start(bf16[1,64,2560]{2,1,0:T(8,128)(2,1)} %param.8) | copy-start | bytes 983044
  7.2 2.9 %copy-start.2 = (f32[1,2560]{1,0:T(1,128)S(1)}, f32[1,2560]{1,0:T(1,128)}, u32[]{:S(2)}) copy-start(f32[1,2560]{1,0:T(1,128)} %refs_3_.3) | copy-start | bytes 30724
  7.2 2.9 %copy-start.3 = (s32[1,2,64,1]{2,3,1,0:T(1,128)S(1)}, s32[1,2,64,1]{2,3,1,0:T(1,128)}, u32[]{:S(2)}) copy-start(s32[1,2,64,1]{2,3,1,0:T(1,128)} %param.13) | copy-start | bytes 1540
  7.2 2.8 %copy-start.4 = (f32[1,2,64,1]{2,3,1,0:T(1,128)S(1)}, f32[1,2,64,1]{2,3,1,0:T(1,128)}, u32[]{:S(2)}) copy-start(f32[1,2,64,1]{2,3,1,0:T(1,128)} %param.14) | copy-start | bytes 1540
  8.4 39.9 %collective-permute-start.1 = (bf16[240,2560]{1,0:T(8,128)(2,1)S(1)}, bf16[240,2560]{1,0:T(8,128)(2,1)S(1)}, u32[]{:S(2)}, u32[]{:S(2)}) collective-permute-start(bf16[240,2560]{1,0:T(8,128)(2,1)S(1)} %pad_maximum_fusion.1.refs_6_.refs_2_), channel_id=1, source_target_pairs={{0,2},{1,3},{2,0},{3,1},{4,6},{5,7},{6,4},{7,5},{8,10},{9,11},{10,... | collective-permute-start | bytes 3686408 | tf_op jit(solution)/shard_map/ppermute | solution.py:59
  10.9 37.3 %collective-permute-start.2 = (bf16[32,5504]{1,0:T(8,128)(2,1)S(1)}, bf16[32,5504]{1,0:T(8,128)(2,1)S(1)}, u32[]{:S(2)}, u32[]{:S(2)}) collective-permute-start(bf16[32,5504]{1,0:T(8,128)(2,1)S(1)} %get-tuple-element.110), channel_id=1, source_target_pairs={{0,4},{1,5},{2,6},{3,7},{4,0},{5,1},{6,2},{7,3},{8,12},{9,13},{10,... | collective-permute-start | bytes 1056776 | tf_op jit(solution)/shard_map/ppermute | solution.py:59
  13.6 33.9 %collective-permute-start.4 = (bf16[16,5504]{1,0:T(8,128)(2,1)S(1)}, bf16[16,5504]{1,0:T(8,128)(2,1)S(1)}, u32[]{:S(2)}, u32[]{:S(2)}) collective-permute-start(bf16[16,5504]{1,0:T(8,128)(2,1)S(1)} %get-tuple-element.122.refs_5_), channel_id=1, source_target_pairs={{0,1},{1,0},{2,3},{3,2},{4,5},{5,4},{6,7},{7,6},{8,9},{9,8},{10,11... | collective-permute-start | bytes 528392 | tf_op jit(solution)/shard_map/ppermute | solution.py:59
  14.1 34.2 %collective-permute-start.3 = (bf16[16,5504]{1,0:T(8,128)(2,1)S(1)}, bf16[16,5504]{1,0:T(8,128)(2,1)S(1)}, u32[]{:S(2)}, u32[]{:S(2)}) collective-permute-start(bf16[16,5504]{1,0:T(8,128)(2,1)S(1)} %get-tuple-element.122.refs_5_), channel_id=1, source_target_pairs={{0,2},{1,3},{2,0},{3,1},{4,6},{5,7},{6,4},{7,5},{8,10},{9,11},{10,... | collective-permute-start | bytes 528392 | tf_op jit(solution)/shard_map/ppermute | solution.py:59
  48.3 5.5 %collective-permute-start.6 = (bf16[16,5504]{1,0:T(8,128)(2,1)S(1)}, bf16[16,5504]{1,0:T(8,128)(2,1)S(1)}, u32[]{:S(2)}, u32[]{:S(2)}) collective-permute-start(bf16[16,5504]{1,0:T(8,128)(2,1)S(1)} %get-tuple-element.119.refs_5_), channel_id=1, source_target_pairs={{0,1},{1,0},{2,3},{3,2},{4,5},{5,4},{6,7},{7,6},{8,9},{9,8},{10,11... | collective-permute-start | bytes 528392 | tf_op jit(solution)/shard_map/ppermute | solution.py:59
  49.3 5.5 %collective-permute-start.5 = (bf16[16,5504]{1,0:T(8,128)(2,1)S(1)}, bf16[16,5504]{1,0:T(8,128)(2,1)S(1)}, u32[]{:S(2)}, u32[]{:S(2)}) collective-permute-start(bf16[16,5504]{1,0:T(8,128)(2,1)S(1)} %get-tuple-element.119.refs_5_), channel_id=1, source_target_pairs={{0,2},{1,3},{2,0},{3,1},{4,6},{5,7},{6,4},{7,5},{8,10},{9,11},{10,... | collective-permute-start | bytes 528392 | tf_op jit(solution)/shard_map/ppermute | solution.py:59
  54.8 8.0 %collective-permute-start.8 = (bf16[32,5504]{1,0:T(8,128)(2,1)S(1)}, bf16[32,5504]{1,0:T(8,128)(2,1)S(1)}, u32[]{:S(2)}, u32[]{:S(2)}) collective-permute-start(bf16[32,5504]{1,0:T(8,128)(2,1)S(1)} %pad_maximum_fusion.2.refs_5_), channel_id=1, source_target_pairs={{0,1},{1,0},{2,3},{3,2},{4,5},{5,4},{6,7},{7,6},{8,9},{9,8},{10,11... | collective-permute-start | bytes 1056776 | tf_op jit(solution)/shard_map/ppermute | solution.py:59
  55.9 8.3 %collective-permute-start.7 = (bf16[32,5504]{1,0:T(8,128)(2,1)S(1)}, bf16[32,5504]{1,0:T(8,128)(2,1)S(1)}, u32[]{:S(2)}, u32[]{:S(2)}) collective-permute-start(bf16[32,5504]{1,0:T(8,128)(2,1)S(1)} %pad_maximum_fusion.2.refs_5_), channel_id=1, source_target_pairs={{0,2},{1,3},{2,0},{3,1},{4,6},{5,7},{6,4},{7,5},{8,10},{9,11},{10,... | collective-permute-start | bytes 1056776 | tf_op jit(solution)/shard_map/ppermute | solution.py:59
  64.2 5.5 %collective-permute-start.10 = (bf16[16,5504]{1,0:T(8,128)(2,1)S(1)}, bf16[16,5504]{1,0:T(8,128)(2,1)S(1)}, u32[]{:S(2)}, u32[]{:S(2)}) collective-permute-start(bf16[16,5504]{1,0:T(8,128)(2,1)S(1)} %get-tuple-element.133), channel_id=1, source_target_pairs={{0,2},{1,3},{2,0},{3,1},{4,6},{5,7},{6,4},{7,5},{8,10},{9,11},{10,... | collective-permute-start | bytes 528392 | tf_op jit(solution)/shard_map/ppermute | solution.py:59
  65.8 5.5 %collective-permute-start.11 = (bf16[16,5504]{1,0:T(8,128)(2,1)S(1)}, bf16[16,5504]{1,0:T(8,128)(2,1)S(1)}, u32[]{:S(2)}, u32[]{:S(2)}) collective-permute-start(bf16[16,5504]{1,0:T(8,128)(2,1)S(1)} %get-tuple-element.134), channel_id=1, source_target_pairs={{0,1},{1,0},{2,3},{3,2},{4,5},{5,4},{6,7},{7,6},{8,9},{9,8},{10,11... | collective-permute-start | bytes 528392 | tf_op jit(solution)/shard_map/ppermute | solution.py:59
  66.8 17.4 %collective-permute-start.9 = (bf16[80,2560]{1,0:T(8,128)(2,1)S(1)}, bf16[80,2560]{1,0:T(8,128)(2,1)S(1)}, u32[]{:S(2)}, u32[]{:S(2)}) collective-permute-start(bf16[80,2560]{1,0:T(8,128)(2,1)S(1)} %get-tuple-element.130), channel_id=1, source_target_pairs={{0,8},{1,9},{2,10},{3,11},{4,12},{5,13},{6,14},{7,15},{8,16},{9,17... | collective-permute-start | bytes 1228808 | tf_op jit(solution)/shard_map/ppermute | solution.py:59
  71.3 12.3 %collective-permute-start.12 = (bf16[16,5504]{1,0:T(8,128)(2,1)S(1)}, bf16[16,5504]{1,0:T(8,128)(2,1)S(1)}, u32[]{:S(2)}, u32[]{:S(2)}) collective-permute-start(bf16[16,5504]{1,0:T(8,128)(2,1)S(1)} %add_convert_fusion.3), channel_id=1, source_target_pairs={{0,12},{1,13},{2,14},{3,15},{4,8},{5,9},{6,10},{7,11},{8,20},{9,21... | collective-permute-start | bytes 528392 | tf_op jit(solution)/shard_map/ppermute | solution.py:59
  71.4 12.3 %collective-permute-start.13 = (bf16[16,5504]{1,0:T(8,128)(2,1)S(1)}, bf16[16,5504]{1,0:T(8,128)(2,1)S(1)}, u32[]{:S(2)}, u32[]{:S(2)}) collective-permute-start(bf16[16,5504]{1,0:T(8,128)(2,1)S(1)} %get-tuple-element.138.refs_7_), channel_id=1, source_target_pairs={{0,10},{1,11},{2,8},{3,9},{4,14},{5,15},{6,12},{7,13},{8,18},{9,19... | collective-permute-start | bytes 528392 | tf_op jit(solution)/shard_map/ppermute | solution.py:59
  75.1 8.6 %collective-permute-start.14 = (bf16[16,5504]{1,0:T(8,128)(2,1)S(1)}, bf16[16,5504]{1,0:T(8,128)(2,1)S(1)}, u32[]{:S(2)}, u32[]{:S(2)}) collective-permute-start(bf16[16,5504]{1,0:T(8,128)(2,1)S(1)} %get-tuple-element.139), channel_id=1, source_target_pairs={{0,9},{1,8},{2,11},{3,10},{4,13},{5,12},{6,15},{7,14},{8,17},{9,16... | collective-permute-start | bytes 528392 | tf_op jit(solution)/shard_map/ppermute | solution.py:59
  75.6 8.6 %collective-permute-start.15 = (bf16[16,5504]{1,0:T(8,128)(2,1)S(1)}, bf16[16,5504]{1,0:T(8,128)(2,1)S(1)}, u32[]{:S(2)}, u32[]{:S(2)}) collective-permute-start(bf16[16,5504]{1,0:T(8,128)(2,1)S(1)} %get-tuple-element.140), channel_id=1, source_target_pairs={{0,8},{1,9},{2,10},{3,11},{4,12},{5,13},{6,14},{7,15},{8,16},{9,17... | collective-permute-start | bytes 528392 | tf_op jit(solution)/shard_map/ppermute | solution.py:59
  85.1 10.9 %collective-permute-start.17 = (bf16[16,5504]{1,0:T(8,128)(2,1)S(1)}, bf16[16,5504]{1,0:T(8,128)(2,1)S(1)}, u32[]{:S(2)}, u32[]{:S(2)}) collective-permute-start(bf16[16,5504]{1,0:T(8,128)(2,1)S(1)} %get-tuple-element.155), channel_id=1, source_target_pairs={{0,4},{1,5},{2,6},{3,7},{4,0},{5,1},{6,2},{7,3},{8,12},{9,13},{10,... | collective-permute-start | bytes 528392 | tf_op jit(solution)/shard_map/ppermute | solution.py:59
  87.3 8.7 %collective-permute-start.19 = (bf16[16,5504]{1,0:T(8,128)(2,1)S(1)}, bf16[16,5504]{1,0:T(8,128)(2,1)S(1)}, u32[]{:S(2)}, u32[]{:S(2)}) collective-permute-start(bf16[16,5504]{1,0:T(8,128)(2,1)S(1)} %get-tuple-element.156.refs_9_), channel_id=1, source_target_pairs={{0,1},{1,0},{2,3},{3,2},{4,5},{5,4},{6,7},{7,6},{8,9},{9,8},{10,11... | collective-permute-start | bytes 528392 | tf_op jit(solution)/shard_map/ppermute | solution.py:59
  88.3 8.2 %collective-permute-start.18 = (bf16[16,5504]{1,0:T(8,128)(2,1)S(1)}, bf16[16,5504]{1,0:T(8,128)(2,1)S(1)}, u32[]{:S(2)}, u32[]{:S(2)}) collective-permute-start(bf16[16,5504]{1,0:T(8,128)(2,1)S(1)} %get-tuple-element.156.refs_9_), channel_id=1, source_target_pairs={{0,2},{1,3},{2,0},{3,1},{4,6},{5,7},{6,4},{7,5},{8,10},{9,11},{10,... | collective-permute-start | bytes 528392 | tf_op jit(solution)/shard_map/ppermute | solution.py:59
  96.5 5.8 %collective-permute-start.21 = (bf16[16,5504]{1,0:T(8,128)(2,1)S(1)}, bf16[16,5504]{1,0:T(8,128)(2,1)S(1)}, u32[]{:S(2)}, u32[]{:S(2)}) collective-permute-start(bf16[16,5504]{1,0:T(8,128)(2,1)S(1)} %collective-permute-done.17.refs_9_), channel_id=1, source_target_pairs={{0,1},{1,0},{2,3},{3,2},{4,5},{5,4},{6,7},{7,6},{8,9},{9,8},{10,11... | collective-permute-start | bytes 528392 | tf_op jit(solution)/shard_map/ppermute | solution.py:59
  97.5 5.5 %collective-permute-start.20 = (bf16[16,5504]{1,0:T(8,128)(2,1)S(1)}, bf16[16,5504]{1,0:T(8,128)(2,1)S(1)}, u32[]{:S(2)}, u32[]{:S(2)}) collective-permute-start(bf16[16,5504]{1,0:T(8,128)(2,1)S(1)} %collective-permute-done.17.refs_9_), channel_id=1, source_target_pairs={{0,2},{1,3},{2,0},{3,1},{4,6},{5,7},{6,4},{7,5},{8,10},{9,11},{10,... | collective-permute-start | bytes 528392 | tf_op jit(solution)/shard_map/ppermute | solution.py:59
  105.6 5.5 %collective-permute-start.22 = (bf16[16,5504]{1,0:T(8,128)(2,1)S(1)}, bf16[16,5504]{1,0:T(8,128)(2,1)S(1)}, u32[]{:S(2)}, u32[]{:S(2)}) collective-permute-start(bf16[16,5504]{1,0:T(8,128)(2,1)S(1)} %get-tuple-element.166), channel_id=1, source_target_pairs={{0,2},{1,3},{2,0},{3,1},{4,6},{5,7},{6,4},{7,5},{8,10},{9,11},{10,... | collective-permute-start | bytes 528392 | tf_op jit(solution)/shard_map/ppermute | solution.py:59
  106.7 5.5 %collective-permute-start.23 = (bf16[16,5504]{1,0:T(8,128)(2,1)S(1)}, bf16[16,5504]{1,0:T(8,128)(2,1)S(1)}, u32[]{:S(2)}, u32[]{:S(2)}) collective-permute-start(bf16[16,5504]{1,0:T(8,128)(2,1)S(1)} %get-tuple-element.167), channel_id=1, source_target_pairs={{0,1},{1,0},{2,3},{3,2},{4,5},{5,4},{6,7},{7,6},{8,9},{9,8},{10,11... | collective-permute-start | bytes 528392 | tf_op jit(solution)/shard_map/ppermute | solution.py:59
  107.7 16.5 %collective-permute-start.16 = (bf16[144,2560]{1,0:T(8,128)(2,1)S(1)}, bf16[144,2560]{1,0:T(8,128)(2,1)S(1)}, u32[]{:S(2)}, u32[]{:S(2)}) collective-permute-start(bf16[144,2560]{1,0:T(8,128)(2,1)S(1)} %get-tuple-element.146), channel_id=1, source_target_pairs={{0,24},{1,25},{2,26},{3,27},{4,28},{5,29},{6,30},{7,31},{8,0},{9,1... | collective-permute-start | bytes 2211848 | tf_op jit(solution)/shard_map/ppermute | solution.py:59
  108.6 8.2 %collective-permute-start.25 = (bf16[16,5504]{1,0:T(8,128)(2,1)S(1)}, bf16[16,5504]{1,0:T(8,128)(2,1)S(1)}, u32[]{:S(2)}, u32[]{:S(2)}) collective-permute-start(bf16[16,5504]{1,0:T(8,128)(2,1)S(1)} %get-tuple-element.176), channel_id=1, source_target_pairs={{0,2},{1,3},{2,0},{3,1},{4,6},{5,7},{6,4},{7,5},{8,10},{9,11},{10,... | collective-permute-start | bytes 528392 | tf_op jit(solution)/shard_map/ppermute | solution.py:59
  109.6 7.2 %collective-permute-start.26 = (bf16[16,5504]{1,0:T(8,128)(2,1)S(1)}, bf16[16,5504]{1,0:T(8,128)(2,1)S(1)}, u32[]{:S(2)}, u32[]{:S(2)}) collective-permute-start(bf16[16,5504]{1,0:T(8,128)(2,1)S(1)} %get-tuple-element.177), channel_id=1, source_target_pairs={{0,1},{1,0},{2,3},{3,2},{4,5},{5,4},{6,7},{7,6},{8,9},{9,8},{10,11... | collective-permute-start | bytes 528392 | tf_op jit(solution)/shard_map/ppermute | solution.py:59
  112.2 10.2 %collective-permute-start.24 = (bf16[16,5504]{1,0:T(8,128)(2,1)S(1)}, bf16[16,5504]{1,0:T(8,128)(2,1)S(1)}, u32[]{:S(2)}, u32[]{:S(2)}) collective-permute-start(bf16[16,5504]{1,0:T(8,128)(2,1)S(1)} %add_convert_fusion.2), channel_id=1, source_target_pairs={{0,28},{1,29},{2,30},{3,31},{4,24},{5,25},{6,26},{7,27},{8,4},{9,5... | collective-permute-start | bytes 528392 | tf_op jit(solution)/shard_map/ppermute | solution.py:59
  112.2 10.4 %collective-permute-start.27 = (bf16[16,5504]{1,0:T(8,128)(2,1)S(1)}, bf16[16,5504]{1,0:T(8,128)(2,1)S(1)}, u32[]{:S(2)}, u32[]{:S(2)}) collective-permute-start(bf16[16,5504]{1,0:T(8,128)(2,1)S(1)} %get-tuple-element.179.refs_11_), channel_id=1, source_target_pairs={{0,26},{1,27},{2,24},{3,25},{4,30},{5,31},{6,28},{7,29},{8,2},{9,3... | collective-permute-start | bytes 528392 | tf_op jit(solution)/shard_map/ppermute | solution.py:59
  116.8 6.3 %collective-permute-start.28 = (bf16[16,5504]{1,0:T(8,128)(2,1)S(1)}, bf16[16,5504]{1,0:T(8,128)(2,1)S(1)}, u32[]{:S(2)}, u32[]{:S(2)}) collective-permute-start(bf16[16,5504]{1,0:T(8,128)(2,1)S(1)} %get-tuple-element.180), channel_id=1, source_target_pairs={{0,25},{1,24},{2,27},{3,26},{4,29},{5,28},{6,31},{7,30},{8,1},{9,0... | collective-permute-start | bytes 528392 | tf_op jit(solution)/shard_map/ppermute | solution.py:59
  116.8 7.4 %collective-permute-start.29 = (bf16[16,5504]{1,0:T(8,128)(2,1)S(1)}, bf16[16,5504]{1,0:T(8,128)(2,1)S(1)}, u32[]{:S(2)}, u32[]{:S(2)}) collective-permute-start(bf16[16,5504]{1,0:T(8,128)(2,1)S(1)} %get-tuple-element.181), channel_id=1, source_target_pairs={{0,24},{1,25},{2,26},{3,27},{4,28},{5,29},{6,30},{7,31},{8,0},{9,1... | collective-permute-start | bytes 528392 | tf_op jit(solution)/shard_map/ppermute | solution.py:59
  125.2 12.0 %collective-permute-start.30 = (bf16[16,5504]{1,0:T(8,128)(2,1)S(1)}, bf16[16,5504]{1,0:T(8,128)(2,1)S(1)}, u32[]{:S(2)}, u32[]{:S(2)}) collective-permute-start(bf16[16,5504]{1,0:T(8,128)(2,1)S(1)} %get-tuple-element.182), channel_id=1, source_target_pairs={{0,4},{1,5},{2,6},{3,7},{4,0},{5,1},{6,2},{7,3},{8,12},{9,13},{10,... | collective-permute-start | bytes 528392 | tf_op jit(solution)/shard_map/ppermute | solution.py:59
  125.9 11.3 %collective-permute-start.32 = (bf16[16,5504]{1,0:T(8,128)(2,1)S(1)}, bf16[16,5504]{1,0:T(8,128)(2,1)S(1)}, u32[]{:S(2)}, u32[]{:S(2)}) collective-permute-start(bf16[16,5504]{1,0:T(8,128)(2,1)S(1)} %get-tuple-element.183.refs_9_), channel_id=1, source_target_pairs={{0,1},{1,0},{2,3},{3,2},{4,5},{5,4},{6,7},{7,6},{8,9},{9,8},{10,11... | collective-permute-start | bytes 528392 | tf_op jit(solution)/shard_map/ppermute | solution.py:59
  126.9 10.4 %collective-permute-start.31 = (bf16[16,5504]{1,0:T(8,128)(2,1)S(1)}, bf16[16,5504]{1,0:T(8,128)(2,1)S(1)}, u32[]{:S(2)}, u32[]{:S(2)}) collective-permute-start(bf16[16,5504]{1,0:T(8,128)(2,1)S(1)} %get-tuple-element.183.refs_9_), channel_id=1, source_target_pairs={{0,2},{1,3},{2,0},{3,1},{4,6},{5,7},{6,4},{7,5},{8,10},{9,11},{10,... | collective-permute-start | bytes 528392 | tf_op jit(solution)/shard_map/ppermute | solution.py:59
  137.3 6.3 %collective-permute-start.34 = (bf16[16,5504]{1,0:T(8,128)(2,1)S(1)}, bf16[16,5504]{1,0:T(8,128)(2,1)S(1)}, u32[]{:S(2)}, u32[]{:S(2)}) collective-permute-start(bf16[16,5504]{1,0:T(8,128)(2,1)S(1)} %collective-permute-done.30.refs_9_), channel_id=1, source_target_pairs={{0,1},{1,0},{2,3},{3,2},{4,5},{5,4},{6,7},{7,6},{8,9},{9,8},{10,11... | collective-permute-start | bytes 528392 | tf_op jit(solution)/shard_map/ppermute | solution.py:59
  138.3 6.1 %collective-permute-start.33 = (bf16[16,5504]{1,0:T(8,128)(2,1)S(1)}, bf16[16,5504]{1,0:T(8,128)(2,1)S(1)}, u32[]{:S(2)}, u32[]{:S(2)}) collective-permute-start(bf16[16,5504]{1,0:T(8,128)(2,1)S(1)} %collective-permute-done.30.refs_9_), channel_id=1, source_target_pairs={{0,2},{1,3},{2,0},{3,1},{4,6},{5,7},{6,4},{7,5},{8,10},{9,11},{10,... | collective-permute-start | bytes 528392 | tf_op jit(solution)/shard_map/ppermute | solution.py:59
  146.4 7.1 %collective-permute-start.35 = (bf16[16,5504]{1,0:T(8,128)(2,1)S(1)}, bf16[16,5504]{1,0:T(8,128)(2,1)S(1)}, u32[]{:S(2)}, u32[]{:S(2)}) collective-permute-start(bf16[16,5504]{1,0:T(8,128)(2,1)S(1)} %get-tuple-element.197), channel_id=1, source_target_pairs={{0,2},{1,3},{2,0},{3,1},{4,6},{5,7},{6,4},{7,5},{8,10},{9,11},{10,... | collective-permute-start | bytes 528392 | tf_op jit(solution)/shard_map/ppermute | solution.py:59
  146.7 6.8 %collective-permute-start.36 = (bf16[16,5504]{1,0:T(8,128)(2,1)S(1)}, bf16[16,5504]{1,0:T(8,128)(2,1)S(1)}, u32[]{:S(2)}, u32[]{:S(2)}) collective-permute-start(bf16[16,5504]{1,0:T(8,128)(2,1)S(1)} %get-tuple-element.198), channel_id=1, source_target_pairs={{0,1},{1,0},{2,3},{3,2},{4,5},{5,4},{6,7},{7,6},{8,9},{9,8},{10,11... | collective-permute-start | bytes 528392 | tf_op jit(solution)/shard_map/ppermute | solution.py:59
  148.6 9.7 %collective-permute-start.37 = (bf16[16,5504]{1,0:T(8,128)(2,1)S(1)}, bf16[16,5504]{1,0:T(8,128)(2,1)S(1)}, u32[]{:S(2)}, u32[]{:S(2)}) collective-permute-start(bf16[16,5504]{1,0:T(8,128)(2,1)S(1)} %add_convert_fusion.1), channel_id=1, source_target_pairs={{0,4},{1,5},{2,6},{3,7},{4,0},{5,1},{6,2},{7,3},{8,12},{9,13},{10,... | collective-permute-start | bytes 528392 | tf_op jit(solution)/shard_map/ppermute | solution.py:59
  158.2 10.6 %collective-permute-start.38 = (bf16[16,5504]{1,0:T(8,128)(2,1)S(1)}, bf16[16,5504]{1,0:T(8,128)(2,1)S(1)}, u32[]{:S(2)}, u32[]{:S(2)}) collective-permute-start(bf16[16,5504]{1,0:T(8,128)(2,1)S(1)} %get-tuple-element.210), channel_id=1, source_target_pairs={{0,2},{1,3},{2,0},{3,1},{4,6},{5,7},{6,4},{7,5},{8,10},{9,11},{10,... | collective-permute-start | bytes 528392 | tf_op jit(solution)/shard_map/ppermute | solution.py:59
  158.2 10.6 %collective-permute-start.39 = (bf16[16,5504]{1,0:T(8,128)(2,1)S(1)}, bf16[16,5504]{1,0:T(8,128)(2,1)S(1)}, u32[]{:S(2)}, u32[]{:S(2)}) collective-permute-start(bf16[16,5504]{1,0:T(8,128)(2,1)S(1)} %get-tuple-element.211), channel_id=1, source_target_pairs={{0,1},{1,0},{2,3},{3,2},{4,5},{5,4},{6,7},{7,6},{8,9},{9,8},{10,11... | collective-permute-start | bytes 528392 | tf_op jit(solution)/shard_map/ppermute | solution.py:59
  159.4 10.6 %collective-permute-start.40 = (bf16[16,5504]{1,0:T(8,128)(2,1)S(1)}, bf16[16,5504]{1,0:T(8,128)(2,1)S(1)}, u32[]{:S(2)}, u32[]{:S(2)}) collective-permute-start(bf16[16,5504]{1,0:T(8,128)(2,1)S(1)} %add_convert_fusion), channel_id=1, source_target_pairs={{0,4},{1,5},{2,6},{3,7},{4,0},{5,1},{6,2},{7,3},{8,12},{9,13},{10,... | collective-permute-start | bytes 528392 | tf_op jit(solution)/shard_map/ppermute | solution.py:59
  161.5 9.2 %collective-permute-start.41 = (bf16[16,5504]{1,0:T(8,128)(2,1)S(1)}, bf16[16,5504]{1,0:T(8,128)(2,1)S(1)}, u32[]{:S(2)}, u32[]{:S(2)}) collective-permute-start(bf16[16,5504]{1,0:T(8,128)(2,1)S(1)} %get-tuple-element.215.refs_11_), channel_id=1, source_target_pairs={{0,2},{1,3},{2,0},{3,1},{4,6},{5,7},{6,4},{7,5},{8,10},{9,11},{10,... | collective-permute-start | bytes 528392 | tf_op jit(solution)/shard_map/ppermute | solution.py:59
  161.6 9.2 %collective-permute-start.42 = (bf16[16,5504]{1,0:T(8,128)(2,1)S(1)}, bf16[16,5504]{1,0:T(8,128)(2,1)S(1)}, u32[]{:S(2)}, u32[]{:S(2)}) collective-permute-start(bf16[16,5504]{1,0:T(8,128)(2,1)S(1)} %get-tuple-element.216), channel_id=1, source_target_pairs={{0,1},{1,0},{2,3},{3,2},{4,5},{5,4},{6,7},{7,6},{8,9},{9,8},{10,11... | collective-permute-start | bytes 528392 | tf_op jit(solution)/shard_map/ppermute | solution.py:59
  (1 other events, 2.3 us)

commit v2 on v1

--- a/solution.py
+++ b/solution.py
@@ -493,8 +493,10 @@
         ]
 
     def give_back(cross, own, sections):
-        total, own = fence((sums(cross), own))
-        return home(total, sections) + own_home(own, sections)
+        total = sums(cross)
+        back = home(total, sections)
+        own, _ = fence((own, total))
+        return back + own_home(own, sections)
 
     units = w_gate.shape[3]
     cut = -(-units * 7 // 12 // ROWS) * ROWS
@@ -524,11 +526,11 @@
     cross0, cots = fence((cross0, cots))
     cots = around(cots)
 
-    own_out, own_kept0 = expert_call(forward_kernel, box, packs, own0, kept=2)
-    cross_out, cross_kept0 = expert_call(
-        forward_kernel, box, packs, cross0, kept=2, after=own_out[:1]
-    )
-    cross_out, cots, ahead = fence((cross_out, cots, ahead))
+    cross_out, cross_kept0 = expert_call(forward_kernel, box, packs, cross0, kept=2)
+    own_out, own_kept0 = expert_call(
+        forward_kernel, box, packs, own0, kept=2, after=list(cross_out[:1]) + list(cots)
+    )
+    cross_out, ahead = fence((cross_out, ahead))
     arrived0 = shift(ahead, sections=1)
     got = give_back(cross_out, own_out, 1)
     h1, behind, own1, *boxes1 = call(
@@ -557,6 +559,7 @@
     arrived1 = shift(behind, sections=-1)
     got = give_back(cross_grad, own_grad, -1)
     got[: experts - 1], fin_sums = fence((got[: experts - 1], sums(cross_fin)))
+    fin_back = home(fin_sums, 0)
     own_fin = down(own1, own_kept1)[0]
     g1, own_g, *boxes_g = call(
         bind(turn_kernel, box, experts),
@@ -567,16 +570,15 @@
         scratch=[picked],
     )
 
-    cross_g, own_z, own_x = fence(
-        (crossing_of(boxes_g), shift(own_g, flip=2), shift(own_g, flip=1))
+    cross_g, own_z, own_x, fin_back = fence(
+        (crossing_of(boxes_g), shift(own_g, flip=2), shift(own_g, flip=1), fin_back)
     )
     cross_g, own_g = around(cross_g), [own_z, own_g, own_x]
-    cross_g, fin_sums = fence((cross_g, fin_sums))
-    fin_back = home(fin_sums, 0)
     back = bind(expert_call, back_kernel, box, packs)
     own_grad = back(own_g, own_kept0)[0]
     cross_grad = back(cross_g, cross_kept0, after=own_grad[:1])[0]
-    total, own_grad, own_fin, fin_back = fence((sums(cross_grad), own_grad, own_fin, fin_back))
+    total = sums(cross_grad)
+    own_grad, own_fin, _ = fence((own_grad, own_fin, total))
     got = home(total, 0) + own_home(own_grad, 0)
     fin_own = own_home(own_fin, 0)
     (g0,) = call(

time: 172 us -> 169 us (0.983)
  starting transfers between devices: 42.6 us -> 39.5 us
    ppermute x43, starting transfers between devices: 42.6 us -> 39.5 us  [shift(): return lax.ppermute(value, ('section', 'expert'), pairs)]
  transfers between devices with their start and end apart: 43 -> 43, of which waited for: 28 -> 29; matrix products, arithmetic and copies ran while one was open for 1% -> 1% of each run, Pallas kernels for 9% -> 8%
where the time goes in v2:
time: 169 us
  waiting for transfers between devices  101 us (60%)
  starting transfers between devices  39.5 us (23%)
  Pallas kernels  23 us (14%)
  local copies, waits for them, and re-layouts  4.53 us (3%)
    ppermute x43, waiting for transfers between devices, shift(): return lax.ppermute(value, ('section', 'expert'), pairs)  101 us
    ppermute x43, starting transfers between devices, shift(): return lax.ppermute(value, ('section', 'expert'), pairs)  39.5 us
    pallas_call x15, Pallas kernels, call(): pl.pallas_call(reading, out_shape=list(outs), in_specs=[vmem] * read + [p...  23 us
  transfers between devices with their start and end apart: 43, of which 29 were waited for; matrix products, arithmetic and copies ran while one was open for 1% of the time, Pallas kernels for 8%

profile of v2, /device:TPU:0, one launch (start us, length us, event | category | flops | bytes accessed | tf_op | source)
XLA Modules:
  0.0 169.0 jit_solution(4613704032092910088)
XLA Ops:
  0.6 1.2 slice.40
  1.8 1.1 slice.41
  3.1 3.0 %collective-permute-start = (bf16[336,2560]{1,0:T(8,128)(2,1)S(1)}, bf16[336,2560]{1,0:T(8,128)(2,1)S(1)}, u32[]{:S(2)}, u32[]{:S(2)}) collective-permute-start(bf16[336,2560]{1,0:T(8,128)(2,1)S(1)} %pad_maximum_fusion.refs_5_.refs_0_), channel_id=1, source_target_pairs={{0,1},{1,0},{2,3},{3,2},{4,5},{5,4},{6,7},{7,6},{8,9},{9,8},{10,11... | collective-permute-start | bytes 5160968 | tf_op jit(solution)/shard_map/ppermute | solution.py:59
  7.2 1.1 slice.43
  8.4 1.6 collective-permute-start.1
  10.9 2.6 %collective-permute-start.2 = (bf16[32,5504]{1,0:T(8,128)(2,1)S(1)}, bf16[32,5504]{1,0:T(8,128)(2,1)S(1)}, u32[]{:S(2)}, u32[]{:S(2)}) collective-permute-start(bf16[32,5504]{1,0:T(8,128)(2,1)S(1)} %get-tuple-element.100), channel_id=1, source_target_pairs={{0,4},{1,5},{2,6},{3,7},{4,0},{5,1},{6,2},{7,3},{8,12},{9,13},{10,... | collective-permute-start | bytes 1056776 | tf_op jit(solution)/shard_map/ppermute | solution.py:59
  14.5 32.9 %collective-permute-done.4.refs_6_ = bf16[16,5504]{1,0:T(8,128)(2,1)S(1)} collective-permute-done((bf16[16,5504]{1,0:T(8,128)(2,1)S(1)}, bf16[16,5504]{1,0:T(8,128)(2,1)S(1)}, u32[]{:S(2)}, u32[]{:S(2)}) %collective-permute-start.4) | collective-permute-done | bytes 176160 | tf_op jit(solution)/shard_map/ppermute | solution.py:59
  49.3 1.6 collective-permute-start.5
  50.9 2.9 %collective-permute-done.6.refs_6_ = bf16[16,5504]{1,0:T(8,128)(2,1)S(1)} collective-permute-done((bf16[16,5504]{1,0:T(8,128)(2,1)S(1)}, bf16[16,5504]{1,0:T(8,128)(2,1)S(1)}, u32[]{:S(2)}, u32[]{:S(2)}) %collective-permute-start.6) | collective-permute-done | bytes 176160 | tf_op jit(solution)/shard_map/ppermute | solution.py:59
  54.8 2.5 %shard_map.96 = (bf16[16,5504]{1,0:T(8,128)(2,1)S(1)}, bf16[16,5504]{1,0:T(8,128)(2,1)S(1)}, bf16[16,5504]{1,0:T(8,128)(2,1)S(1)}, f32[96,224]{1,0:T(8,128)S(1)}...) custom-call(bf16[336,2560]{1,0:T(8,128)(2,1)S(1)} %pad_maximum_fusion.refs_5_.refs_0_, ...), custom_call_target="tpu_custom_call" | custom-call | flops 566231040 | bytes 7249920 | tf_op jit(solution)/shard_map/pallas_call | solution.py:71
  57.2 1.6 collective-permute-start.8
  58.9 1.1 collective-permute-start.9
  61.3 3.2 %collective-permute-done.8 = bf16[16,5504]{1,0:T(8,128)(2,1)S(1)} collective-permute-done((bf16[16,5504]{1,0:T(8,128)(2,1)S(1)}, bf16[16,5504]{1,0:T(8,128)(2,1)S(1)}, u32[]{:S(2)}, u32[]{:S(2)}) %collective-permute-start.8) | collective-permute-done | bytes 176160 | tf_op jit(solution)/shard_map/ppermute | solution.py:59
  64.5 1.7 %collective-permute-done.9 = bf16[16,5504]{1,0:T(8,128)(2,1)S(1)} collective-permute-done((bf16[16,5504]{1,0:T(8,128)(2,1)S(1)}, bf16[16,5504]{1,0:T(8,128)(2,1)S(1)}, u32[]{:S(2)}, u32[]{:S(2)}) %collective-permute-start.9) | collective-permute-done | bytes 176160 | tf_op jit(solution)/shard_map/ppermute | solution.py:59
  66.4 3.9 %collective-permute-done.12.refs_10_.refs_6_ = bf16[32,5504]{1,0:T(8,128)(2,1)S(1)} collective-permute-done((bf16[32,5504]{1,0:T(8,128)(2,1)S(1)}, bf16[32,5504]{1,0:T(8,128)(2,1)S(1)}, u32[]{:S(2)}, u32[]{:S(2)}) %collective-permute-start.12) | collective-permute-done | bytes 352288 | tf_op jit(solution)/shard_map/ppermute | solution.py:59
  70.3 2.5 %shard_map.97 = (bf16[16,5504]{1,0:T(8,128)(2,1)S(1)}, bf16[16,5504]{1,0:T(8,128)(2,1)S(1)}, bf16[16,5504]{1,0:T(8,128)(2,1)S(1)}, f32[96,224]{1,0:T(8,128)S(1)}...) custom-call(bf16[336,2560]{1,0:T(8,128)(2,1)S(1)} %pad_maximum_fusion.refs_5_.refs_0_, ...), custom_call_target="tpu_custom_call" | custom-call | flops 566231040 | bytes 7249920 | tf_op jit(solution)/shard_map/pallas_call | solution.py:71
  72.9 1.9 %collective-permute-start.14 = (bf16[16,5504]{1,0:T(8,128)(2,1)S(1)}, bf16[16,5504]{1,0:T(8,128)(2,1)S(1)}, u32[]{:S(2)}, u32[]{:S(2)}) collective-permute-start(bf16[16,5504]{1,0:T(8,128)(2,1)S(1)} %get-tuple-element.128), channel_id=1, source_target_pairs={{0,9},{1,8},{2,11},{3,10},{4,13},{5,12},{6,15},{7,14},{8,17},{9,16... | collective-permute-start | bytes 528392 | tf_op jit(solution)/shard_map/ppermute | solution.py:59
  74.8 4.2 %collective-permute-done.10.refs_4_ = bf16[16,5504]{1,0:T(8,128)(2,1)S(1)} collective-permute-done((bf16[16,5504]{1,0:T(8,128)(2,1)S(1)}, bf16[16,5504]{1,0:T(8,128)(2,1)S(1)}, u32[]{:S(2)}, u32[]{:S(2)}) %collective-permute-start.10) | collective-permute-done | bytes 176160 | tf_op jit(solution)/shard_map/ppermute | solution.py:59
  79.0 2.5 %collective-permute-done.13.refs_5_ = bf16[16,5504]{1,0:T(8,128)(2,1)S(1)} collective-permute-done((bf16[16,5504]{1,0:T(8,128)(2,1)S(1)}, bf16[16,5504]{1,0:T(8,128)(2,1)S(1)}, u32[]{:S(2)}, u32[]{:S(2)}) %collective-permute-start.13) | collective-permute-done | bytes 176160 | tf_op jit(solution)/shard_map/ppermute | solution.py:59
  81.6 1.7 %collective-permute-done.15.refs_7_ = bf16[16,5504]{1,0:T(8,128)(2,1)S(1)} collective-permute-done((bf16[16,5504]{1,0:T(8,128)(2,1)S(1)}, bf16[16,5504]{1,0:T(8,128)(2,1)S(1)}, u32[]{:S(2)}, u32[]{:S(2)}) %collective-permute-start.15) | collective-permute-done | bytes 176160 | tf_op jit(solution)/shard_map/ppermute | solution.py:59
  84.3 2.0 %collective-permute-start.17 = (bf16[16,5504]{1,0:T(8,128)(2,1)S(1)}, bf16[16,5504]{1,0:T(8,128)(2,1)S(1)}, u32[]{:S(2)}, u32[]{:S(2)}) collective-permute-start(bf16[16,5504]{1,0:T(8,128)(2,1)S(1)} %get-tuple-element.137), channel_id=1, source_target_pairs={{0,4},{1,5},{2,6},{3,7},{4,0},{5,1},{6,2},{7,3},{8,12},{9,13},{10,... | collective-permute-start | bytes 528392 | tf_op jit(solution)/shard_map/ppermute | solution.py:59
  87.2 1.2 collective-permute-start.18
  88.4 6.4 %collective-permute-done.17.refs_9_ = bf16[16,5504]{1,0:T(8,128)(2,1)S(1)} collective-permute-done((bf16[16,5504]{1,0:T(8,128)(2,1)S(1)}, bf16[16,5504]{1,0:T(8,128)(2,1)S(1)}, u32[]{:S(2)}, u32[]{:S(2)}) %collective-permute-start.17) | collective-permute-done | bytes 176160 | tf_op jit(solution)/shard_map/ppermute | solution.py:59
  94.8 1.6 collective-permute-done.18.refs_8_
  96.4 1.4 collective-permute-start.21
  99.6 2.6 %shard_map.101 = (bf16[16,5504]{1,0:T(8,128)(2,1)S(1)}, bf16[16,5504]{1,0:T(8,128)(2,1)S(1)}, bf16[16,5504]{1,0:T(8,128)(2,1)S(1)}, f32[96,224]{1,0:T(8,128)S(1)...) custom-call(bf16[336,2560]{1,0:T(8,128)(2,1)S(1)} %pad_maximum_fusion.refs_5_.refs_0_, ...), custom_call_target="tpu_custom_call" | custom-call | flops 566231040 | bytes 7397376 | tf_op jit(solution)/shard_map/pallas_call | solution.py:71
  102.2 1.0 collective-permute-done.20.refs_8_
  103.3 2.6 %shard_map.102 = (bf16[16,5504]{1,0:T(8,128)(2,1)S(1)}, bf16[16,5504]{1,0:T(8,128)(2,1)S(1)}, bf16[16,5504]{1,0:T(8,128)(2,1)S(1)}, f32[96,224]{1,0:T(8,128)S(1)...) custom-call(bf16[336,2560]{1,0:T(8,128)(2,1)S(1)} %pad_maximum_fusion.refs_5_.refs_0_, ...), custom_call_target="tpu_custom_call" | custom-call | flops 566231040 | bytes 7397376 | tf_op jit(solution)/shard_map/pallas_call | solution.py:71
  105.9 1.0 collective-permute-start.22
  108.4 1.1 collective-permute-start.25
  109.5 1.4 collective-permute-start.26
  111.4 1.1 collective-permute-done.23
  113.1 3.7 %collective-permute-done.25 = bf16[16,5504]{1,0:T(8,128)(2,1)S(1)} collective-permute-done((bf16[16,5504]{1,0:T(8,128)(2,1)S(1)}, bf16[16,5504]{1,0:T(8,128)(2,1)S(1)}, u32[]{:S(2)}, u32[]{:S(2)}) %collective-permute-start.25) | collective-permute-done | bytes 176160 | tf_op jit(solution)/shard_map/ppermute | solution.py:59
  117.5 4.7 %collective-permute-done.24.refs_2_ = bf16[16,5504]{1,0:T(8,128)(2,1)S(1)} collective-permute-done((bf16[16,5504]{1,0:T(8,128)(2,1)S(1)}, bf16[16,5504]{1,0:T(8,128)(2,1)S(1)}, u32[]{:S(2)}, u32[]{:S(2)}) %collective-permute-start.24) | collective-permute-done | bytes 176160 | tf_op jit(solution)/shard_map/ppermute | solution.py:59
  127.6 9.1 %collective-permute-done.33.refs_2_ = bf16[16,5504]{1,0:T(8,128)(2,1)S(1)} collective-permute-done((bf16[16,5504]{1,0:T(8,128)(2,1)S(1)}, bf16[16,5504]{1,0:T(8,128)(2,1)S(1)}, u32[]{:S(2)}, u32[]{:S(2)}) %collective-permute-start.33) | collective-permute-done | bytes 176160 | tf_op jit(solution)/shard_map/ppermute | solution.py:59
  136.8 3.8 %collective-permute-done.30.refs_9_ = bf16[16,5504]{1,0:T(8,128)(2,1)S(1)} collective-permute-done((bf16[16,5504]{1,0:T(8,128)(2,1)S(1)}, bf16[16,5504]{1,0:T(8,128)(2,1)S(1)}, u32[]{:S(2)}, u32[]{:S(2)}) %collective-permute-start.30) | collective-permute-done | bytes 176160 | tf_op jit(solution)/shard_map/ppermute | solution.py:59
  141.8 2.0 %shard_map.105 = (bf16[16,5504]{1,0:T(8,128)(2,1)S(1)}, bf16[16,5504]{1,0:T(8,128)(2,1)S(1)}, bf16[16,5504]{1,0:T(8,128)(2,1)S(1)}) custom-call(bf16[336,2560]{1,0:T(8,128)(2,1)S(1)} %pad_maximum_fusion.refs_5_.refs_0_, bf16[336,2560]{1,0:T(8,128)(2,1)S(1)} %collective-permute-done.refs_1_, bf16[240,2560]{1,0:T(8,128)(2,1)S(1)} %pad_maximum_fusion.1.refs_6_.refs_2_, ...), custom_call_target="tpu_custom_call" | custom-call | flops 566231040 | bytes 7249920 | tf_op jit(solution)/shard_map/pallas_call | solution.py:71
  143.8 3.4 %collective-permute-done.35.refs_10_ = bf16[16,5504]{1,0:T(8,128)(2,1)S(1)} collective-permute-done((bf16[16,5504]{1,0:T(8,128)(2,1)S(1)}, bf16[16,5504]{1,0:T(8,128)(2,1)S(1)}, u32[]{:S(2)}, u32[]{:S(2)}) %collective-permute-start.35) | collective-permute-done | bytes 176160 | tf_op jit(solution)/shard_map/ppermute | solution.py:59
  147.7 2.0 %shard_map.107 = (bf16[16,5504]{1,0:T(8,128)(2,1)S(1)}, bf16[16,5504]{1,0:T(8,128)(2,1)S(1)}, bf16[16,5504]{1,0:T(8,128)(2,1)S(1)}) custom-call(bf16[336,2560]{1,0:T(8,128)(2,1)S(1)} %pad_maximum_fusion.refs_5_.refs_0_, bf16[336,2560]{1,0:T(8,128)(2,1)S(1)} %collective-permute-done.refs_1_, bf16[240,2560]{1,0:T(8,128)(2,1)S(1)} %pad_maximum_fusion.1.refs_6_.refs_2_, ...), custom_call_target="tpu_custom_call" | custom-call | flops 566231040 | bytes 7249920 | tf_op jit(solution)/shard_map/pallas_call | solution.py:71
  150.0 1.2 collective-permute-start.37
  152.1 3.1 %collective-permute-done.36 = bf16[16,5504]{1,0:T(8,128)(2,1)S(1)} collective-permute-done((bf16[16,5504]{1,0:T(8,128)(2,1)S(1)}, bf16[16,5504]{1,0:T(8,128)(2,1)S(1)}, u32[]{:S(2)}, u32[]{:S(2)}) %collective-permute-start.36) | collective-permute-done | bytes 176160 | tf_op jit(solution)/shard_map/ppermute | solution.py:59
  155.6 1.8 %collective-permute-start.38 = (bf16[16,5504]{1,0:T(8,128)(2,1)S(1)}, bf16[16,5504]{1,0:T(8,128)(2,1)S(1)}, u32[]{:S(2)}, u32[]{:S(2)}) collective-permute-start(bf16[16,5504]{1,0:T(8,128)(2,1)S(1)} %get-tuple-element.191), channel_id=1, source_target_pairs={{0,2},{1,3},{2,0},{3,1},{4,6},{5,7},{6,4},{7,5},{8,10},{9,11},{10,... | collective-permute-start | bytes 528392 | tf_op jit(solution)/shard_map/ppermute | solution.py:59
  157.4 1.2 collective-permute-start.39
  159.7 2.6 %collective-permute-start.40 = (bf16[16,5504]{1,0:T(8,128)(2,1)S(1)}, bf16[16,5504]{1,0:T(8,128)(2,1)S(1)}, u32[]{:S(2)}, u32[]{:S(2)}) collective-permute-start(bf16[16,5504]{1,0:T(8,128)(2,1)S(1)} %add_convert_fusion), channel_id=1, source_target_pairs={{0,4},{1,5},{2,6},{3,7},{4,0},{5,1},{6,2},{7,3},{8,12},{9,13},{10,... | collective-permute-start | bytes 528392 | tf_op jit(solution)/shard_map/ppermute | solution.py:59
  162.3 1.6 collective-permute-done.38.refs_3_
  163.8 1.1 shard_map.108
  165.0 2.6 %collective-permute-done.41.refs_5_ = bf16[16,5504]{1,0:T(8,128)(2,1)S(1)} collective-permute-done((bf16[16,5504]{1,0:T(8,128)(2,1)S(1)}, bf16[16,5504]{1,0:T(8,128)(2,1)S(1)}, u32[]{:S(2)}, u32[]{:S(2)}) %collective-permute-start.41) | collective-permute-done | bytes 176160 | tf_op jit(solution)/shard_map/ppermute | solution.py:59
  167.6 1.3 shard_map.109
  (79 shorter events, 24.2 us)
Async XLA Ops:
  3.1 45.2 %collective-permute-start = (bf16[336,2560]{1,0:T(8,128)(2,1)S(1)}, bf16[336,2560]{1,0:T(8,128)(2,1)S(1)}, u32[]{:S(2)}, u32[]{:S(2)}) collective-permute-start(bf16[336,2560]{1,0:T(8,128)(2,1)S(1)} %pad_maximum_fusion.refs_5_.refs_0_), channel_id=1, source_target_pairs={{0,1},{1,0},{2,3},{3,2},{4,5},{5,4},{6,7},{7,6},{8,9},{9,8},{10,11... | collective-permute-start | bytes 5160968 | tf_op jit(solution)/shard_map/ppermute | solution.py:59
  7.2 2.9 %copy-start = (bf16[1,64,2560]{2,1,0:T(8,128)(2,1)S(1)}, bf16[1,64,2560]{2,1,0:T(8,128)(2,1)}, u32[]{:S(2)}) copy-start(bf16[1,64,2560]{2,1,0:T(8,128)(2,1)} %param.15) | copy-start | bytes 983044
  7.2 2.9 %copy-start.1 = (bf16[1,64,2560]{2,1,0:T(8,128)(2,1)S(1)}, bf16[1,64,2560]{2,1,0:T(8,128)(2,1)}, u32[]{:S(2)}) copy-start(bf16[1,64,2560]{2,1,0:T(8,128)(2,1)} %param.8) | copy-start | bytes 983044
  7.2 2.9 %copy-start.2 = (f32[1,2560]{1,0:T(1,128)S(1)}, f32[1,2560]{1,0:T(1,128)}, u32[]{:S(2)}) copy-start(f32[1,2560]{1,0:T(1,128)} %refs_3_.3) | copy-start | bytes 30724
  7.2 2.9 %copy-start.3 = (s32[1,2,64,1]{2,3,1,0:T(1,128)S(1)}, s32[1,2,64,1]{2,3,1,0:T(1,128)}, u32[]{:S(2)}) copy-start(s32[1,2,64,1]{2,3,1,0:T(1,128)} %param.13) | copy-start | bytes 1540
  7.2 2.8 %copy-start.4 = (f32[1,2,64,1]{2,3,1,0:T(1,128)S(1)}, f32[1,2,64,1]{2,3,1,0:T(1,128)}, u32[]{:S(2)}) copy-start(f32[1,2,64,1]{2,3,1,0:T(1,128)} %param.14) | copy-start | bytes 1540
  8.4 39.9 %collective-permute-start.1 = (bf16[240,2560]{1,0:T(8,128)(2,1)S(1)}, bf16[240,2560]{1,0:T(8,128)(2,1)S(1)}, u32[]{:S(2)}, u32[]{:S(2)}) collective-permute-start(bf16[240,2560]{1,0:T(8,128)(2,1)S(1)} %pad_maximum_fusion.1.refs_6_.refs_2_), channel_id=1, source_target_pairs={{0,2},{1,3},{2,0},{3,1},{4,6},{5,7},{6,4},{7,5},{8,10},{9,11},{10,... | collective-permute-start | bytes 3686408 | tf_op jit(solution)/shard_map/ppermute | solution.py:59
  10.9 37.3 %collective-permute-start.2 = (bf16[32,5504]{1,0:T(8,128)(2,1)S(1)}, bf16[32,5504]{1,0:T(8,128)(2,1)S(1)}, u32[]{:S(2)}, u32[]{:S(2)}) collective-permute-start(bf16[32,5504]{1,0:T(8,128)(2,1)S(1)} %get-tuple-element.100), channel_id=1, source_target_pairs={{0,4},{1,5},{2,6},{3,7},{4,0},{5,1},{6,2},{7,3},{8,12},{9,13},{10,... | collective-permute-start | bytes 1056776 | tf_op jit(solution)/shard_map/ppermute | solution.py:59
  13.6 33.9 %collective-permute-start.4 = (bf16[16,5504]{1,0:T(8,128)(2,1)S(1)}, bf16[16,5504]{1,0:T(8,128)(2,1)S(1)}, u32[]{:S(2)}, u32[]{:S(2)}) collective-permute-start(bf16[16,5504]{1,0:T(8,128)(2,1)S(1)} %get-tuple-element.121.refs_5_), channel_id=1, source_target_pairs={{0,1},{1,0},{2,3},{3,2},{4,5},{5,4},{6,7},{7,6},{8,9},{9,8},{10,11... | collective-permute-start | bytes 528392 | tf_op jit(solution)/shard_map/ppermute | solution.py:59
  14.1 34.2 %collective-permute-start.3 = (bf16[16,5504]{1,0:T(8,128)(2,1)S(1)}, bf16[16,5504]{1,0:T(8,128)(2,1)S(1)}, u32[]{:S(2)}, u32[]{:S(2)}) collective-permute-start(bf16[16,5504]{1,0:T(8,128)(2,1)S(1)} %get-tuple-element.121.refs_5_), channel_id=1, source_target_pairs={{0,2},{1,3},{2,0},{3,1},{4,6},{5,7},{6,4},{7,5},{8,10},{9,11},{10,... | collective-permute-start | bytes 528392 | tf_op jit(solution)/shard_map/ppermute | solution.py:59
  48.3 5.5 %collective-permute-start.6 = (bf16[16,5504]{1,0:T(8,128)(2,1)S(1)}, bf16[16,5504]{1,0:T(8,128)(2,1)S(1)}, u32[]{:S(2)}, u32[]{:S(2)}) collective-permute-start(bf16[16,5504]{1,0:T(8,128)(2,1)S(1)} %get-tuple-element.109.refs_5_), channel_id=1, source_target_pairs={{0,1},{1,0},{2,3},{3,2},{4,5},{5,4},{6,7},{7,6},{8,9},{9,8},{10,11... | collective-permute-start | bytes 528392 | tf_op jit(solution)/shard_map/ppermute | solution.py:59
  49.3 5.5 %collective-permute-start.5 = (bf16[16,5504]{1,0:T(8,128)(2,1)S(1)}, bf16[16,5504]{1,0:T(8,128)(2,1)S(1)}, u32[]{:S(2)}, u32[]{:S(2)}) collective-permute-start(bf16[16,5504]{1,0:T(8,128)(2,1)S(1)} %get-tuple-element.109.refs_5_), channel_id=1, source_target_pairs={{0,2},{1,3},{2,0},{3,1},{4,6},{5,7},{6,4},{7,5},{8,10},{9,11},{10,... | collective-permute-start | bytes 528392 | tf_op jit(solution)/shard_map/ppermute | solution.py:59
  57.2 7.3 %collective-permute-start.8 = (bf16[16,5504]{1,0:T(8,128)(2,1)S(1)}, bf16[16,5504]{1,0:T(8,128)(2,1)S(1)}, u32[]{:S(2)}, u32[]{:S(2)}) collective-permute-start(bf16[16,5504]{1,0:T(8,128)(2,1)S(1)} %get-tuple-element.118.refs_7_), channel_id=1, source_target_pairs={{0,2},{1,3},{2,0},{3,1},{4,6},{5,7},{6,4},{7,5},{8,10},{9,11},{10,... | collective-permute-start | bytes 528392 | tf_op jit(solution)/shard_map/ppermute | solution.py:59
  58.9 7.4 %collective-permute-start.9 = (bf16[16,5504]{1,0:T(8,128)(2,1)S(1)}, bf16[16,5504]{1,0:T(8,128)(2,1)S(1)}, u32[]{:S(2)}, u32[]{:S(2)}) collective-permute-start(bf16[16,5504]{1,0:T(8,128)(2,1)S(1)} %get-tuple-element.119), channel_id=1, source_target_pairs={{0,1},{1,0},{2,3},{3,2},{4,5},{5,4},{6,7},{7,6},{8,9},{9,8},{10,11... | collective-permute-start | bytes 528392 | tf_op jit(solution)/shard_map/ppermute | solution.py:59
  60.0 10.3 %collective-permute-start.12 = (bf16[32,5504]{1,0:T(8,128)(2,1)S(1)}, bf16[32,5504]{1,0:T(8,128)(2,1)S(1)}, u32[]{:S(2)}, u32[]{:S(2)}) collective-permute-start(bf16[32,5504]{1,0:T(8,128)(2,1)S(1)} %pad_maximum_fusion.2.refs_9_.refs_5_), channel_id=1, source_target_pairs={{0,1},{1,0},{2,3},{3,2},{4,5},{5,4},{6,7},{7,6},{8,9},{9,8},{10,11... | collective-permute-start | bytes 1056776 | tf_op jit(solution)/shard_map/ppermute | solution.py:59
  60.9 9.4 %collective-permute-start.11 = (bf16[32,5504]{1,0:T(8,128)(2,1)S(1)}, bf16[32,5504]{1,0:T(8,128)(2,1)S(1)}, u32[]{:S(2)}, u32[]{:S(2)}) collective-permute-start(bf16[32,5504]{1,0:T(8,128)(2,1)S(1)} %pad_maximum_fusion.2.refs_9_.refs_5_), channel_id=1, source_target_pairs={{0,2},{1,3},{2,0},{3,1},{4,6},{5,7},{6,4},{7,5},{8,10},{9,11},{10,... | collective-permute-start | bytes 1056776 | tf_op jit(solution)/shard_map/ppermute | solution.py:59
  61.3 17.7 %collective-permute-start.7 = (bf16[80,2560]{1,0:T(8,128)(2,1)S(1)}, bf16[80,2560]{1,0:T(8,128)(2,1)S(1)}, u32[]{:S(2)}, u32[]{:S(2)}) collective-permute-start(bf16[80,2560]{1,0:T(8,128)(2,1)S(1)} %get-tuple-element.115), channel_id=1, source_target_pairs={{0,8},{1,9},{2,10},{3,11},{4,12},{5,13},{6,14},{7,15},{8,16},{9,17... | collective-permute-start | bytes 1228808 | tf_op jit(solution)/shard_map/ppermute | solution.py:59
  66.3 12.7 %collective-permute-start.10 = (bf16[16,5504]{1,0:T(8,128)(2,1)S(1)}, bf16[16,5504]{1,0:T(8,128)(2,1)S(1)}, u32[]{:S(2)}, u32[]{:S(2)}) collective-permute-start(bf16[16,5504]{1,0:T(8,128)(2,1)S(1)} %add_convert_fusion.3), channel_id=1, source_target_pairs={{0,12},{1,13},{2,14},{3,15},{4,8},{5,9},{6,10},{7,11},{8,20},{9,21... | collective-permute-start | bytes 528392 | tf_op jit(solution)/shard_map/ppermute | solution.py:59
  72.8 8.7 %collective-permute-start.13 = (bf16[16,5504]{1,0:T(8,128)(2,1)S(1)}, bf16[16,5504]{1,0:T(8,128)(2,1)S(1)}, u32[]{:S(2)}, u32[]{:S(2)}) collective-permute-start(bf16[16,5504]{1,0:T(8,128)(2,1)S(1)} %get-tuple-element.127), channel_id=1, source_target_pairs={{0,10},{1,11},{2,8},{3,9},{4,14},{5,15},{6,12},{7,13},{8,18},{9,19... | collective-permute-start | bytes 528392 | tf_op jit(solution)/shard_map/ppermute | solution.py:59
  72.9 8.7 %collective-permute-start.14 = (bf16[16,5504]{1,0:T(8,128)(2,1)S(1)}, bf16[16,5504]{1,0:T(8,128)(2,1)S(1)}, u32[]{:S(2)}, u32[]{:S(2)}) collective-permute-start(bf16[16,5504]{1,0:T(8,128)(2,1)S(1)} %get-tuple-element.128), channel_id=1, source_target_pairs={{0,9},{1,8},{2,11},{3,10},{4,13},{5,12},{6,15},{7,14},{8,17},{9,16... | collective-permute-start | bytes 528392 | tf_op jit(solution)/shard_map/ppermute | solution.py:59
  74.8 8.5 %collective-permute-start.15 = (bf16[16,5504]{1,0:T(8,128)(2,1)S(1)}, bf16[16,5504]{1,0:T(8,128)(2,1)S(1)}, u32[]{:S(2)}, u32[]{:S(2)}) collective-permute-start(bf16[16,5504]{1,0:T(8,128)(2,1)S(1)} %get-tuple-element.129), channel_id=1, source_target_pairs={{0,8},{1,9},{2,10},{3,11},{4,12},{5,13},{6,14},{7,15},{8,16},{9,17... | collective-permute-start | bytes 528392 | tf_op jit(solution)/shard_map/ppermute | solution.py:59
  84.3 10.6 %collective-permute-start.17 = (bf16[16,5504]{1,0:T(8,128)(2,1)S(1)}, bf16[16,5504]{1,0:T(8,128)(2,1)S(1)}, u32[]{:S(2)}, u32[]{:S(2)}) collective-permute-start(bf16[16,5504]{1,0:T(8,128)(2,1)S(1)} %get-tuple-element.137), channel_id=1, source_target_pairs={{0,4},{1,5},{2,6},{3,7},{4,0},{5,1},{6,2},{7,3},{8,12},{9,13},{10,... | collective-permute-start | bytes 528392 | tf_op jit(solution)/shard_map/ppermute | solution.py:59
  86.3 8.6 %collective-permute-start.19 = (bf16[16,5504]{1,0:T(8,128)(2,1)S(1)}, bf16[16,5504]{1,0:T(8,128)(2,1)S(1)}, u32[]{:S(2)}, u32[]{:S(2)}) collective-permute-start(bf16[16,5504]{1,0:T(8,128)(2,1)S(1)} %get-tuple-element.138.refs_9_), channel_id=1, source_target_pairs={{0,1},{1,0},{2,3},{3,2},{4,5},{5,4},{6,7},{7,6},{8,9},{9,8},{10,11... | collective-permute-start | bytes 528392 | tf_op jit(solution)/shard_map/ppermute | solution.py:59
  87.2 9.2 %collective-permute-start.18 = (bf16[16,5504]{1,0:T(8,128)(2,1)S(1)}, bf16[16,5504]{1,0:T(8,128)(2,1)S(1)}, u32[]{:S(2)}, u32[]{:S(2)}) collective-permute-start(bf16[16,5504]{1,0:T(8,128)(2,1)S(1)} %get-tuple-element.138.refs_9_), channel_id=1, source_target_pairs={{0,2},{1,3},{2,0},{3,1},{4,6},{5,7},{6,4},{7,5},{8,10},{9,11},{10,... | collective-permute-start | bytes 528392 | tf_op jit(solution)/shard_map/ppermute | solution.py:59
  96.4 5.8 %collective-permute-start.21 = (bf16[16,5504]{1,0:T(8,128)(2,1)S(1)}, bf16[16,5504]{1,0:T(8,128)(2,1)S(1)}, u32[]{:S(2)}, u32[]{:S(2)}) collective-permute-start(bf16[16,5504]{1,0:T(8,128)(2,1)S(1)} %collective-permute-done.17.refs_9_), channel_id=1, source_target_pairs={{0,1},{1,0},{2,3},{3,2},{4,5},{5,4},{6,7},{7,6},{8,9},{9,8},{10,11... | collective-permute-start | bytes 528392 | tf_op jit(solution)/shard_map/ppermute | solution.py:59
  97.8 5.5 %collective-permute-start.20 = (bf16[16,5504]{1,0:T(8,128)(2,1)S(1)}, bf16[16,5504]{1,0:T(8,128)(2,1)S(1)}, u32[]{:S(2)}, u32[]{:S(2)}) collective-permute-start(bf16[16,5504]{1,0:T(8,128)(2,1)S(1)} %collective-permute-done.17.refs_9_), channel_id=1, source_target_pairs={{0,2},{1,3},{2,0},{3,1},{4,6},{5,7},{6,4},{7,5},{8,10},{9,11},{10,... | collective-permute-start | bytes 528392 | tf_op jit(solution)/shard_map/ppermute | solution.py:59
  105.9 5.5 %collective-permute-start.22 = (bf16[16,5504]{1,0:T(8,128)(2,1)S(1)}, bf16[16,5504]{1,0:T(8,128)(2,1)S(1)}, u32[]{:S(2)}, u32[]{:S(2)}) collective-permute-start(bf16[16,5504]{1,0:T(8,128)(2,1)S(1)} %get-tuple-element.148), channel_id=1, source_target_pairs={{0,2},{1,3},{2,0},{3,1},{4,6},{5,7},{6,4},{7,5},{8,10},{9,11},{10,... | collective-permute-start | bytes 528392 | tf_op jit(solution)/shard_map/ppermute | solution.py:59
  107.0 5.5 %collective-permute-start.23 = (bf16[16,5504]{1,0:T(8,128)(2,1)S(1)}, bf16[16,5504]{1,0:T(8,128)(2,1)S(1)}, u32[]{:S(2)}, u32[]{:S(2)}) collective-permute-start(bf16[16,5504]{1,0:T(8,128)(2,1)S(1)} %get-tuple-element.149), channel_id=1, source_target_pairs={{0,1},{1,0},{2,3},{3,2},{4,5},{5,4},{6,7},{7,6},{8,9},{9,8},{10,11... | collective-permute-start | bytes 528392 | tf_op jit(solution)/shard_map/ppermute | solution.py:59
  107.6 16.5 %collective-permute-start.16 = (bf16[144,2560]{1,0:T(8,128)(2,1)S(1)}, bf16[144,2560]{1,0:T(8,128)(2,1)S(1)}, u32[]{:S(2)}, u32[]{:S(2)}) collective-permute-start(bf16[144,2560]{1,0:T(8,128)(2,1)S(1)} %get-tuple-element.131), channel_id=1, source_target_pairs={{0,24},{1,25},{2,26},{3,27},{4,28},{5,29},{6,30},{7,31},{8,0},{9,1... | collective-permute-start | bytes 2211848 | tf_op jit(solution)/shard_map/ppermute | solution.py:59
  108.4 8.4 %collective-permute-start.25 = (bf16[16,5504]{1,0:T(8,128)(2,1)S(1)}, bf16[16,5504]{1,0:T(8,128)(2,1)S(1)}, u32[]{:S(2)}, u32[]{:S(2)}) collective-permute-start(bf16[16,5504]{1,0:T(8,128)(2,1)S(1)} %get-tuple-element.155), channel_id=1, source_target_pairs={{0,2},{1,3},{2,0},{3,1},{4,6},{5,7},{6,4},{7,5},{8,10},{9,11},{10,... | collective-permute-start | bytes 528392 | tf_op jit(solution)/shard_map/ppermute | solution.py:59
  109.5 7.3 %collective-permute-start.26 = (bf16[16,5504]{1,0:T(8,128)(2,1)S(1)}, bf16[16,5504]{1,0:T(8,128)(2,1)S(1)}, u32[]{:S(2)}, u32[]{:S(2)}) collective-permute-start(bf16[16,5504]{1,0:T(8,128)(2,1)S(1)} %get-tuple-element.156), channel_id=1, source_target_pairs={{0,1},{1,0},{2,3},{3,2},{4,5},{5,4},{6,7},{7,6},{8,9},{9,8},{10,11... | collective-permute-start | bytes 528392 | tf_op jit(solution)/shard_map/ppermute | solution.py:59
  112.5 9.6 %collective-permute-start.24 = (bf16[16,5504]{1,0:T(8,128)(2,1)S(1)}, bf16[16,5504]{1,0:T(8,128)(2,1)S(1)}, u32[]{:S(2)}, u32[]{:S(2)}) collective-permute-start(bf16[16,5504]{1,0:T(8,128)(2,1)S(1)} %add_convert_fusion.2), channel_id=1, source_target_pairs={{0,28},{1,29},{2,30},{3,31},{4,24},{5,25},{6,26},{7,27},{8,4},{9,5... | collective-permute-start | bytes 528392 | tf_op jit(solution)/shard_map/ppermute | solution.py:59
  112.6 9.9 %collective-permute-start.27 = (bf16[16,5504]{1,0:T(8,128)(2,1)S(1)}, bf16[16,5504]{1,0:T(8,128)(2,1)S(1)}, u32[]{:S(2)}, u32[]{:S(2)}) collective-permute-start(bf16[16,5504]{1,0:T(8,128)(2,1)S(1)} %get-tuple-element.160.refs_11_), channel_id=1, source_target_pairs={{0,26},{1,27},{2,24},{3,25},{4,30},{5,31},{6,28},{7,29},{8,2},{9,3... | collective-permute-start | bytes 528392 | tf_op jit(solution)/shard_map/ppermute | solution.py:59
  116.8 6.5 %collective-permute-start.28 = (bf16[16,5504]{1,0:T(8,128)(2,1)S(1)}, bf16[16,5504]{1,0:T(8,128)(2,1)S(1)}, u32[]{:S(2)}, u32[]{:S(2)}) collective-permute-start(bf16[16,5504]{1,0:T(8,128)(2,1)S(1)} %get-tuple-element.161), channel_id=1, source_target_pairs={{0,25},{1,24},{2,27},{3,26},{4,29},{5,28},{6,31},{7,30},{8,1},{9,0... | collective-permute-start | bytes 528392 | tf_op jit(solution)/shard_map/ppermute | solution.py:59
  116.8 7.3 %collective-permute-start.29 = (bf16[16,5504]{1,0:T(8,128)(2,1)S(1)}, bf16[16,5504]{1,0:T(8,128)(2,1)S(1)}, u32[]{:S(2)}, u32[]{:S(2)}) collective-permute-start(bf16[16,5504]{1,0:T(8,128)(2,1)S(1)} %get-tuple-element.162), channel_id=1, source_target_pairs={{0,24},{1,25},{2,26},{3,27},{4,28},{5,29},{6,30},{7,31},{8,0},{9,1... | collective-permute-start | bytes 528392 | tf_op jit(solution)/shard_map/ppermute | solution.py:59
  122.1 14.6 %collective-permute-start.33 = (bf16[16,5504]{1,0:T(8,128)(2,1)S(1)}, bf16[16,5504]{1,0:T(8,128)(2,1)S(1)}, u32[]{:S(2)}, u32[]{:S(2)}) collective-permute-start(bf16[16,5504]{1,0:T(8,128)(2,1)S(1)} %add_convert_fusion.1), channel_id=1, source_target_pairs={{0,4},{1,5},{2,6},{3,7},{4,0},{5,1},{6,2},{7,3},{8,12},{9,13},{10,... | collective-permute-start | bytes 528392 | tf_op jit(solution)/shard_map/ppermute | solution.py:59
  125.1 15.5 %collective-permute-start.30 = (bf16[16,5504]{1,0:T(8,128)(2,1)S(1)}, bf16[16,5504]{1,0:T(8,128)(2,1)S(1)}, u32[]{:S(2)}, u32[]{:S(2)}) collective-permute-start(bf16[16,5504]{1,0:T(8,128)(2,1)S(1)} %get-tuple-element.163), channel_id=1, source_target_pairs={{0,4},{1,5},{2,6},{3,7},{4,0},{5,1},{6,2},{7,3},{8,12},{9,13},{10,... | collective-permute-start | bytes 528392 | tf_op jit(solution)/shard_map/ppermute | solution.py:59
  126.1 14.5 %collective-permute-start.32 = (bf16[16,5504]{1,0:T(8,128)(2,1)S(1)}, bf16[16,5504]{1,0:T(8,128)(2,1)S(1)}, u32[]{:S(2)}, u32[]{:S(2)}) collective-permute-start(bf16[16,5504]{1,0:T(8,128)(2,1)S(1)} %get-tuple-element.164.refs_9_), channel_id=1, source_target_pairs={{0,1},{1,0},{2,3},{3,2},{4,5},{5,4},{6,7},{7,6},{8,9},{9,8},{10,11... | collective-permute-start | bytes 528392 | tf_op jit(solution)/shard_map/ppermute | solution.py:59
  127.0 14.0 %collective-permute-start.31 = (bf16[16,5504]{1,0:T(8,128)(2,1)S(1)}, bf16[16,5504]{1,0:T(8,128)(2,1)S(1)}, u32[]{:S(2)}, u32[]{:S(2)}) collective-permute-start(bf16[16,5504]{1,0:T(8,128)(2,1)S(1)} %get-tuple-element.164.refs_9_), channel_id=1, source_target_pairs={{0,2},{1,3},{2,0},{3,1},{4,6},{5,7},{6,4},{7,5},{8,10},{9,11},{10,... | collective-permute-start | bytes 528392 | tf_op jit(solution)/shard_map/ppermute | solution.py:59
  141.0 6.2 %collective-permute-start.35 = (bf16[16,5504]{1,0:T(8,128)(2,1)S(1)}, bf16[16,5504]{1,0:T(8,128)(2,1)S(1)}, u32[]{:S(2)}, u32[]{:S(2)}) collective-permute-start(bf16[16,5504]{1,0:T(8,128)(2,1)S(1)} %collective-permute-done.30.refs_9_), channel_id=1, source_target_pairs={{0,1},{1,0},{2,3},{3,2},{4,5},{5,4},{6,7},{7,6},{8,9},{9,8},{10,11... | collective-permute-start | bytes 528392 | tf_op jit(solution)/shard_map/ppermute | solution.py:59
  141.8 5.9 %collective-permute-start.34 = (bf16[16,5504]{1,0:T(8,128)(2,1)S(1)}, bf16[16,5504]{1,0:T(8,128)(2,1)S(1)}, u32[]{:S(2)}, u32[]{:S(2)}) collective-permute-start(bf16[16,5504]{1,0:T(8,128)(2,1)S(1)} %collective-permute-done.30.refs_9_), channel_id=1, source_target_pairs={{0,2},{1,3},{2,0},{3,1},{4,6},{5,7},{6,4},{7,5},{8,10},{9,11},{10,... | collective-permute-start | bytes 528392 | tf_op jit(solution)/shard_map/ppermute | solution.py:59
  149.7 5.5 %collective-permute-start.36 = (bf16[16,5504]{1,0:T(8,128)(2,1)S(1)}, bf16[16,5504]{1,0:T(8,128)(2,1)S(1)}, u32[]{:S(2)}, u32[]{:S(2)}) collective-permute-start(bf16[16,5504]{1,0:T(8,128)(2,1)S(1)} %get-tuple-element.189), channel_id=1, source_target_pairs={{0,2},{1,3},{2,0},{3,1},{4,6},{5,7},{6,4},{7,5},{8,10},{9,11},{10,... | collective-permute-start | bytes 528392 | tf_op jit(solution)/shard_map/ppermute | solution.py:59
  150.0 5.5 %collective-permute-start.37 = (bf16[16,5504]{1,0:T(8,128)(2,1)S(1)}, bf16[16,5504]{1,0:T(8,128)(2,1)S(1)}, u32[]{:S(2)}, u32[]{:S(2)}) collective-permute-start(bf16[16,5504]{1,0:T(8,128)(2,1)S(1)} %get-tuple-element.190), channel_id=1, source_target_pairs={{0,1},{1,0},{2,3},{3,2},{4,5},{5,4},{6,7},{7,6},{8,9},{9,8},{10,11... | collective-permute-start | bytes 528392 | tf_op jit(solution)/shard_map/ppermute | solution.py:59
  155.6 8.3 %collective-permute-start.38 = (bf16[16,5504]{1,0:T(8,128)(2,1)S(1)}, bf16[16,5504]{1,0:T(8,128)(2,1)S(1)}, u32[]{:S(2)}, u32[]{:S(2)}) collective-permute-start(bf16[16,5504]{1,0:T(8,128)(2,1)S(1)} %get-tuple-element.191), channel_id=1, source_target_pairs={{0,2},{1,3},{2,0},{3,1},{4,6},{5,7},{6,4},{7,5},{8,10},{9,11},{10,... | collective-permute-start | bytes 528392 | tf_op jit(solution)/shard_map/ppermute | solution.py:59
  157.4 6.5 %collective-permute-start.39 = (bf16[16,5504]{1,0:T(8,128)(2,1)S(1)}, bf16[16,5504]{1,0:T(8,128)(2,1)S(1)}, u32[]{:S(2)}, u32[]{:S(2)}) collective-permute-start(bf16[16,5504]{1,0:T(8,128)(2,1)S(1)} %get-tuple-element.192), channel_id=1, source_target_pairs={{0,1},{1,0},{2,3},{3,2},{4,5},{5,4},{6,7},{7,6},{8,9},{9,8},{10,11... | collective-permute-start | bytes 528392 | tf_op jit(solution)/shard_map/ppermute | solution.py:59
  158.6 9.0 %collective-permute-start.41 = (bf16[16,5504]{1,0:T(8,128)(2,1)S(1)}, bf16[16,5504]{1,0:T(8,128)(2,1)S(1)}, u32[]{:S(2)}, u32[]{:S(2)}) collective-permute-start(bf16[16,5504]{1,0:T(8,128)(2,1)S(1)} %get-tuple-element.195.refs_11_), channel_id=1, source_target_pairs={{0,2},{1,3},{2,0},{3,1},{4,6},{5,7},{6,4},{7,5},{8,10},{9,11},{10,... | collective-permute-start | bytes 528392 | tf_op jit(solution)/shard_map/ppermute | solution.py:59
  158.9 8.7 %collective-permute-start.42 = (bf16[16,5504]{1,0:T(8,128)(2,1)S(1)}, bf16[16,5504]{1,0:T(8,128)(2,1)S(1)}, u32[]{:S(2)}, u32[]{:S(2)}) collective-permute-start(bf16[16,5504]{1,0:T(8,128)(2,1)S(1)} %get-tuple-element.196), channel_id=1, source_target_pairs={{0,1},{1,0},{2,3},{3,2},{4,5},{5,4},{6,7},{7,6},{8,9},{9,8},{10,11... | collective-permute-start | bytes 528392 | tf_op jit(solution)/shard_map/ppermute | solution.py:59
  159.7 7.9 %collective-permute-start.40 = (bf16[16,5504]{1,0:T(8,128)(2,1)S(1)}, bf16[16,5504]{1,0:T(8,128)(2,1)S(1)}, u32[]{:S(2)}, u32[]{:S(2)}) collective-permute-start(bf16[16,5504]{1,0:T(8,128)(2,1)S(1)} %add_convert_fusion), channel_id=1, source_target_pairs={{0,4},{1,5},{2,6},{3,7},{4,0},{5,1},{6,2},{7,3},{8,12},{9,13},{10,... | collective-permute-start | bytes 528392 | tf_op jit(solution)/shard_map/ppermute | solution.py:59
  (1 other events, 2.3 us)

commit v3 on v2

--- a/solution.py
+++ b/solution.py
@@ -492,11 +492,11 @@
             shift(parts[1], sections=sections),
         ]
 
-    def give_back(cross, own, sections):
+    def give_back(cross, own, sections, others=()):
         total = sums(cross)
         back = home(total, sections)
-        own, _ = fence((own, total))
-        return back + own_home(own, sections)
+        own, _, others = fence((own, total, others))
+        return back + own_home(own, sections), others
 
     units = w_gate.shape[3]
     cut = -(-units * 7 // 12 // ROWS) * ROWS
@@ -528,11 +528,11 @@
 
     cross_out, cross_kept0 = expert_call(forward_kernel, box, packs, cross0, kept=2)
     own_out, own_kept0 = expert_call(
-        forward_kernel, box, packs, own0, kept=2, after=list(cross_out[:1]) + list(cots)
+        forward_kernel, box, packs, own0, kept=2, after=cross_out[:1]
     )
     cross_out, ahead = fence((cross_out, ahead))
     arrived0 = shift(ahead, sections=1)
-    got = give_back(cross_out, own_out, 1)
+    got, cots = give_back(cross_out, own_out, 1, cots)
     h1, behind, own1, *boxes1 = call(
         bind(middle_kernel, box, experts),
         [rows_of(n), rows_of(2 * n + ROWS)] + [boxed] * experts,
@@ -557,9 +557,8 @@
     down = bind(expert_call, down_kernel, box, packs, reads=False)
     cross_fin = down(cross1, cross_kept1)[0]
     arrived1 = shift(behind, sections=-1)
-    got = give_back(cross_grad, own_grad, -1)
-    got[: experts - 1], fin_sums = fence((got[: experts - 1], sums(cross_fin)))
-    fin_back = home(fin_sums, 0)
+    got, _ = give_back(cross_grad, own_grad, -1)
+    fin_back = home(sums(cross_fin), 0)
     own_fin = down(own1, own_kept1)[0]
     g1, own_g, *boxes_g = call(
         bind(turn_kernel, box, experts),
@@ -568,10 +567,11 @@
         notes0,
         *got,
         scratch=[picked],
-    )
-
-    cross_g, own_z, own_x, fin_back = fence(
-        (crossing_of(boxes_g), shift(own_g, flip=2), shift(own_g, flip=1), fin_back)
+        after=fin_back,
+    )
+
+    cross_g, own_z, own_x = fence(
+        (crossing_of(boxes_g), shift(own_g, flip=2), shift(own_g, flip=1))
     )
     cross_g, own_g = around(cross_g), [own_z, own_g, own_x]
     back = bind(expert_call, back_kernel, box, packs)
@@ -599,6 +599,7 @@
         *fin_back,
         *fin_own,
         scratch=[picked],
+        after=[g0],
     )
     return (final[None], g0[None])
 

time: 169 us -> 170 us (level)
  waiting for transfers between devices: 101 us -> 93.9 us
  starting transfers between devices: 39.5 us -> 46.2 us
    ppermute x43, starting transfers between devices: 39.5 us -> 46.2 us  [shift(): return lax.ppermute(value, ('section', 'expert'), pairs)]
    ppermute x43, waiting for transfers between devices: 101 us -> 93.9 us  [shift(): return lax.ppermute(value, ('section', 'expert'), pairs)]
  transfers between devices with their start and end apart: 43 -> 43, of which waited for: 29 -> 26; matrix products, arithmetic and copies ran while one was open for 1% -> 1% of each run, Pallas kernels for 8% -> 7%
where the time goes in v3:
time: 170 us
  waiting for transfers between devices  93.9 us (55%)
  starting transfers between devices  46.2 us (27%)
  Pallas kernels  23 us (14%)
  local copies, waits for them, and re-layouts  5.5 us (3%)
    ppermute x43, waiting for transfers between devices, shift(): return lax.ppermute(value, ('section', 'expert'), pairs)  93.9 us
    ppermute x43, starting transfers between devices, shift(): return lax.ppermute(value, ('section', 'expert'), pairs)  46.2 us
    pallas_call x15, Pallas kernels, call(): pl.pallas_call(reading, out_shape=list(outs), in_specs=[vmem] * read + [p...  23 us
  transfers between devices with their start and end apart: 43, of which 26 were waited for; matrix products, arithmetic and copies ran while one was open for 1% of the time, Pallas kernels for 7%

profile of v3, /device:TPU:0, one launch (start us, length us, event | category | flops | bytes accessed | tf_op | source)
XLA Modules:
  0.0 170.0 jit_solution(5376042989498155942)
XLA Ops:
  0.6 1.2 slice.40
  1.8 1.1 slice.41
  3.1 3.0 %collective-permute-start = (bf16[336,2560]{1,0:T(8,128)(2,1)S(1)}, bf16[336,2560]{1,0:T(8,128)(2,1)S(1)}, u32[]{:S(2)}, u32[]{:S(2)}) collective-permute-start(bf16[336,2560]{1,0:T(8,128)(2,1)S(1)} %pad_maximum_fusion.refs_5_.refs_0_), channel_id=1, source_target_pairs={{0,1},{1,0},{2,3},{3,2},{4,5},{5,4},{6,7},{7,6},{8,9},{9,8},{10,11... | collective-permute-start | bytes 5160968 | tf_op jit(solution)/shard_map/ppermute | solution.py:59
  6.1 1.0 slice.42
  7.2 1.1 slice.43
  8.4 1.6 collective-permute-start.1
  10.9 2.6 %collective-permute-start.2 = (bf16[32,5504]{1,0:T(8,128)(2,1)S(1)}, bf16[32,5504]{1,0:T(8,128)(2,1)S(1)}, u32[]{:S(2)}, u32[]{:S(2)}) collective-permute-start(bf16[32,5504]{1,0:T(8,128)(2,1)S(1)} %get-tuple-element.100), channel_id=1, source_target_pairs={{0,4},{1,5},{2,6},{3,7},{4,0},{5,1},{6,2},{7,3},{8,12},{9,13},{10,... | collective-permute-start | bytes 1056776 | tf_op jit(solution)/shard_map/ppermute | solution.py:59
  14.5 32.9 %collective-permute-done.4.refs_6_ = bf16[16,5504]{1,0:T(8,128)(2,1)S(1)} collective-permute-done((bf16[16,5504]{1,0:T(8,128)(2,1)S(1)}, bf16[16,5504]{1,0:T(8,128)(2,1)S(1)}, u32[]{:S(2)}, u32[]{:S(2)}) %collective-permute-start.4) | collective-permute-done | bytes 176160 | tf_op jit(solution)/shard_map/ppermute | solution.py:59
  49.3 1.6 collective-permute-start.5
  50.9 2.9 %collective-permute-done.6.refs_6_ = bf16[16,5504]{1,0:T(8,128)(2,1)S(1)} collective-permute-done((bf16[16,5504]{1,0:T(8,128)(2,1)S(1)}, bf16[16,5504]{1,0:T(8,128)(2,1)S(1)}, u32[]{:S(2)}, u32[]{:S(2)}) %collective-permute-start.6) | collective-permute-done | bytes 176160 | tf_op jit(solution)/shard_map/ppermute | solution.py:59
  54.8 2.5 %shard_map.96 = (bf16[16,5504]{1,0:T(8,128)(2,1)S(1)}, bf16[16,5504]{1,0:T(8,128)(2,1)S(1)}, bf16[16,5504]{1,0:T(8,128)(2,1)S(1)}, f32[96,224]{1,0:T(8,128)S(1)}...) custom-call(bf16[336,2560]{1,0:T(8,128)(2,1)S(1)} %pad_maximum_fusion.refs_5_.refs_0_, ...), custom_call_target="tpu_custom_call" | custom-call | flops 566231040 | bytes 7249920 | tf_op jit(solution)/shard_map/pallas_call | solution.py:71
  57.2 1.6 collective-permute-start.8
  58.9 1.1 collective-permute-start.9
  61.3 2.5 %shard_map.97 = (bf16[16,5504]{1,0:T(8,128)(2,1)S(1)}, bf16[16,5504]{1,0:T(8,128)(2,1)S(1)}, bf16[16,5504]{1,0:T(8,128)(2,1)S(1)}, f32[96,224]{1,0:T(8,128)S(1)}...) custom-call(bf16[336,2560]{1,0:T(8,128)(2,1)S(1)} %pad_maximum_fusion.refs_5_.refs_0_, ...), custom_call_target="tpu_custom_call" | custom-call | flops 566231040 | bytes 7249920 | tf_op jit(solution)/shard_map/pallas_call | solution.py:71
  64.5 1.7 %collective-permute-done.9 = bf16[16,5504]{1,0:T(8,128)(2,1)S(1)} collective-permute-done((bf16[16,5504]{1,0:T(8,128)(2,1)S(1)}, bf16[16,5504]{1,0:T(8,128)(2,1)S(1)}, u32[]{:S(2)}, u32[]{:S(2)}) %collective-permute-start.9) | collective-permute-done | bytes 176160 | tf_op jit(solution)/shard_map/ppermute | solution.py:59
  66.3 1.5 collective-permute-start.10
  67.8 2.5 %collective-permute-done.12.refs_6_ = bf16[32,5504]{1,0:T(8,128)(2,1)S(1)} collective-permute-done((bf16[32,5504]{1,0:T(8,128)(2,1)S(1)}, bf16[32,5504]{1,0:T(8,128)(2,1)S(1)}, u32[]{:S(2)}, u32[]{:S(2)}) %collective-permute-start.12) | collective-permute-done | bytes 352288 | tf_op jit(solution)/shard_map/ppermute | solution.py:59
  70.3 1.9 %collective-permute-start.14 = (bf16[16,5504]{1,0:T(8,128)(2,1)S(1)}, bf16[16,5504]{1,0:T(8,128)(2,1)S(1)}, u32[]{:S(2)}, u32[]{:S(2)}) collective-permute-start(bf16[16,5504]{1,0:T(8,128)(2,1)S(1)} %get-tuple-element.128), channel_id=1, source_target_pairs={{0,9},{1,8},{2,11},{3,10},{4,13},{5,12},{6,15},{7,14},{8,17},{9,16... | collective-permute-start | bytes 528392 | tf_op jit(solution)/shard_map/ppermute | solution.py:59
  72.3 6.4 %collective-permute-done.10.refs_4_ = bf16[16,5504]{1,0:T(8,128)(2,1)S(1)} collective-permute-done((bf16[16,5504]{1,0:T(8,128)(2,1)S(1)}, bf16[16,5504]{1,0:T(8,128)(2,1)S(1)}, u32[]{:S(2)}, u32[]{:S(2)}) %collective-permute-start.10) | collective-permute-done | bytes 176160 | tf_op jit(solution)/shard_map/ppermute | solution.py:59
  78.6 1.2 collective-permute-done.13.refs_5_
  79.8 1.1 collective-permute-done.15.refs_7_
  81.9 1.9 %collective-permute-start.16 = (bf16[16,5504]{1,0:T(8,128)(2,1)S(1)}, bf16[16,5504]{1,0:T(8,128)(2,1)S(1)}, u32[]{:S(2)}, u32[]{:S(2)}) collective-permute-start(bf16[16,5504]{1,0:T(8,128)(2,1)S(1)} %get-tuple-element.138), channel_id=1, source_target_pairs={{0,4},{1,5},{2,6},{3,7},{4,0},{5,1},{6,2},{7,3},{8,12},{9,13},{10,... | collective-permute-start | bytes 528392 | tf_op jit(solution)/shard_map/ppermute | solution.py:59
  84.3 2.5 %collective-permute-start.17 = (bf16[16,5504]{1,0:T(8,128)(2,1)S(1)}, bf16[16,5504]{1,0:T(8,128)(2,1)S(1)}, u32[]{:S(2)}, u32[]{:S(2)}) collective-permute-start(bf16[16,5504]{1,0:T(8,128)(2,1)S(1)} %get-tuple-element.139.refs_9_), channel_id=1, source_target_pairs={{0,2},{1,3},{2,0},{3,1},{4,6},{5,7},{6,4},{7,5},{8,10},{9,11},{10,... | collective-permute-start | bytes 528392 | tf_op jit(solution)/shard_map/ppermute | solution.py:59
  86.8 5.8 %collective-permute-done.16.refs_9_ = bf16[16,5504]{1,0:T(8,128)(2,1)S(1)} collective-permute-done((bf16[16,5504]{1,0:T(8,128)(2,1)S(1)}, bf16[16,5504]{1,0:T(8,128)(2,1)S(1)}, u32[]{:S(2)}, u32[]{:S(2)}) %collective-permute-start.16) | collective-permute-done | bytes 176160 | tf_op jit(solution)/shard_map/ppermute | solution.py:59
  96.4 2.6 %shard_map.101 = (bf16[16,5504]{1,0:T(8,128)(2,1)S(1)}, bf16[16,5504]{1,0:T(8,128)(2,1)S(1)}, bf16[16,5504]{1,0:T(8,128)(2,1)S(1)}, f32[96,224]{1,0:T(8,128)S(1)...) custom-call(bf16[336,2560]{1,0:T(8,128)(2,1)S(1)} %pad_maximum_fusion.refs_5_.refs_0_, ...), custom_call_target="tpu_custom_call" | custom-call | flops 566231040 | bytes 7397376 | tf_op jit(solution)/shard_map/pallas_call | solution.py:71
  99.9 2.6 %shard_map.102 = (bf16[16,5504]{1,0:T(8,128)(2,1)S(1)}, bf16[16,5504]{1,0:T(8,128)(2,1)S(1)}, bf16[16,5504]{1,0:T(8,128)(2,1)S(1)}, f32[96,224]{1,0:T(8,128)S(1)...) custom-call(bf16[336,2560]{1,0:T(8,128)(2,1)S(1)} %pad_maximum_fusion.refs_5_.refs_0_, ...), custom_call_target="tpu_custom_call" | custom-call | flops 566231040 | bytes 7397376 | tf_op jit(solution)/shard_map/pallas_call | solution.py:71
  103.4 1.1 collective-permute-start.21
  107.5 1.7 collective-permute-done.21
  109.1 1.3 collective-permute-done.22
  110.5 2.6 %collective-permute-start.23 = (bf16[16,5504]{1,0:T(8,128)(2,1)S(1)}, bf16[16,5504]{1,0:T(8,128)(2,1)S(1)}, u32[]{:S(2)}, u32[]{:S(2)}) collective-permute-start(bf16[16,5504]{1,0:T(8,128)(2,1)S(1)} %add_convert_fusion.2), channel_id=1, source_target_pairs={{0,4},{1,5},{2,6},{3,7},{4,0},{5,1},{6,2},{7,3},{8,12},{9,13},{10,... | collective-permute-start | bytes 528392 | tf_op jit(solution)/shard_map/ppermute | solution.py:59
  113.2 1.4 collective-permute-done.25
  116.2 3.7 %collective-permute-done.23.refs_6_.refs_2_ = bf16[16,5504]{1,0:T(8,128)(2,1)S(1)} collective-permute-done((bf16[16,5504]{1,0:T(8,128)(2,1)S(1)}, bf16[16,5504]{1,0:T(8,128)(2,1)S(1)}, u32[]{:S(2)}, u32[]{:S(2)}) %collective-permute-start.23) | collective-permute-done | bytes 176160 | tf_op jit(solution)/shard_map/ppermute | solution.py:59
  119.9 3.4 %collective-permute-done.28.refs_3_ = bf16[16,5504]{1,0:T(8,128)(2,1)S(1)} collective-permute-done((bf16[16,5504]{1,0:T(8,128)(2,1)S(1)}, bf16[16,5504]{1,0:T(8,128)(2,1)S(1)}, u32[]{:S(2)}, u32[]{:S(2)}) %collective-permute-start.28) | collective-permute-done | bytes 176160 | tf_op jit(solution)/shard_map/ppermute | solution.py:59
  123.3 6.2 %collective-permute-done.27.refs_2_ = bf16[16,5504]{1,0:T(8,128)(2,1)S(1)} collective-permute-done((bf16[16,5504]{1,0:T(8,128)(2,1)S(1)}, bf16[16,5504]{1,0:T(8,128)(2,1)S(1)}, u32[]{:S(2)}, u32[]{:S(2)}) %collective-permute-start.27) | collective-permute-done | bytes 176160 | tf_op jit(solution)/shard_map/ppermute | solution.py:59
  130.7 3.2 %collective-permute-start.32 = (bf16[16,5504]{1,0:T(8,128)(2,1)S(1)}, bf16[16,5504]{1,0:T(8,128)(2,1)S(1)}, u32[]{:S(2)}, u32[]{:S(2)}) collective-permute-start(bf16[16,5504]{1,0:T(8,128)(2,1)S(1)} %get-tuple-element.170.refs_9_), channel_id=1, source_target_pairs={{0,2},{1,3},{2,0},{3,1},{4,6},{5,7},{6,4},{7,5},{8,10},{9,11},{10,... | collective-permute-start | bytes 528392 | tf_op jit(solution)/shard_map/ppermute | solution.py:59
  133.9 6.1 %collective-permute-done.31.refs_9_ = bf16[16,5504]{1,0:T(8,128)(2,1)S(1)} collective-permute-done((bf16[16,5504]{1,0:T(8,128)(2,1)S(1)}, bf16[16,5504]{1,0:T(8,128)(2,1)S(1)}, u32[]{:S(2)}, u32[]{:S(2)}) %collective-permute-start.31) | collective-permute-done | bytes 176160 | tf_op jit(solution)/shard_map/ppermute | solution.py:59
  141.1 2.0 %shard_map.105 = (bf16[16,5504]{1,0:T(8,128)(2,1)S(1)}, bf16[16,5504]{1,0:T(8,128)(2,1)S(1)}, bf16[16,5504]{1,0:T(8,128)(2,1)S(1)}) custom-call(bf16[336,2560]{1,0:T(8,128)(2,1)S(1)} %pad_maximum_fusion.refs_5_.refs_0_, bf16[336,2560]{1,0:T(8,128)(2,1)S(1)} %collective-permute-done.refs_1_, bf16[240,2560]{1,0:T(8,128)(2,1)S(1)} %pad_maximum_fusion.1.refs_6_.refs_2_, ...), custom_call_target="tpu_custom_call" | custom-call | flops 566231040 | bytes 7249920 | tf_op jit(solution)/shard_map/pallas_call | solution.py:71
  143.1 3.2 %collective-permute-done.35.refs_10_ = bf16[16,5504]{1,0:T(8,128)(2,1)S(1)} collective-permute-done((bf16[16,5504]{1,0:T(8,128)(2,1)S(1)}, bf16[16,5504]{1,0:T(8,128)(2,1)S(1)}, u32[]{:S(2)}, u32[]{:S(2)}) %collective-permute-start.35) | collective-permute-done | bytes 176160 | tf_op jit(solution)/shard_map/ppermute | solution.py:59
  146.5 2.0 %shard_map.107 = (bf16[16,5504]{1,0:T(8,128)(2,1)S(1)}, bf16[16,5504]{1,0:T(8,128)(2,1)S(1)}, bf16[16,5504]{1,0:T(8,128)(2,1)S(1)}) custom-call(bf16[336,2560]{1,0:T(8,128)(2,1)S(1)} %pad_maximum_fusion.refs_5_.refs_0_, bf16[336,2560]{1,0:T(8,128)(2,1)S(1)} %collective-permute-done.refs_1_, bf16[240,2560]{1,0:T(8,128)(2,1)S(1)} %pad_maximum_fusion.1.refs_6_.refs_2_, ...), custom_call_target="tpu_custom_call" | custom-call | flops 566231040 | bytes 7249920 | tf_op jit(solution)/shard_map/pallas_call | solution.py:71
  148.6 1.8 %collective-permute-start.37 = (bf16[16,5504]{1,0:T(8,128)(2,1)S(1)}, bf16[16,5504]{1,0:T(8,128)(2,1)S(1)}, u32[]{:S(2)}, u32[]{:S(2)}) collective-permute-start(bf16[16,5504]{1,0:T(8,128)(2,1)S(1)} %get-tuple-element.190), channel_id=1, source_target_pairs={{0,1},{1,0},{2,3},{3,2},{4,5},{5,4},{6,7},{7,6},{8,9},{9,8},{10,11... | collective-permute-start | bytes 528392 | tf_op jit(solution)/shard_map/ppermute | solution.py:59
  151.3 2.8 %collective-permute-done.36 = bf16[16,5504]{1,0:T(8,128)(2,1)S(1)} collective-permute-done((bf16[16,5504]{1,0:T(8,128)(2,1)S(1)}, bf16[16,5504]{1,0:T(8,128)(2,1)S(1)}, u32[]{:S(2)}, u32[]{:S(2)}) %collective-permute-start.36) | collective-permute-done | bytes 176160 | tf_op jit(solution)/shard_map/ppermute | solution.py:59
  154.2 2.3 %collective-permute-start.41 = (bf16[16,5504]{1,0:T(8,128)(2,1)S(1)}, bf16[16,5504]{1,0:T(8,128)(2,1)S(1)}, u32[]{:S(2)}, u32[]{:S(2)}) collective-permute-start(bf16[16,5504]{1,0:T(8,128)(2,1)S(1)} %get-tuple-element.195.refs_11_), channel_id=1, source_target_pairs={{0,2},{1,3},{2,0},{3,1},{4,6},{5,7},{6,4},{7,5},{8,10},{9,11},{10,... | collective-permute-start | bytes 528392 | tf_op jit(solution)/shard_map/ppermute | solution.py:59
  156.5 1.9 %collective-permute-start.42 = (bf16[16,5504]{1,0:T(8,128)(2,1)S(1)}, bf16[16,5504]{1,0:T(8,128)(2,1)S(1)}, u32[]{:S(2)}, u32[]{:S(2)}) collective-permute-start(bf16[16,5504]{1,0:T(8,128)(2,1)S(1)} %get-tuple-element.196), channel_id=1, source_target_pairs={{0,1},{1,0},{2,3},{3,2},{4,5},{5,4},{6,7},{7,6},{8,9},{9,8},{10,11... | collective-permute-start | bytes 528392 | tf_op jit(solution)/shard_map/ppermute | solution.py:59
  158.3 1.8 %collective-permute-start.38 = (bf16[16,5504]{1,0:T(8,128)(2,1)S(1)}, bf16[16,5504]{1,0:T(8,128)(2,1)S(1)}, u32[]{:S(2)}, u32[]{:S(2)}) collective-permute-start(bf16[16,5504]{1,0:T(8,128)(2,1)S(1)} %get-tuple-element.191), channel_id=1, source_target_pairs={{0,2},{1,3},{2,0},{3,1},{4,6},{5,7},{6,4},{7,5},{8,10},{9,11},{10,... | collective-permute-start | bytes 528392 | tf_op jit(solution)/shard_map/ppermute | solution.py:59
  160.1 2.0 %collective-permute-start.39 = (bf16[16,5504]{1,0:T(8,128)(2,1)S(1)}, bf16[16,5504]{1,0:T(8,128)(2,1)S(1)}, u32[]{:S(2)}, u32[]{:S(2)}) collective-permute-start(bf16[16,5504]{1,0:T(8,128)(2,1)S(1)} %get-tuple-element.192), channel_id=1, source_target_pairs={{0,1},{1,0},{2,3},{3,2},{4,5},{5,4},{6,7},{7,6},{8,9},{9,8},{10,11... | collective-permute-start | bytes 528392 | tf_op jit(solution)/shard_map/ppermute | solution.py:59
  162.5 4.0 %collective-permute-done.40.refs_4_ = bf16[16,5504]{1,0:T(8,128)(2,1)S(1)} collective-permute-done((bf16[16,5504]{1,0:T(8,128)(2,1)S(1)}, bf16[16,5504]{1,0:T(8,128)(2,1)S(1)}, u32[]{:S(2)}, u32[]{:S(2)}) %collective-permute-start.40) | collective-permute-done | bytes 176160 | tf_op jit(solution)/shard_map/ppermute | solution.py:59
  166.6 1.3 shard_map.108.refs_6_
  168.9 1.1 shard_map.109
  (81 shorter events, 23.7 us)
Async XLA Ops:
  3.1 45.2 %collective-permute-start = (bf16[336,2560]{1,0:T(8,128)(2,1)S(1)}, bf16[336,2560]{1,0:T(8,128)(2,1)S(1)}, u32[]{:S(2)}, u32[]{:S(2)}) collective-permute-start(bf16[336,2560]{1,0:T(8,128)(2,1)S(1)} %pad_maximum_fusion.refs_5_.refs_0_), channel_id=1, source_target_pairs={{0,1},{1,0},{2,3},{3,2},{4,5},{5,4},{6,7},{7,6},{8,9},{9,8},{10,11... | collective-permute-start | bytes 5160968 | tf_op jit(solution)/shard_map/ppermute | solution.py:59
  7.2 2.9 %copy-start.1 = (bf16[1,64,2560]{2,1,0:T(8,128)(2,1)S(1)}, bf16[1,64,2560]{2,1,0:T(8,128)(2,1)}, u32[]{:S(2)}) copy-start(bf16[1,64,2560]{2,1,0:T(8,128)(2,1)} %param.15) | copy-start | bytes 983044
  7.2 2.9 %copy-start.2 = (bf16[1,64,2560]{2,1,0:T(8,128)(2,1)S(1)}, bf16[1,64,2560]{2,1,0:T(8,128)(2,1)}, u32[]{:S(2)}) copy-start(bf16[1,64,2560]{2,1,0:T(8,128)(2,1)} %param.8) | copy-start | bytes 983044
  7.2 2.9 %copy-start.3 = (f32[1,2560]{1,0:T(1,128)S(1)}, f32[1,2560]{1,0:T(1,128)}, u32[]{:S(2)}) copy-start(f32[1,2560]{1,0:T(1,128)} %refs_3_.3) | copy-start | bytes 30724
  7.2 2.9 %copy-start.4 = (s32[1,2,64,1]{2,3,1,0:T(1,128)S(1)}, s32[1,2,64,1]{2,3,1,0:T(1,128)}, u32[]{:S(2)}) copy-start(s32[1,2,64,1]{2,3,1,0:T(1,128)} %param.13) | copy-start | bytes 1540
  7.2 2.9 %copy-start.5 = (f32[1,2,64,1]{2,3,1,0:T(1,128)S(1)}, f32[1,2,64,1]{2,3,1,0:T(1,128)}, u32[]{:S(2)}) copy-start(f32[1,2,64,1]{2,3,1,0:T(1,128)} %param.14) | copy-start | bytes 1540
  8.4 39.9 %collective-permute-start.1 = (bf16[240,2560]{1,0:T(8,128)(2,1)S(1)}, bf16[240,2560]{1,0:T(8,128)(2,1)S(1)}, u32[]{:S(2)}, u32[]{:S(2)}) collective-permute-start(bf16[240,2560]{1,0:T(8,128)(2,1)S(1)} %pad_maximum_fusion.1.refs_6_.refs_2_), channel_id=1, source_target_pairs={{0,2},{1,3},{2,0},{3,1},{4,6},{5,7},{6,4},{7,5},{8,10},{9,11},{10,... | collective-permute-start | bytes 3686408 | tf_op jit(solution)/shard_map/ppermute | solution.py:59
  10.9 37.4 %collective-permute-start.2 = (bf16[32,5504]{1,0:T(8,128)(2,1)S(1)}, bf16[32,5504]{1,0:T(8,128)(2,1)S(1)}, u32[]{:S(2)}, u32[]{:S(2)}) collective-permute-start(bf16[32,5504]{1,0:T(8,128)(2,1)S(1)} %get-tuple-element.100), channel_id=1, source_target_pairs={{0,4},{1,5},{2,6},{3,7},{4,0},{5,1},{6,2},{7,3},{8,12},{9,13},{10,... | collective-permute-start | bytes 1056776 | tf_op jit(solution)/shard_map/ppermute | solution.py:59
  13.6 33.9 %collective-permute-start.4 = (bf16[16,5504]{1,0:T(8,128)(2,1)S(1)}, bf16[16,5504]{1,0:T(8,128)(2,1)S(1)}, u32[]{:S(2)}, u32[]{:S(2)}) collective-permute-start(bf16[16,5504]{1,0:T(8,128)(2,1)S(1)} %get-tuple-element.121.refs_5_), channel_id=1, source_target_pairs={{0,1},{1,0},{2,3},{3,2},{4,5},{5,4},{6,7},{7,6},{8,9},{9,8},{10,11... | collective-permute-start | bytes 528392 | tf_op jit(solution)/shard_map/ppermute | solution.py:59
  14.1 34.2 %collective-permute-start.3 = (bf16[16,5504]{1,0:T(8,128)(2,1)S(1)}, bf16[16,5504]{1,0:T(8,128)(2,1)S(1)}, u32[]{:S(2)}, u32[]{:S(2)}) collective-permute-start(bf16[16,5504]{1,0:T(8,128)(2,1)S(1)} %get-tuple-element.121.refs_5_), channel_id=1, source_target_pairs={{0,2},{1,3},{2,0},{3,1},{4,6},{5,7},{6,4},{7,5},{8,10},{9,11},{10,... | collective-permute-start | bytes 528392 | tf_op jit(solution)/shard_map/ppermute | solution.py:59
  48.3 5.5 %collective-permute-start.6 = (bf16[16,5504]{1,0:T(8,128)(2,1)S(1)}, bf16[16,5504]{1,0:T(8,128)(2,1)S(1)}, u32[]{:S(2)}, u32[]{:S(2)}) collective-permute-start(bf16[16,5504]{1,0:T(8,128)(2,1)S(1)} %get-tuple-element.109.refs_5_), channel_id=1, source_target_pairs={{0,1},{1,0},{2,3},{3,2},{4,5},{5,4},{6,7},{7,6},{8,9},{9,8},{10,11... | collective-permute-start | bytes 528392 | tf_op jit(solution)/shard_map/ppermute | solution.py:59
  49.3 5.5 %collective-permute-start.5 = (bf16[16,5504]{1,0:T(8,128)(2,1)S(1)}, bf16[16,5504]{1,0:T(8,128)(2,1)S(1)}, u32[]{:S(2)}, u32[]{:S(2)}) collective-permute-start(bf16[16,5504]{1,0:T(8,128)(2,1)S(1)} %get-tuple-element.109.refs_5_), channel_id=1, source_target_pairs={{0,2},{1,3},{2,0},{3,1},{4,6},{5,7},{6,4},{7,5},{8,10},{9,11},{10,... | collective-permute-start | bytes 528392 | tf_op jit(solution)/shard_map/ppermute | solution.py:59
  57.2 7.3 %collective-permute-start.8 = (bf16[16,5504]{1,0:T(8,128)(2,1)S(1)}, bf16[16,5504]{1,0:T(8,128)(2,1)S(1)}, u32[]{:S(2)}, u32[]{:S(2)}) collective-permute-start(bf16[16,5504]{1,0:T(8,128)(2,1)S(1)} %get-tuple-element.118.refs_7_), channel_id=1, source_target_pairs={{0,2},{1,3},{2,0},{3,1},{4,6},{5,7},{6,4},{7,5},{8,10},{9,11},{10,... | collective-permute-start | bytes 528392 | tf_op jit(solution)/shard_map/ppermute | solution.py:59
  58.9 7.4 %collective-permute-start.9 = (bf16[16,5504]{1,0:T(8,128)(2,1)S(1)}, bf16[16,5504]{1,0:T(8,128)(2,1)S(1)}, u32[]{:S(2)}, u32[]{:S(2)}) collective-permute-start(bf16[16,5504]{1,0:T(8,128)(2,1)S(1)} %get-tuple-element.119), channel_id=1, source_target_pairs={{0,1},{1,0},{2,3},{3,2},{4,5},{5,4},{6,7},{7,6},{8,9},{9,8},{10,11... | collective-permute-start | bytes 528392 | tf_op jit(solution)/shard_map/ppermute | solution.py:59
  60.0 10.3 %collective-permute-start.12 = (bf16[32,5504]{1,0:T(8,128)(2,1)S(1)}, bf16[32,5504]{1,0:T(8,128)(2,1)S(1)}, u32[]{:S(2)}, u32[]{:S(2)}) collective-permute-start(bf16[32,5504]{1,0:T(8,128)(2,1)S(1)} %pad_maximum_fusion.2.refs_5_), channel_id=1, source_target_pairs={{0,1},{1,0},{2,3},{3,2},{4,5},{5,4},{6,7},{7,6},{8,9},{9,8},{10,11... | collective-permute-start | bytes 1056776 | tf_op jit(solution)/shard_map/ppermute | solution.py:59
  60.9 9.4 %collective-permute-start.11 = (bf16[32,5504]{1,0:T(8,128)(2,1)S(1)}, bf16[32,5504]{1,0:T(8,128)(2,1)S(1)}, u32[]{:S(2)}, u32[]{:S(2)}) collective-permute-start(bf16[32,5504]{1,0:T(8,128)(2,1)S(1)} %pad_maximum_fusion.2.refs_5_), channel_id=1, source_target_pairs={{0,2},{1,3},{2,0},{3,1},{4,6},{5,7},{6,4},{7,5},{8,10},{9,11},{10,... | collective-permute-start | bytes 1056776 | tf_op jit(solution)/shard_map/ppermute | solution.py:59
  61.3 17.3 %collective-permute-start.7 = (bf16[80,2560]{1,0:T(8,128)(2,1)S(1)}, bf16[80,2560]{1,0:T(8,128)(2,1)S(1)}, u32[]{:S(2)}, u32[]{:S(2)}) collective-permute-start(bf16[80,2560]{1,0:T(8,128)(2,1)S(1)} %get-tuple-element.115), channel_id=1, source_target_pairs={{0,8},{1,9},{2,10},{3,11},{4,12},{5,13},{6,14},{7,15},{8,16},{9,17... | collective-permute-start | bytes 1228808 | tf_op jit(solution)/shard_map/ppermute | solution.py:59
  66.3 12.3 %collective-permute-start.10 = (bf16[16,5504]{1,0:T(8,128)(2,1)S(1)}, bf16[16,5504]{1,0:T(8,128)(2,1)S(1)}, u32[]{:S(2)}, u32[]{:S(2)}) collective-permute-start(bf16[16,5504]{1,0:T(8,128)(2,1)S(1)} %add_convert_fusion.3), channel_id=1, source_target_pairs={{0,12},{1,13},{2,14},{3,15},{4,8},{5,9},{6,10},{7,11},{8,20},{9,21... | collective-permute-start | bytes 528392 | tf_op jit(solution)/shard_map/ppermute | solution.py:59
  70.3 9.5 %collective-permute-start.13 = (bf16[16,5504]{1,0:T(8,128)(2,1)S(1)}, bf16[16,5504]{1,0:T(8,128)(2,1)S(1)}, u32[]{:S(2)}, u32[]{:S(2)}) collective-permute-start(bf16[16,5504]{1,0:T(8,128)(2,1)S(1)} %get-tuple-element.127), channel_id=1, source_target_pairs={{0,10},{1,11},{2,8},{3,9},{4,14},{5,15},{6,12},{7,13},{8,18},{9,19... | collective-permute-start | bytes 528392 | tf_op jit(solution)/shard_map/ppermute | solution.py:59
  70.3 9.5 %collective-permute-start.14 = (bf16[16,5504]{1,0:T(8,128)(2,1)S(1)}, bf16[16,5504]{1,0:T(8,128)(2,1)S(1)}, u32[]{:S(2)}, u32[]{:S(2)}) collective-permute-start(bf16[16,5504]{1,0:T(8,128)(2,1)S(1)} %get-tuple-element.128), channel_id=1, source_target_pairs={{0,9},{1,8},{2,11},{3,10},{4,13},{5,12},{6,15},{7,14},{8,17},{9,16... | collective-permute-start | bytes 528392 | tf_op jit(solution)/shard_map/ppermute | solution.py:59
  72.3 8.7 %collective-permute-start.15 = (bf16[16,5504]{1,0:T(8,128)(2,1)S(1)}, bf16[16,5504]{1,0:T(8,128)(2,1)S(1)}, u32[]{:S(2)}, u32[]{:S(2)}) collective-permute-start(bf16[16,5504]{1,0:T(8,128)(2,1)S(1)} %get-tuple-element.129), channel_id=1, source_target_pairs={{0,8},{1,9},{2,10},{3,11},{4,12},{5,13},{6,14},{7,15},{8,16},{9,17... | collective-permute-start | bytes 528392 | tf_op jit(solution)/shard_map/ppermute | solution.py:59
  81.9 10.8 %collective-permute-start.16 = (bf16[16,5504]{1,0:T(8,128)(2,1)S(1)}, bf16[16,5504]{1,0:T(8,128)(2,1)S(1)}, u32[]{:S(2)}, u32[]{:S(2)}) collective-permute-start(bf16[16,5504]{1,0:T(8,128)(2,1)S(1)} %get-tuple-element.138), channel_id=1, source_target_pairs={{0,4},{1,5},{2,6},{3,7},{4,0},{5,1},{6,2},{7,3},{8,12},{9,13},{10,... | collective-permute-start | bytes 528392 | tf_op jit(solution)/shard_map/ppermute | solution.py:59
  83.8 8.9 %collective-permute-start.18 = (bf16[16,5504]{1,0:T(8,128)(2,1)S(1)}, bf16[16,5504]{1,0:T(8,128)(2,1)S(1)}, u32[]{:S(2)}, u32[]{:S(2)}) collective-permute-start(bf16[16,5504]{1,0:T(8,128)(2,1)S(1)} %get-tuple-element.139.refs_9_), channel_id=1, source_target_pairs={{0,1},{1,0},{2,3},{3,2},{4,5},{5,4},{6,7},{7,6},{8,9},{9,8},{10,11... | collective-permute-start | bytes 528392 | tf_op jit(solution)/shard_map/ppermute | solution.py:59
  84.3 9.1 %collective-permute-start.17 = (bf16[16,5504]{1,0:T(8,128)(2,1)S(1)}, bf16[16,5504]{1,0:T(8,128)(2,1)S(1)}, u32[]{:S(2)}, u32[]{:S(2)}) collective-permute-start(bf16[16,5504]{1,0:T(8,128)(2,1)S(1)} %get-tuple-element.139.refs_9_), channel_id=1, source_target_pairs={{0,2},{1,3},{2,0},{3,1},{4,6},{5,7},{6,4},{7,5},{8,10},{9,11},{10,... | collective-permute-start | bytes 528392 | tf_op jit(solution)/shard_map/ppermute | solution.py:59
  93.4 5.7 %collective-permute-start.20 = (bf16[16,5504]{1,0:T(8,128)(2,1)S(1)}, bf16[16,5504]{1,0:T(8,128)(2,1)S(1)}, u32[]{:S(2)}, u32[]{:S(2)}) collective-permute-start(bf16[16,5504]{1,0:T(8,128)(2,1)S(1)} %collective-permute-done.16.refs_9_), channel_id=1, source_target_pairs={{0,1},{1,0},{2,3},{3,2},{4,5},{5,4},{6,7},{7,6},{8,9},{9,8},{10,11... | collective-permute-start | bytes 528392 | tf_op jit(solution)/shard_map/ppermute | solution.py:59
  94.4 5.5 %collective-permute-start.19 = (bf16[16,5504]{1,0:T(8,128)(2,1)S(1)}, bf16[16,5504]{1,0:T(8,128)(2,1)S(1)}, u32[]{:S(2)}, u32[]{:S(2)}) collective-permute-start(bf16[16,5504]{1,0:T(8,128)(2,1)S(1)} %collective-permute-done.16.refs_9_), channel_id=1, source_target_pairs={{0,2},{1,3},{2,0},{3,1},{4,6},{5,7},{6,4},{7,5},{8,10},{9,11},{10,... | collective-permute-start | bytes 528392 | tf_op jit(solution)/shard_map/ppermute | solution.py:59
  103.4 5.8 %collective-permute-start.21 = (bf16[16,5504]{1,0:T(8,128)(2,1)S(1)}, bf16[16,5504]{1,0:T(8,128)(2,1)S(1)}, u32[]{:S(2)}, u32[]{:S(2)}) collective-permute-start(bf16[16,5504]{1,0:T(8,128)(2,1)S(1)} %get-tuple-element.153), channel_id=1, source_target_pairs={{0,2},{1,3},{2,0},{3,1},{4,6},{5,7},{6,4},{7,5},{8,10},{9,11},{10,... | collective-permute-start | bytes 528392 | tf_op jit(solution)/shard_map/ppermute | solution.py:59
  104.4 6.0 %collective-permute-start.22 = (bf16[16,5504]{1,0:T(8,128)(2,1)S(1)}, bf16[16,5504]{1,0:T(8,128)(2,1)S(1)}, u32[]{:S(2)}, u32[]{:S(2)}) collective-permute-start(bf16[16,5504]{1,0:T(8,128)(2,1)S(1)} %get-tuple-element.154), channel_id=1, source_target_pairs={{0,1},{1,0},{2,3},{3,2},{4,5},{5,4},{6,7},{7,6},{8,9},{9,8},{10,11... | collective-permute-start | bytes 528392 | tf_op jit(solution)/shard_map/ppermute | solution.py:59
  105.4 24.1 %collective-permute-start.24 = (bf16[144,2560]{1,0:T(8,128)(2,1)S(1)}, bf16[144,2560]{1,0:T(8,128)(2,1)S(1)}, u32[]{:S(2)}, u32[]{:S(2)}) collective-permute-start(bf16[144,2560]{1,0:T(8,128)(2,1)S(1)} %get-tuple-element.159), channel_id=1, source_target_pairs={{0,24},{1,25},{2,26},{3,27},{4,28},{5,29},{6,30},{7,31},{8,0},{9,1... | collective-permute-start | bytes 2211848 | tf_op jit(solution)/shard_map/ppermute | solution.py:59
  105.4 9.1 %collective-permute-start.25 = (bf16[16,5504]{1,0:T(8,128)(2,1)S(1)}, bf16[16,5504]{1,0:T(8,128)(2,1)S(1)}, u32[]{:S(2)}, u32[]{:S(2)}) collective-permute-start(bf16[16,5504]{1,0:T(8,128)(2,1)S(1)} %get-tuple-element.162), channel_id=1, source_target_pairs={{0,2},{1,3},{2,0},{3,1},{4,6},{5,7},{6,4},{7,5},{8,10},{9,11},{10,... | collective-permute-start | bytes 528392 | tf_op jit(solution)/shard_map/ppermute | solution.py:59
  106.5 8.1 %collective-permute-start.26 = (bf16[16,5504]{1,0:T(8,128)(2,1)S(1)}, bf16[16,5504]{1,0:T(8,128)(2,1)S(1)}, u32[]{:S(2)}, u32[]{:S(2)}) collective-permute-start(bf16[16,5504]{1,0:T(8,128)(2,1)S(1)} %get-tuple-element.163), channel_id=1, source_target_pairs={{0,1},{1,0},{2,3},{3,2},{4,5},{5,4},{6,7},{7,6},{8,9},{9,8},{10,11... | collective-permute-start | bytes 528392 | tf_op jit(solution)/shard_map/ppermute | solution.py:59
  110.5 9.3 %collective-permute-start.23 = (bf16[16,5504]{1,0:T(8,128)(2,1)S(1)}, bf16[16,5504]{1,0:T(8,128)(2,1)S(1)}, u32[]{:S(2)}, u32[]{:S(2)}) collective-permute-start(bf16[16,5504]{1,0:T(8,128)(2,1)S(1)} %add_convert_fusion.2), channel_id=1, source_target_pairs={{0,4},{1,5},{2,6},{3,7},{4,0},{5,1},{6,2},{7,3},{8,12},{9,13},{10,... | collective-permute-start | bytes 528392 | tf_op jit(solution)/shard_map/ppermute | solution.py:59
  114.6 8.7 %collective-permute-start.28 = (bf16[16,5504]{1,0:T(8,128)(2,1)S(1)}, bf16[16,5504]{1,0:T(8,128)(2,1)S(1)}, u32[]{:S(2)}, u32[]{:S(2)}) collective-permute-start(bf16[16,5504]{1,0:T(8,128)(2,1)S(1)} %get-tuple-element.166.refs_11_), channel_id=1, source_target_pairs={{0,26},{1,27},{2,24},{3,25},{4,30},{5,31},{6,28},{7,29},{8,2},{9,3... | collective-permute-start | bytes 528392 | tf_op jit(solution)/shard_map/ppermute | solution.py:59
  114.7 8.6 %collective-permute-start.29 = (bf16[16,5504]{1,0:T(8,128)(2,1)S(1)}, bf16[16,5504]{1,0:T(8,128)(2,1)S(1)}, u32[]{:S(2)}, u32[]{:S(2)}) collective-permute-start(bf16[16,5504]{1,0:T(8,128)(2,1)S(1)} %get-tuple-element.167), channel_id=1, source_target_pairs={{0,25},{1,24},{2,27},{3,26},{4,29},{5,28},{6,31},{7,30},{8,1},{9,0... | collective-permute-start | bytes 528392 | tf_op jit(solution)/shard_map/ppermute | solution.py:59
  115.3 8.1 %collective-permute-start.30 = (bf16[16,5504]{1,0:T(8,128)(2,1)S(1)}, bf16[16,5504]{1,0:T(8,128)(2,1)S(1)}, u32[]{:S(2)}, u32[]{:S(2)}) collective-permute-start(bf16[16,5504]{1,0:T(8,128)(2,1)S(1)} %get-tuple-element.168), channel_id=1, source_target_pairs={{0,24},{1,25},{2,26},{3,27},{4,28},{5,29},{6,30},{7,31},{8,0},{9,1... | collective-permute-start | bytes 528392 | tf_op jit(solution)/shard_map/ppermute | solution.py:59
  119.9 9.6 %collective-permute-start.27 = (bf16[16,5504]{1,0:T(8,128)(2,1)S(1)}, bf16[16,5504]{1,0:T(8,128)(2,1)S(1)}, u32[]{:S(2)}, u32[]{:S(2)}) collective-permute-start(bf16[16,5504]{1,0:T(8,128)(2,1)S(1)} %add_convert_fusion.1), channel_id=1, source_target_pairs={{0,28},{1,29},{2,30},{3,31},{4,24},{5,25},{6,26},{7,27},{8,4},{9,5... | collective-permute-start | bytes 528392 | tf_op jit(solution)/shard_map/ppermute | solution.py:59
  130.5 9.5 %collective-permute-start.31 = (bf16[16,5504]{1,0:T(8,128)(2,1)S(1)}, bf16[16,5504]{1,0:T(8,128)(2,1)S(1)}, u32[]{:S(2)}, u32[]{:S(2)}) collective-permute-start(bf16[16,5504]{1,0:T(8,128)(2,1)S(1)} %get-tuple-element.169), channel_id=1, source_target_pairs={{0,4},{1,5},{2,6},{3,7},{4,0},{5,1},{6,2},{7,3},{8,12},{9,13},{10,... | collective-permute-start | bytes 528392 | tf_op jit(solution)/shard_map/ppermute | solution.py:59
  130.6 9.4 %collective-permute-start.33 = (bf16[16,5504]{1,0:T(8,128)(2,1)S(1)}, bf16[16,5504]{1,0:T(8,128)(2,1)S(1)}, u32[]{:S(2)}, u32[]{:S(2)}) collective-permute-start(bf16[16,5504]{1,0:T(8,128)(2,1)S(1)} %get-tuple-element.170.refs_9_), channel_id=1, source_target_pairs={{0,1},{1,0},{2,3},{3,2},{4,5},{5,4},{6,7},{7,6},{8,9},{9,8},{10,11... | collective-permute-start | bytes 528392 | tf_op jit(solution)/shard_map/ppermute | solution.py:59
  130.7 10.1 %collective-permute-start.32 = (bf16[16,5504]{1,0:T(8,128)(2,1)S(1)}, bf16[16,5504]{1,0:T(8,128)(2,1)S(1)}, u32[]{:S(2)}, u32[]{:S(2)}) collective-permute-start(bf16[16,5504]{1,0:T(8,128)(2,1)S(1)} %get-tuple-element.170.refs_9_), channel_id=1, source_target_pairs={{0,2},{1,3},{2,0},{3,1},{4,6},{5,7},{6,4},{7,5},{8,10},{9,11},{10,... | collective-permute-start | bytes 528392 | tf_op jit(solution)/shard_map/ppermute | solution.py:59
  140.8 5.5 %collective-permute-start.35 = (bf16[16,5504]{1,0:T(8,128)(2,1)S(1)}, bf16[16,5504]{1,0:T(8,128)(2,1)S(1)}, u32[]{:S(2)}, u32[]{:S(2)}) collective-permute-start(bf16[16,5504]{1,0:T(8,128)(2,1)S(1)} %collective-permute-done.31.refs_9_), channel_id=1, source_target_pairs={{0,1},{1,0},{2,3},{3,2},{4,5},{5,4},{6,7},{7,6},{8,9},{9,8},{10,11... | collective-permute-start | bytes 528392 | tf_op jit(solution)/shard_map/ppermute | solution.py:59
  141.1 5.5 %collective-permute-start.34 = (bf16[16,5504]{1,0:T(8,128)(2,1)S(1)}, bf16[16,5504]{1,0:T(8,128)(2,1)S(1)}, u32[]{:S(2)}, u32[]{:S(2)}) collective-permute-start(bf16[16,5504]{1,0:T(8,128)(2,1)S(1)} %collective-permute-done.31.refs_9_), channel_id=1, source_target_pairs={{0,2},{1,3},{2,0},{3,1},{4,6},{5,7},{6,4},{7,5},{8,10},{9,11},{10,... | collective-permute-start | bytes 528392 | tf_op jit(solution)/shard_map/ppermute | solution.py:59
  148.6 5.5 %collective-permute-start.36 = (bf16[16,5504]{1,0:T(8,128)(2,1)S(1)}, bf16[16,5504]{1,0:T(8,128)(2,1)S(1)}, u32[]{:S(2)}, u32[]{:S(2)}) collective-permute-start(bf16[16,5504]{1,0:T(8,128)(2,1)S(1)} %get-tuple-element.189), channel_id=1, source_target_pairs={{0,2},{1,3},{2,0},{3,1},{4,6},{5,7},{6,4},{7,5},{8,10},{9,11},{10,... | collective-permute-start | bytes 528392 | tf_op jit(solution)/shard_map/ppermute | solution.py:59
  148.6 5.5 %collective-permute-start.37 = (bf16[16,5504]{1,0:T(8,128)(2,1)S(1)}, bf16[16,5504]{1,0:T(8,128)(2,1)S(1)}, u32[]{:S(2)}, u32[]{:S(2)}) collective-permute-start(bf16[16,5504]{1,0:T(8,128)(2,1)S(1)} %get-tuple-element.190), channel_id=1, source_target_pairs={{0,1},{1,0},{2,3},{3,2},{4,5},{5,4},{6,7},{7,6},{8,9},{9,8},{10,11... | collective-permute-start | bytes 528392 | tf_op jit(solution)/shard_map/ppermute | solution.py:59
  154.2 8.3 %collective-permute-start.41 = (bf16[16,5504]{1,0:T(8,128)(2,1)S(1)}, bf16[16,5504]{1,0:T(8,128)(2,1)S(1)}, u32[]{:S(2)}, u32[]{:S(2)}) collective-permute-start(bf16[16,5504]{1,0:T(8,128)(2,1)S(1)} %get-tuple-element.195.refs_11_), channel_id=1, source_target_pairs={{0,2},{1,3},{2,0},{3,1},{4,6},{5,7},{6,4},{7,5},{8,10},{9,11},{10,... | collective-permute-start | bytes 528392 | tf_op jit(solution)/shard_map/ppermute | solution.py:59
  156.5 6.1 %collective-permute-start.42 = (bf16[16,5504]{1,0:T(8,128)(2,1)S(1)}, bf16[16,5504]{1,0:T(8,128)(2,1)S(1)}, u32[]{:S(2)}, u32[]{:S(2)}) collective-permute-start(bf16[16,5504]{1,0:T(8,128)(2,1)S(1)} %get-tuple-element.196), channel_id=1, source_target_pairs={{0,1},{1,0},{2,3},{3,2},{4,5},{5,4},{6,7},{7,6},{8,9},{9,8},{10,11... | collective-permute-start | bytes 528392 | tf_op jit(solution)/shard_map/ppermute | solution.py:59
  158.3 8.2 %collective-permute-start.40 = (bf16[16,5504]{1,0:T(8,128)(2,1)S(1)}, bf16[16,5504]{1,0:T(8,128)(2,1)S(1)}, u32[]{:S(2)}, u32[]{:S(2)}) collective-permute-start(bf16[16,5504]{1,0:T(8,128)(2,1)S(1)} %add_convert_fusion), channel_id=1, source_target_pairs={{0,4},{1,5},{2,6},{3,7},{4,0},{5,1},{6,2},{7,3},{8,12},{9,13},{10,... | collective-permute-start | bytes 528392 | tf_op jit(solution)/shard_map/ppermute | solution.py:59
  158.3 9.6 %collective-permute-start.38 = (bf16[16,5504]{1,0:T(8,128)(2,1)S(1)}, bf16[16,5504]{1,0:T(8,128)(2,1)S(1)}, u32[]{:S(2)}, u32[]{:S(2)}) collective-permute-start(bf16[16,5504]{1,0:T(8,128)(2,1)S(1)} %get-tuple-element.191), channel_id=1, source_target_pairs={{0,2},{1,3},{2,0},{3,1},{4,6},{5,7},{6,4},{7,5},{8,10},{9,11},{10,... | collective-permute-start | bytes 528392 | tf_op jit(solution)/shard_map/ppermute | solution.py:59
  160.1 7.8 %collective-permute-start.39 = (bf16[16,5504]{1,0:T(8,128)(2,1)S(1)}, bf16[16,5504]{1,0:T(8,128)(2,1)S(1)}, u32[]{:S(2)}, u32[]{:S(2)}) collective-permute-start(bf16[16,5504]{1,0:T(8,128)(2,1)S(1)} %get-tuple-element.192), channel_id=1, source_target_pairs={{0,1},{1,0},{2,3},{3,2},{4,5},{5,4},{6,7},{7,6},{8,9},{9,8},{10,11... | collective-permute-start | bytes 528392 | tf_op jit(solution)/shard_map/ppermute | solution.py:59
  (2 other events, 3.3 us)

commit v4 on v3

--- a/solution.py
+++ b/solution.py
@@ -262,7 +262,7 @@
 
 
 def combine(box, notes, n, own, back, picked):
-    sums = [total_of(own)] + [ref[...] for ref in back]
+    sums = [total_of(own)] + [ref[...].astype(BF) for ref in back]
     pick_rows(box, slots_in(notes, n), sums, n, picked)
     return mix_in(notes, n) * picked[...]
 
@@ -558,7 +558,8 @@
     cross_fin = down(cross1, cross_kept1)[0]
     arrived1 = shift(behind, sections=-1)
     got, _ = give_back(cross_grad, own_grad, -1)
-    fin_back = home(sums(cross_fin), 0)
+    got[: experts - 1], fin_sums = fence((got[: experts - 1], sums(cross_fin)))
+    fin_back = home(fin_sums, 0)
     own_fin = down(own1, own_kept1)[0]
     g1, own_g, *boxes_g = call(
         bind(turn_kernel, box, experts),
@@ -567,11 +568,10 @@
         notes0,
         *got,
         scratch=[picked],
-        after=fin_back,
-    )
-
-    cross_g, own_z, own_x = fence(
-        (crossing_of(boxes_g), shift(own_g, flip=2), shift(own_g, flip=1))
+    )
+
+    cross_g, own_z, own_x, fin_back = fence(
+        (crossing_of(boxes_g), shift(own_g, flip=2), shift(own_g, flip=1), fin_back)
     )
     cross_g, own_g = around(cross_g), [own_z, own_g, own_x]
     back = bind(expert_call, back_kernel, box, packs)
@@ -579,7 +579,7 @@
     cross_grad = back(cross_g, cross_kept0, after=own_grad[:1])[0]
     total = sums(cross_grad)
     own_grad, own_fin, _ = fence((own_grad, own_fin, total))
-    got = home(total, 0) + own_home(own_grad, 0)
+    got = [array.astype(F32) for array in home(total, 0)] + own_home(own_grad, 0)
     fin_own = own_home(own_fin, 0)
     (g0,) = call(
         bind(last_kernel, box, experts),
@@ -599,7 +599,6 @@
         *fin_back,
         *fin_own,
         scratch=[picked],
-        after=[g0],
     )
     return (final[None], g0[None])
 

time: 170 us -> 168 us (0.988)
  waiting for transfers between devices: 93.9 us -> 92.1 us
    ppermute x43, waiting for transfers between devices: 93.9 us -> 92.1 us  [shift(): return lax.ppermute(value, ('section', 'expert'), pairs)]
  transfers between devices with their start and end apart: 43 -> 43, of which waited for: 26 -> 29; matrix products, arithmetic and copies ran while one was open for 1% -> 1% of each run, Pallas kernels for 7% -> 8%
where the time goes in v4:
time: 168 us; the launch traced here: 167 us
  waiting for transfers between devices  92.1 us (55%)
  starting transfers between devices  46.3 us (28%)
  Pallas kernels  23 us (14%)
  local copies, waits for them, and re-layouts  4.53 us (3%)
    ppermute x43, waiting for transfers between devices, shift(): return lax.ppermute(value, ('section', 'expert'), pairs)  92.1 us
    ppermute x43, starting transfers between devices, shift(): return lax.ppermute(value, ('section', 'expert'), pairs)  46.3 us
    pallas_call x15, Pallas kernels, call(): pl.pallas_call(reading, out_shape=list(outs), in_specs=[vmem] * read + [p...  23 us
  transfers between devices with their start and end apart: 43, of which 29 were waited for; matrix products, arithmetic and copies ran while one was open for 1% of the time, Pallas kernels for 8%

profile of v4, /device:TPU:0, one launch (start us, length us, event | category | flops | bytes accessed | tf_op | source)
XLA Modules:
  0.0 167.3 jit_solution(2288544658298479671)
XLA Ops:
  0.6 1.2 slice.40
  1.8 1.1 slice.41
  3.1 3.0 %collective-permute-start = (bf16[336,2560]{1,0:T(8,128)(2,1)S(1)}, bf16[336,2560]{1,0:T(8,128)(2,1)S(1)}, u32[]{:S(2)}, u32[]{:S(2)}) collective-permute-start(bf16[336,2560]{1,0:T(8,128)(2,1)S(1)} %pad_maximum_fusion.refs_5_.refs_0_), channel_id=1, source_target_pairs={{0,1},{1,0},{2,3},{3,2},{4,5},{5,4},{6,7},{7,6},{8,9},{9,8},{10,11... | collective-permute-start | bytes 5160968 | tf_op jit(solution)/shard_map/ppermute | solution.py:59
  6.1 1.0 slice.42
  7.2 1.1 slice.43
  8.4 1.6 collective-permute-start.1
  10.9 2.6 %collective-permute-start.2 = (bf16[32,5504]{1,0:T(8,128)(2,1)S(1)}, bf16[32,5504]{1,0:T(8,128)(2,1)S(1)}, u32[]{:S(2)}, u32[]{:S(2)}) collective-permute-start(bf16[32,5504]{1,0:T(8,128)(2,1)S(1)} %get-tuple-element.103), channel_id=1, source_target_pairs={{0,4},{1,5},{2,6},{3,7},{4,0},{5,1},{6,2},{7,3},{8,12},{9,13},{10,... | collective-permute-start | bytes 1056776 | tf_op jit(solution)/shard_map/ppermute | solution.py:59
  14.5 32.9 %collective-permute-done.4.refs_6_ = bf16[16,5504]{1,0:T(8,128)(2,1)S(1)} collective-permute-done((bf16[16,5504]{1,0:T(8,128)(2,1)S(1)}, bf16[16,5504]{1,0:T(8,128)(2,1)S(1)}, u32[]{:S(2)}, u32[]{:S(2)}) %collective-permute-start.4) | collective-permute-done | bytes 176160 | tf_op jit(solution)/shard_map/ppermute | solution.py:59
  49.3 1.6 collective-permute-start.5
  50.9 2.9 %collective-permute-done.6.refs_6_ = bf16[16,5504]{1,0:T(8,128)(2,1)S(1)} collective-permute-done((bf16[16,5504]{1,0:T(8,128)(2,1)S(1)}, bf16[16,5504]{1,0:T(8,128)(2,1)S(1)}, u32[]{:S(2)}, u32[]{:S(2)}) %collective-permute-start.6) | collective-permute-done | bytes 176160 | tf_op jit(solution)/shard_map/ppermute | solution.py:59
  54.8 2.5 %shard_map.96 = (bf16[16,5504]{1,0:T(8,128)(2,1)S(1)}, bf16[16,5504]{1,0:T(8,128)(2,1)S(1)}, bf16[16,5504]{1,0:T(8,128)(2,1)S(1)}, f32[96,224]{1,0:T(8,128)S(1)}...) custom-call(bf16[336,2560]{1,0:T(8,128)(2,1)S(1)} %pad_maximum_fusion.refs_5_.refs_0_, ...), custom_call_target="tpu_custom_call" | custom-call | flops 566231040 | bytes 7249920 | tf_op jit(solution)/shard_map/pallas_call | solution.py:71
  57.2 1.6 collective-permute-start.8
  58.9 1.1 collective-permute-start.9
  61.3 2.5 %shard_map.97 = (bf16[16,5504]{1,0:T(8,128)(2,1)S(1)}, bf16[16,5504]{1,0:T(8,128)(2,1)S(1)}, bf16[16,5504]{1,0:T(8,128)(2,1)S(1)}, f32[96,224]{1,0:T(8,128)S(1)}...) custom-call(bf16[336,2560]{1,0:T(8,128)(2,1)S(1)} %pad_maximum_fusion.refs_5_.refs_0_, ...), custom_call_target="tpu_custom_call" | custom-call | flops 566231040 | bytes 7249920 | tf_op jit(solution)/shard_map/pallas_call | solution.py:71
  64.5 1.7 %collective-permute-done.9 = bf16[16,5504]{1,0:T(8,128)(2,1)S(1)} collective-permute-done((bf16[16,5504]{1,0:T(8,128)(2,1)S(1)}, bf16[16,5504]{1,0:T(8,128)(2,1)S(1)}, u32[]{:S(2)}, u32[]{:S(2)}) %collective-permute-start.9) | collective-permute-done | bytes 176160 | tf_op jit(solution)/shard_map/ppermute | solution.py:59
  66.3 1.5 collective-permute-start.10
  67.8 2.5 %collective-permute-done.12.refs_6_ = bf16[32,5504]{1,0:T(8,128)(2,1)S(1)} collective-permute-done((bf16[32,5504]{1,0:T(8,128)(2,1)S(1)}, bf16[32,5504]{1,0:T(8,128)(2,1)S(1)}, u32[]{:S(2)}, u32[]{:S(2)}) %collective-permute-start.12) | collective-permute-done | bytes 352288 | tf_op jit(solution)/shard_map/ppermute | solution.py:59
  70.3 1.9 %collective-permute-start.14 = (bf16[16,5504]{1,0:T(8,128)(2,1)S(1)}, bf16[16,5504]{1,0:T(8,128)(2,1)S(1)}, u32[]{:S(2)}, u32[]{:S(2)}) collective-permute-start(bf16[16,5504]{1,0:T(8,128)(2,1)S(1)} %get-tuple-element.131), channel_id=1, source_target_pairs={{0,9},{1,8},{2,11},{3,10},{4,13},{5,12},{6,15},{7,14},{8,17},{9,16... | collective-permute-start | bytes 528392 | tf_op jit(solution)/shard_map/ppermute | solution.py:59
  72.3 6.4 %collective-permute-done.10.refs_4_ = bf16[16,5504]{1,0:T(8,128)(2,1)S(1)} collective-permute-done((bf16[16,5504]{1,0:T(8,128)(2,1)S(1)}, bf16[16,5504]{1,0:T(8,128)(2,1)S(1)}, u32[]{:S(2)}, u32[]{:S(2)}) %collective-permute-start.10) | collective-permute-done | bytes 176160 | tf_op jit(solution)/shard_map/ppermute | solution.py:59
  78.6 1.2 collective-permute-done.13.refs_5_
  79.8 1.1 collective-permute-done.15.refs_7_
  81.9 1.9 %collective-permute-start.17 = (bf16[16,5504]{1,0:T(8,128)(2,1)S(1)}, bf16[16,5504]{1,0:T(8,128)(2,1)S(1)}, u32[]{:S(2)}, u32[]{:S(2)}) collective-permute-start(bf16[16,5504]{1,0:T(8,128)(2,1)S(1)} %get-tuple-element.143), channel_id=1, source_target_pairs={{0,4},{1,5},{2,6},{3,7},{4,0},{5,1},{6,2},{7,3},{8,12},{9,13},{10,... | collective-permute-start | bytes 528392 | tf_op jit(solution)/shard_map/ppermute | solution.py:59
  84.3 2.5 %collective-permute-start.18 = (bf16[16,5504]{1,0:T(8,128)(2,1)S(1)}, bf16[16,5504]{1,0:T(8,128)(2,1)S(1)}, u32[]{:S(2)}, u32[]{:S(2)}) collective-permute-start(bf16[16,5504]{1,0:T(8,128)(2,1)S(1)} %get-tuple-element.144.refs_9_), channel_id=1, source_target_pairs={{0,2},{1,3},{2,0},{3,1},{4,6},{5,7},{6,4},{7,5},{8,10},{9,11},{10,... | collective-permute-start | bytes 528392 | tf_op jit(solution)/shard_map/ppermute | solution.py:59
  86.8 5.8 %collective-permute-done.17.refs_9_ = bf16[16,5504]{1,0:T(8,128)(2,1)S(1)} collective-permute-done((bf16[16,5504]{1,0:T(8,128)(2,1)S(1)}, bf16[16,5504]{1,0:T(8,128)(2,1)S(1)}, u32[]{:S(2)}, u32[]{:S(2)}) %collective-permute-start.17) | collective-permute-done | bytes 176160 | tf_op jit(solution)/shard_map/ppermute | solution.py:59
  93.4 1.0 collective-permute-start.21
  96.4 2.6 %shard_map.101 = (bf16[16,5504]{1,0:T(8,128)(2,1)S(1)}, bf16[16,5504]{1,0:T(8,128)(2,1)S(1)}, bf16[16,5504]{1,0:T(8,128)(2,1)S(1)}, f32[96,224]{1,0:T(8,128)S(1)...) custom-call(bf16[336,2560]{1,0:T(8,128)(2,1)S(1)} %pad_maximum_fusion.refs_5_.refs_0_, ...), custom_call_target="tpu_custom_call" | custom-call | flops 566231040 | bytes 7397376 | tf_op jit(solution)/shard_map/pallas_call | solution.py:71
  99.9 2.6 %shard_map.102 = (bf16[16,5504]{1,0:T(8,128)(2,1)S(1)}, bf16[16,5504]{1,0:T(8,128)(2,1)S(1)}, bf16[16,5504]{1,0:T(8,128)(2,1)S(1)}, f32[96,224]{1,0:T(8,128)S(1)...) custom-call(bf16[336,2560]{1,0:T(8,128)(2,1)S(1)} %pad_maximum_fusion.refs_5_.refs_0_, ...), custom_call_target="tpu_custom_call" | custom-call | flops 566231040 | bytes 7397376 | tf_op jit(solution)/shard_map/pallas_call | solution.py:71
  102.5 1.0 collective-permute-start.22
  103.5 1.0 collective-permute-start.23
  105.4 1.0 collective-permute-start.25
  108.0 1.0 collective-permute-done.23
  109.5 2.7 %collective-permute-start.27 = (bf16[16,5504]{1,0:T(8,128)(2,1)S(1)}, bf16[16,5504]{1,0:T(8,128)(2,1)S(1)}, u32[]{:S(2)}, u32[]{:S(2)}) collective-permute-start(bf16[16,5504]{1,0:T(8,128)(2,1)S(1)} %get-tuple-element.166.refs_11_), channel_id=1, source_target_pairs={{0,26},{1,27},{2,24},{3,25},{4,30},{5,31},{6,28},{7,29},{8,2},{9,3... | collective-permute-start | bytes 528392 | tf_op jit(solution)/shard_map/ppermute | solution.py:59
  114.1 6.4 %collective-permute-done.24.refs_2_ = bf16[16,5504]{1,0:T(8,128)(2,1)S(1)} collective-permute-done((bf16[16,5504]{1,0:T(8,128)(2,1)S(1)}, bf16[16,5504]{1,0:T(8,128)(2,1)S(1)}, u32[]{:S(2)}, u32[]{:S(2)}) %collective-permute-start.24) | collective-permute-done | bytes 176160 | tf_op jit(solution)/shard_map/ppermute | solution.py:59
  122.1 2.4 %collective-permute-start.30 = (bf16[16,5504]{1,0:T(8,128)(2,1)S(1)}, bf16[16,5504]{1,0:T(8,128)(2,1)S(1)}, u32[]{:S(2)}, u32[]{:S(2)}) collective-permute-start(bf16[16,5504]{1,0:T(8,128)(2,1)S(1)} %get-tuple-element.169), channel_id=1, source_target_pairs={{0,4},{1,5},{2,6},{3,7},{4,0},{5,1},{6,2},{7,3},{8,12},{9,13},{10,... | collective-permute-start | bytes 528392 | tf_op jit(solution)/shard_map/ppermute | solution.py:59
  126.2 8.6 %collective-permute-done.33.refs_2_ = bf16[16,5504]{1,0:T(8,128)(2,1)S(1)} collective-permute-done((bf16[16,5504]{1,0:T(8,128)(2,1)S(1)}, bf16[16,5504]{1,0:T(8,128)(2,1)S(1)}, u32[]{:S(2)}, u32[]{:S(2)}) %collective-permute-start.33) | collective-permute-done | bytes 176160 | tf_op jit(solution)/shard_map/ppermute | solution.py:59
  134.8 3.7 %collective-permute-done.30.refs_9_ = bf16[16,5504]{1,0:T(8,128)(2,1)S(1)} collective-permute-done((bf16[16,5504]{1,0:T(8,128)(2,1)S(1)}, bf16[16,5504]{1,0:T(8,128)(2,1)S(1)}, u32[]{:S(2)}, u32[]{:S(2)}) %collective-permute-start.30) | collective-permute-done | bytes 176160 | tf_op jit(solution)/shard_map/ppermute | solution.py:59
  140.0 2.0 %shard_map.105 = (bf16[16,5504]{1,0:T(8,128)(2,1)S(1)}, bf16[16,5504]{1,0:T(8,128)(2,1)S(1)}, bf16[16,5504]{1,0:T(8,128)(2,1)S(1)}) custom-call(bf16[336,2560]{1,0:T(8,128)(2,1)S(1)} %pad_maximum_fusion.refs_5_.refs_0_, bf16[336,2560]{1,0:T(8,128)(2,1)S(1)} %collective-permute-done.refs_1_, bf16[240,2560]{1,0:T(8,128)(2,1)S(1)} %pad_maximum_fusion.1.refs_6_.refs_2_, ...), custom_call_target="tpu_custom_call" | custom-call | flops 566231040 | bytes 7249920 | tf_op jit(solution)/shard_map/pallas_call | solution.py:71
  142.0 3.3 %collective-permute-done.35.refs_10_ = bf16[16,5504]{1,0:T(8,128)(2,1)S(1)} collective-permute-done((bf16[16,5504]{1,0:T(8,128)(2,1)S(1)}, bf16[16,5504]{1,0:T(8,128)(2,1)S(1)}, u32[]{:S(2)}, u32[]{:S(2)}) %collective-permute-start.35) | collective-permute-done | bytes 176160 | tf_op jit(solution)/shard_map/ppermute | solution.py:59
  145.4 2.0 %shard_map.107 = (bf16[16,5504]{1,0:T(8,128)(2,1)S(1)}, bf16[16,5504]{1,0:T(8,128)(2,1)S(1)}, bf16[16,5504]{1,0:T(8,128)(2,1)S(1)}) custom-call(bf16[336,2560]{1,0:T(8,128)(2,1)S(1)} %pad_maximum_fusion.refs_5_.refs_0_, bf16[336,2560]{1,0:T(8,128)(2,1)S(1)} %collective-permute-done.refs_1_, bf16[240,2560]{1,0:T(8,128)(2,1)S(1)} %pad_maximum_fusion.1.refs_6_.refs_2_, ...), custom_call_target="tpu_custom_call" | custom-call | flops 566231040 | bytes 7249920 | tf_op jit(solution)/shard_map/pallas_call | solution.py:71
  147.7 1.7 %collective-permute-start.37 = (bf16[16,5504]{1,0:T(8,128)(2,1)S(1)}, bf16[16,5504]{1,0:T(8,128)(2,1)S(1)}, u32[]{:S(2)}, u32[]{:S(2)}) collective-permute-start(bf16[16,5504]{1,0:T(8,128)(2,1)S(1)} %get-tuple-element.196), channel_id=1, source_target_pairs={{0,1},{1,0},{2,3},{3,2},{4,5},{5,4},{6,7},{7,6},{8,9},{9,8},{10,11... | collective-permute-start | bytes 528392 | tf_op jit(solution)/shard_map/ppermute | solution.py:59
  150.3 2.6 %collective-permute-done.36 = bf16[16,5504]{1,0:T(8,128)(2,1)S(1)} collective-permute-done((bf16[16,5504]{1,0:T(8,128)(2,1)S(1)}, bf16[16,5504]{1,0:T(8,128)(2,1)S(1)}, u32[]{:S(2)}, u32[]{:S(2)}) %collective-permute-start.36) | collective-permute-done | bytes 176160 | tf_op jit(solution)/shard_map/ppermute | solution.py:59
  153.2 2.5 %collective-permute-start.40 = (bf16[16,5504]{1,0:T(8,128)(2,1)S(1)}, bf16[16,5504]{1,0:T(8,128)(2,1)S(1)}, u32[]{:S(2)}, u32[]{:S(2)}) collective-permute-start(bf16[16,5504]{1,0:T(8,128)(2,1)S(1)} %add_convert_fusion), channel_id=1, source_target_pairs={{0,4},{1,5},{2,6},{3,7},{4,0},{5,1},{6,2},{7,3},{8,12},{9,13},{10,... | collective-permute-start | bytes 528392 | tf_op jit(solution)/shard_map/ppermute | solution.py:59
  156.0 1.2 collective-permute-start.39
  157.2 1.7 %collective-permute-start.41 = (bf16[16,5504]{1,0:T(8,128)(2,1)S(1)}, bf16[16,5504]{1,0:T(8,128)(2,1)S(1)}, u32[]{:S(2)}, u32[]{:S(2)}) collective-permute-start(bf16[16,5504]{1,0:T(8,128)(2,1)S(1)} %get-tuple-element.201.refs_11_), channel_id=1, source_target_pairs={{0,2},{1,3},{2,0},{3,1},{4,6},{5,7},{6,4},{7,5},{8,10},{9,11},{10,... | collective-permute-start | bytes 528392 | tf_op jit(solution)/shard_map/ppermute | solution.py:59
  159.8 1.2 collective-permute-done.40
  161.0 3.0 %collective-permute-done.38.refs_3_ = bf16[16,5504]{1,0:T(8,128)(2,1)S(1)} collective-permute-done((bf16[16,5504]{1,0:T(8,128)(2,1)S(1)}, bf16[16,5504]{1,0:T(8,128)(2,1)S(1)}, u32[]{:S(2)}, u32[]{:S(2)}) %collective-permute-start.38) | collective-permute-done | bytes 176160 | tf_op jit(solution)/shard_map/ppermute | solution.py:59
  164.0 1.1 shard_map.108
  166.0 1.3 shard_map.109
  (80 shorter events, 25.0 us)
Async XLA Ops:
  3.1 45.2 %collective-permute-start = (bf16[336,2560]{1,0:T(8,128)(2,1)S(1)}, bf16[336,2560]{1,0:T(8,128)(2,1)S(1)}, u32[]{:S(2)}, u32[]{:S(2)}) collective-permute-start(bf16[336,2560]{1,0:T(8,128)(2,1)S(1)} %pad_maximum_fusion.refs_5_.refs_0_), channel_id=1, source_target_pairs={{0,1},{1,0},{2,3},{3,2},{4,5},{5,4},{6,7},{7,6},{8,9},{9,8},{10,11... | collective-permute-start | bytes 5160968 | tf_op jit(solution)/shard_map/ppermute | solution.py:59
  7.2 2.9 %copy-start = (bf16[1,64,2560]{2,1,0:T(8,128)(2,1)S(1)}, bf16[1,64,2560]{2,1,0:T(8,128)(2,1)}, u32[]{:S(2)}) copy-start(bf16[1,64,2560]{2,1,0:T(8,128)(2,1)} %param.15) | copy-start | bytes 983044
  7.2 2.9 %copy-start.1 = (bf16[1,64,2560]{2,1,0:T(8,128)(2,1)S(1)}, bf16[1,64,2560]{2,1,0:T(8,128)(2,1)}, u32[]{:S(2)}) copy-start(bf16[1,64,2560]{2,1,0:T(8,128)(2,1)} %param.8) | copy-start | bytes 983044
  7.2 2.9 %copy-start.2 = (f32[1,2560]{1,0:T(1,128)S(1)}, f32[1,2560]{1,0:T(1,128)}, u32[]{:S(2)}) copy-start(f32[1,2560]{1,0:T(1,128)} %refs_3_.3) | copy-start | bytes 30724
  7.2 2.9 %copy-start.3 = (s32[1,2,64,1]{2,3,1,0:T(1,128)S(1)}, s32[1,2,64,1]{2,3,1,0:T(1,128)}, u32[]{:S(2)}) copy-start(s32[1,2,64,1]{2,3,1,0:T(1,128)} %param.13) | copy-start | bytes 1540
  7.2 2.9 %copy-start.4 = (f32[1,2,64,1]{2,3,1,0:T(1,128)S(1)}, f32[1,2,64,1]{2,3,1,0:T(1,128)}, u32[]{:S(2)}) copy-start(f32[1,2,64,1]{2,3,1,0:T(1,128)} %param.14) | copy-start | bytes 1540
  8.4 39.9 %collective-permute-start.1 = (bf16[240,2560]{1,0:T(8,128)(2,1)S(1)}, bf16[240,2560]{1,0:T(8,128)(2,1)S(1)}, u32[]{:S(2)}, u32[]{:S(2)}) collective-permute-start(bf16[240,2560]{1,0:T(8,128)(2,1)S(1)} %pad_maximum_fusion.1.refs_6_.refs_2_), channel_id=1, source_target_pairs={{0,2},{1,3},{2,0},{3,1},{4,6},{5,7},{6,4},{7,5},{8,10},{9,11},{10,... | collective-permute-start | bytes 3686408 | tf_op jit(solution)/shard_map/ppermute | solution.py:59
  10.9 37.3 %collective-permute-start.2 = (bf16[32,5504]{1,0:T(8,128)(2,1)S(1)}, bf16[32,5504]{1,0:T(8,128)(2,1)S(1)}, u32[]{:S(2)}, u32[]{:S(2)}) collective-permute-start(bf16[32,5504]{1,0:T(8,128)(2,1)S(1)} %get-tuple-element.103), channel_id=1, source_target_pairs={{0,4},{1,5},{2,6},{3,7},{4,0},{5,1},{6,2},{7,3},{8,12},{9,13},{10,... | collective-permute-start | bytes 1056776 | tf_op jit(solution)/shard_map/ppermute | solution.py:59
  13.6 33.9 %collective-permute-start.4 = (bf16[16,5504]{1,0:T(8,128)(2,1)S(1)}, bf16[16,5504]{1,0:T(8,128)(2,1)S(1)}, u32[]{:S(2)}, u32[]{:S(2)}) collective-permute-start(bf16[16,5504]{1,0:T(8,128)(2,1)S(1)} %get-tuple-element.124.refs_5_), channel_id=1, source_target_pairs={{0,1},{1,0},{2,3},{3,2},{4,5},{5,4},{6,7},{7,6},{8,9},{9,8},{10,11... | collective-permute-start | bytes 528392 | tf_op jit(solution)/shard_map/ppermute | solution.py:59
  14.1 34.2 %collective-permute-start.3 = (bf16[16,5504]{1,0:T(8,128)(2,1)S(1)}, bf16[16,5504]{1,0:T(8,128)(2,1)S(1)}, u32[]{:S(2)}, u32[]{:S(2)}) collective-permute-start(bf16[16,5504]{1,0:T(8,128)(2,1)S(1)} %get-tuple-element.124.refs_5_), channel_id=1, source_target_pairs={{0,2},{1,3},{2,0},{3,1},{4,6},{5,7},{6,4},{7,5},{8,10},{9,11},{10,... | collective-permute-start | bytes 528392 | tf_op jit(solution)/shard_map/ppermute | solution.py:59
  48.3 5.5 %collective-permute-start.6 = (bf16[16,5504]{1,0:T(8,128)(2,1)S(1)}, bf16[16,5504]{1,0:T(8,128)(2,1)S(1)}, u32[]{:S(2)}, u32[]{:S(2)}) collective-permute-start(bf16[16,5504]{1,0:T(8,128)(2,1)S(1)} %get-tuple-element.112.refs_5_), channel_id=1, source_target_pairs={{0,1},{1,0},{2,3},{3,2},{4,5},{5,4},{6,7},{7,6},{8,9},{9,8},{10,11... | collective-permute-start | bytes 528392 | tf_op jit(solution)/shard_map/ppermute | solution.py:59
  49.3 5.5 %collective-permute-start.5 = (bf16[16,5504]{1,0:T(8,128)(2,1)S(1)}, bf16[16,5504]{1,0:T(8,128)(2,1)S(1)}, u32[]{:S(2)}, u32[]{:S(2)}) collective-permute-start(bf16[16,5504]{1,0:T(8,128)(2,1)S(1)} %get-tuple-element.112.refs_5_), channel_id=1, source_target_pairs={{0,2},{1,3},{2,0},{3,1},{4,6},{5,7},{6,4},{7,5},{8,10},{9,11},{10,... | collective-permute-start | bytes 528392 | tf_op jit(solution)/shard_map/ppermute | solution.py:59
  57.2 7.3 %collective-permute-start.8 = (bf16[16,5504]{1,0:T(8,128)(2,1)S(1)}, bf16[16,5504]{1,0:T(8,128)(2,1)S(1)}, u32[]{:S(2)}, u32[]{:S(2)}) collective-permute-start(bf16[16,5504]{1,0:T(8,128)(2,1)S(1)} %get-tuple-element.121.refs_7_), channel_id=1, source_target_pairs={{0,2},{1,3},{2,0},{3,1},{4,6},{5,7},{6,4},{7,5},{8,10},{9,11},{10,... | collective-permute-start | bytes 528392 | tf_op jit(solution)/shard_map/ppermute | solution.py:59
  58.9 7.4 %collective-permute-start.9 = (bf16[16,5504]{1,0:T(8,128)(2,1)S(1)}, bf16[16,5504]{1,0:T(8,128)(2,1)S(1)}, u32[]{:S(2)}, u32[]{:S(2)}) collective-permute-start(bf16[16,5504]{1,0:T(8,128)(2,1)S(1)} %get-tuple-element.122), channel_id=1, source_target_pairs={{0,1},{1,0},{2,3},{3,2},{4,5},{5,4},{6,7},{7,6},{8,9},{9,8},{10,11... | collective-permute-start | bytes 528392 | tf_op jit(solution)/shard_map/ppermute | solution.py:59
  60.0 10.3 %collective-permute-start.12 = (bf16[32,5504]{1,0:T(8,128)(2,1)S(1)}, bf16[32,5504]{1,0:T(8,128)(2,1)S(1)}, u32[]{:S(2)}, u32[]{:S(2)}) collective-permute-start(bf16[32,5504]{1,0:T(8,128)(2,1)S(1)} %pad_maximum_fusion.2.refs_5_), channel_id=1, source_target_pairs={{0,1},{1,0},{2,3},{3,2},{4,5},{5,4},{6,7},{7,6},{8,9},{9,8},{10,11... | collective-permute-start | bytes 1056776 | tf_op jit(solution)/shard_map/ppermute | solution.py:59
  60.9 9.4 %collective-permute-start.11 = (bf16[32,5504]{1,0:T(8,128)(2,1)S(1)}, bf16[32,5504]{1,0:T(8,128)(2,1)S(1)}, u32[]{:S(2)}, u32[]{:S(2)}) collective-permute-start(bf16[32,5504]{1,0:T(8,128)(2,1)S(1)} %pad_maximum_fusion.2.refs_5_), channel_id=1, source_target_pairs={{0,2},{1,3},{2,0},{3,1},{4,6},{5,7},{6,4},{7,5},{8,10},{9,11},{10,... | collective-permute-start | bytes 1056776 | tf_op jit(solution)/shard_map/ppermute | solution.py:59
  61.3 17.3 %collective-permute-start.7 = (bf16[80,2560]{1,0:T(8,128)(2,1)S(1)}, bf16[80,2560]{1,0:T(8,128)(2,1)S(1)}, u32[]{:S(2)}, u32[]{:S(2)}) collective-permute-start(bf16[80,2560]{1,0:T(8,128)(2,1)S(1)} %get-tuple-element.118), channel_id=1, source_target_pairs={{0,8},{1,9},{2,10},{3,11},{4,12},{5,13},{6,14},{7,15},{8,16},{9,17... | collective-permute-start | bytes 1228808 | tf_op jit(solution)/shard_map/ppermute | solution.py:59
  66.3 12.3 %collective-permute-start.10 = (bf16[16,5504]{1,0:T(8,128)(2,1)S(1)}, bf16[16,5504]{1,0:T(8,128)(2,1)S(1)}, u32[]{:S(2)}, u32[]{:S(2)}) collective-permute-start(bf16[16,5504]{1,0:T(8,128)(2,1)S(1)} %add_convert_fusion.3), channel_id=1, source_target_pairs={{0,12},{1,13},{2,14},{3,15},{4,8},{5,9},{6,10},{7,11},{8,20},{9,21... | collective-permute-start | bytes 528392 | tf_op jit(solution)/shard_map/ppermute | solution.py:59
  70.3 9.5 %collective-permute-start.13 = (bf16[16,5504]{1,0:T(8,128)(2,1)S(1)}, bf16[16,5504]{1,0:T(8,128)(2,1)S(1)}, u32[]{:S(2)}, u32[]{:S(2)}) collective-permute-start(bf16[16,5504]{1,0:T(8,128)(2,1)S(1)} %get-tuple-element.130), channel_id=1, source_target_pairs={{0,10},{1,11},{2,8},{3,9},{4,14},{5,15},{6,12},{7,13},{8,18},{9,19... | collective-permute-start | bytes 528392 | tf_op jit(solution)/shard_map/ppermute | solution.py:59
  70.3 9.5 %collective-permute-start.14 = (bf16[16,5504]{1,0:T(8,128)(2,1)S(1)}, bf16[16,5504]{1,0:T(8,128)(2,1)S(1)}, u32[]{:S(2)}, u32[]{:S(2)}) collective-permute-start(bf16[16,5504]{1,0:T(8,128)(2,1)S(1)} %get-tuple-element.131), channel_id=1, source_target_pairs={{0,9},{1,8},{2,11},{3,10},{4,13},{5,12},{6,15},{7,14},{8,17},{9,16... | collective-permute-start | bytes 528392 | tf_op jit(solution)/shard_map/ppermute | solution.py:59
  72.3 8.7 %collective-permute-start.15 = (bf16[16,5504]{1,0:T(8,128)(2,1)S(1)}, bf16[16,5504]{1,0:T(8,128)(2,1)S(1)}, u32[]{:S(2)}, u32[]{:S(2)}) collective-permute-start(bf16[16,5504]{1,0:T(8,128)(2,1)S(1)} %get-tuple-element.132), channel_id=1, source_target_pairs={{0,8},{1,9},{2,10},{3,11},{4,12},{5,13},{6,14},{7,15},{8,16},{9,17... | collective-permute-start | bytes 528392 | tf_op jit(solution)/shard_map/ppermute | solution.py:59
  81.9 10.8 %collective-permute-start.17 = (bf16[16,5504]{1,0:T(8,128)(2,1)S(1)}, bf16[16,5504]{1,0:T(8,128)(2,1)S(1)}, u32[]{:S(2)}, u32[]{:S(2)}) collective-permute-start(bf16[16,5504]{1,0:T(8,128)(2,1)S(1)} %get-tuple-element.143), channel_id=1, source_target_pairs={{0,4},{1,5},{2,6},{3,7},{4,0},{5,1},{6,2},{7,3},{8,12},{9,13},{10,... | collective-permute-start | bytes 528392 | tf_op jit(solution)/shard_map/ppermute | solution.py:59
  83.8 8.9 %collective-permute-start.19 = (bf16[16,5504]{1,0:T(8,128)(2,1)S(1)}, bf16[16,5504]{1,0:T(8,128)(2,1)S(1)}, u32[]{:S(2)}, u32[]{:S(2)}) collective-permute-start(bf16[16,5504]{1,0:T(8,128)(2,1)S(1)} %get-tuple-element.144.refs_9_), channel_id=1, source_target_pairs={{0,1},{1,0},{2,3},{3,2},{4,5},{5,4},{6,7},{7,6},{8,9},{9,8},{10,11... | collective-permute-start | bytes 528392 | tf_op jit(solution)/shard_map/ppermute | solution.py:59
  84.3 9.1 %collective-permute-start.18 = (bf16[16,5504]{1,0:T(8,128)(2,1)S(1)}, bf16[16,5504]{1,0:T(8,128)(2,1)S(1)}, u32[]{:S(2)}, u32[]{:S(2)}) collective-permute-start(bf16[16,5504]{1,0:T(8,128)(2,1)S(1)} %get-tuple-element.144.refs_9_), channel_id=1, source_target_pairs={{0,2},{1,3},{2,0},{3,1},{4,6},{5,7},{6,4},{7,5},{8,10},{9,11},{10,... | collective-permute-start | bytes 528392 | tf_op jit(solution)/shard_map/ppermute | solution.py:59
  93.4 5.7 %collective-permute-start.21 = (bf16[16,5504]{1,0:T(8,128)(2,1)S(1)}, bf16[16,5504]{1,0:T(8,128)(2,1)S(1)}, u32[]{:S(2)}, u32[]{:S(2)}) collective-permute-start(bf16[16,5504]{1,0:T(8,128)(2,1)S(1)} %collective-permute-done.17.refs_9_), channel_id=1, source_target_pairs={{0,1},{1,0},{2,3},{3,2},{4,5},{5,4},{6,7},{7,6},{8,9},{9,8},{10,11... | collective-permute-start | bytes 528392 | tf_op jit(solution)/shard_map/ppermute | solution.py:59
  94.4 5.5 %collective-permute-start.20 = (bf16[16,5504]{1,0:T(8,128)(2,1)S(1)}, bf16[16,5504]{1,0:T(8,128)(2,1)S(1)}, u32[]{:S(2)}, u32[]{:S(2)}) collective-permute-start(bf16[16,5504]{1,0:T(8,128)(2,1)S(1)} %collective-permute-done.17.refs_9_), channel_id=1, source_target_pairs={{0,2},{1,3},{2,0},{3,1},{4,6},{5,7},{6,4},{7,5},{8,10},{9,11},{10,... | collective-permute-start | bytes 528392 | tf_op jit(solution)/shard_map/ppermute | solution.py:59
  102.5 5.5 %collective-permute-start.22 = (bf16[16,5504]{1,0:T(8,128)(2,1)S(1)}, bf16[16,5504]{1,0:T(8,128)(2,1)S(1)}, u32[]{:S(2)}, u32[]{:S(2)}) collective-permute-start(bf16[16,5504]{1,0:T(8,128)(2,1)S(1)} %get-tuple-element.154), channel_id=1, source_target_pairs={{0,2},{1,3},{2,0},{3,1},{4,6},{5,7},{6,4},{7,5},{8,10},{9,11},{10,... | collective-permute-start | bytes 528392 | tf_op jit(solution)/shard_map/ppermute | solution.py:59
  103.5 5.5 %collective-permute-start.23 = (bf16[16,5504]{1,0:T(8,128)(2,1)S(1)}, bf16[16,5504]{1,0:T(8,128)(2,1)S(1)}, u32[]{:S(2)}, u32[]{:S(2)}) collective-permute-start(bf16[16,5504]{1,0:T(8,128)(2,1)S(1)} %get-tuple-element.155), channel_id=1, source_target_pairs={{0,1},{1,0},{2,3},{3,2},{4,5},{5,4},{6,7},{7,6},{8,9},{9,8},{10,11... | collective-permute-start | bytes 528392 | tf_op jit(solution)/shard_map/ppermute | solution.py:59
  104.6 16.5 %collective-permute-start.16 = (bf16[144,2560]{1,0:T(8,128)(2,1)S(1)}, bf16[144,2560]{1,0:T(8,128)(2,1)S(1)}, u32[]{:S(2)}, u32[]{:S(2)}) collective-permute-start(bf16[144,2560]{1,0:T(8,128)(2,1)S(1)} %get-tuple-element.134), channel_id=1, source_target_pairs={{0,24},{1,25},{2,26},{3,27},{4,28},{5,29},{6,30},{7,31},{8,0},{9,1... | collective-permute-start | bytes 2211848 | tf_op jit(solution)/shard_map/ppermute | solution.py:59
  105.4 6.9 %collective-permute-start.25 = (bf16[16,5504]{1,0:T(8,128)(2,1)S(1)}, bf16[16,5504]{1,0:T(8,128)(2,1)S(1)}, u32[]{:S(2)}, u32[]{:S(2)}) collective-permute-start(bf16[16,5504]{1,0:T(8,128)(2,1)S(1)} %get-tuple-element.161), channel_id=1, source_target_pairs={{0,2},{1,3},{2,0},{3,1},{4,6},{5,7},{6,4},{7,5},{8,10},{9,11},{10,... | collective-permute-start | bytes 528392 | tf_op jit(solution)/shard_map/ppermute | solution.py:59
  106.5 6.6 %collective-permute-start.26 = (bf16[16,5504]{1,0:T(8,128)(2,1)S(1)}, bf16[16,5504]{1,0:T(8,128)(2,1)S(1)}, u32[]{:S(2)}, u32[]{:S(2)}) collective-permute-start(bf16[16,5504]{1,0:T(8,128)(2,1)S(1)} %get-tuple-element.162), channel_id=1, source_target_pairs={{0,1},{1,0},{2,3},{3,2},{4,5},{5,4},{6,7},{7,6},{8,9},{9,8},{10,11... | collective-permute-start | bytes 528392 | tf_op jit(solution)/shard_map/ppermute | solution.py:59
  109.1 11.5 %collective-permute-start.24 = (bf16[16,5504]{1,0:T(8,128)(2,1)S(1)}, bf16[16,5504]{1,0:T(8,128)(2,1)S(1)}, u32[]{:S(2)}, u32[]{:S(2)}) collective-permute-start(bf16[16,5504]{1,0:T(8,128)(2,1)S(1)} %add_convert_fusion.2), channel_id=1, source_target_pairs={{0,28},{1,29},{2,30},{3,31},{4,24},{5,25},{6,26},{7,27},{8,4},{9,5... | collective-permute-start | bytes 528392 | tf_op jit(solution)/shard_map/ppermute | solution.py:59
  109.5 11.1 %collective-permute-start.27 = (bf16[16,5504]{1,0:T(8,128)(2,1)S(1)}, bf16[16,5504]{1,0:T(8,128)(2,1)S(1)}, u32[]{:S(2)}, u32[]{:S(2)}) collective-permute-start(bf16[16,5504]{1,0:T(8,128)(2,1)S(1)} %get-tuple-element.166.refs_11_), channel_id=1, source_target_pairs={{0,26},{1,27},{2,24},{3,25},{4,30},{5,31},{6,28},{7,29},{8,2},{9,3... | collective-permute-start | bytes 528392 | tf_op jit(solution)/shard_map/ppermute | solution.py:59
  112.4 8.2 %collective-permute-start.28 = (bf16[16,5504]{1,0:T(8,128)(2,1)S(1)}, bf16[16,5504]{1,0:T(8,128)(2,1)S(1)}, u32[]{:S(2)}, u32[]{:S(2)}) collective-permute-start(bf16[16,5504]{1,0:T(8,128)(2,1)S(1)} %get-tuple-element.167), channel_id=1, source_target_pairs={{0,25},{1,24},{2,27},{3,26},{4,29},{5,28},{6,31},{7,30},{8,1},{9,0... | collective-permute-start | bytes 528392 | tf_op jit(solution)/shard_map/ppermute | solution.py:59
  113.1 8.0 %collective-permute-start.29 = (bf16[16,5504]{1,0:T(8,128)(2,1)S(1)}, bf16[16,5504]{1,0:T(8,128)(2,1)S(1)}, u32[]{:S(2)}, u32[]{:S(2)}) collective-permute-start(bf16[16,5504]{1,0:T(8,128)(2,1)S(1)} %get-tuple-element.168), channel_id=1, source_target_pairs={{0,24},{1,25},{2,26},{3,27},{4,28},{5,29},{6,30},{7,31},{8,0},{9,1... | collective-permute-start | bytes 528392 | tf_op jit(solution)/shard_map/ppermute | solution.py:59
  120.6 14.2 %collective-permute-start.33 = (bf16[16,5504]{1,0:T(8,128)(2,1)S(1)}, bf16[16,5504]{1,0:T(8,128)(2,1)S(1)}, u32[]{:S(2)}, u32[]{:S(2)}) collective-permute-start(bf16[16,5504]{1,0:T(8,128)(2,1)S(1)} %add_convert_fusion.1), channel_id=1, source_target_pairs={{0,4},{1,5},{2,6},{3,7},{4,0},{5,1},{6,2},{7,3},{8,12},{9,13},{10,... | collective-permute-start | bytes 528392 | tf_op jit(solution)/shard_map/ppermute | solution.py:59
  122.1 16.4 %collective-permute-start.30 = (bf16[16,5504]{1,0:T(8,128)(2,1)S(1)}, bf16[16,5504]{1,0:T(8,128)(2,1)S(1)}, u32[]{:S(2)}, u32[]{:S(2)}) collective-permute-start(bf16[16,5504]{1,0:T(8,128)(2,1)S(1)} %get-tuple-element.169), channel_id=1, source_target_pairs={{0,4},{1,5},{2,6},{3,7},{4,0},{5,1},{6,2},{7,3},{8,12},{9,13},{10,... | collective-permute-start | bytes 528392 | tf_op jit(solution)/shard_map/ppermute | solution.py:59
  124.5 14.0 %collective-permute-start.32 = (bf16[16,5504]{1,0:T(8,128)(2,1)S(1)}, bf16[16,5504]{1,0:T(8,128)(2,1)S(1)}, u32[]{:S(2)}, u32[]{:S(2)}) collective-permute-start(bf16[16,5504]{1,0:T(8,128)(2,1)S(1)} %get-tuple-element.170.refs_9_), channel_id=1, source_target_pairs={{0,1},{1,0},{2,3},{3,2},{4,5},{5,4},{6,7},{7,6},{8,9},{9,8},{10,11... | collective-permute-start | bytes 528392 | tf_op jit(solution)/shard_map/ppermute | solution.py:59
  125.4 14.1 %collective-permute-start.31 = (bf16[16,5504]{1,0:T(8,128)(2,1)S(1)}, bf16[16,5504]{1,0:T(8,128)(2,1)S(1)}, u32[]{:S(2)}, u32[]{:S(2)}) collective-permute-start(bf16[16,5504]{1,0:T(8,128)(2,1)S(1)} %get-tuple-element.170.refs_9_), channel_id=1, source_target_pairs={{0,2},{1,3},{2,0},{3,1},{4,6},{5,7},{6,4},{7,5},{8,10},{9,11},{10,... | collective-permute-start | bytes 528392 | tf_op jit(solution)/shard_map/ppermute | solution.py:59
  139.5 5.9 %collective-permute-start.35 = (bf16[16,5504]{1,0:T(8,128)(2,1)S(1)}, bf16[16,5504]{1,0:T(8,128)(2,1)S(1)}, u32[]{:S(2)}, u32[]{:S(2)}) collective-permute-start(bf16[16,5504]{1,0:T(8,128)(2,1)S(1)} %collective-permute-done.30.refs_9_), channel_id=1, source_target_pairs={{0,1},{1,0},{2,3},{3,2},{4,5},{5,4},{6,7},{7,6},{8,9},{9,8},{10,11... | collective-permute-start | bytes 528392 | tf_op jit(solution)/shard_map/ppermute | solution.py:59
  140.0 5.5 %collective-permute-start.34 = (bf16[16,5504]{1,0:T(8,128)(2,1)S(1)}, bf16[16,5504]{1,0:T(8,128)(2,1)S(1)}, u32[]{:S(2)}, u32[]{:S(2)}) collective-permute-start(bf16[16,5504]{1,0:T(8,128)(2,1)S(1)} %collective-permute-done.30.refs_9_), channel_id=1, source_target_pairs={{0,2},{1,3},{2,0},{3,1},{4,6},{5,7},{6,4},{7,5},{8,10},{9,11},{10,... | collective-permute-start | bytes 528392 | tf_op jit(solution)/shard_map/ppermute | solution.py:59
  147.4 5.5 %collective-permute-start.36 = (bf16[16,5504]{1,0:T(8,128)(2,1)S(1)}, bf16[16,5504]{1,0:T(8,128)(2,1)S(1)}, u32[]{:S(2)}, u32[]{:S(2)}) collective-permute-start(bf16[16,5504]{1,0:T(8,128)(2,1)S(1)} %get-tuple-element.195), channel_id=1, source_target_pairs={{0,2},{1,3},{2,0},{3,1},{4,6},{5,7},{6,4},{7,5},{8,10},{9,11},{10,... | collective-permute-start | bytes 528392 | tf_op jit(solution)/shard_map/ppermute | solution.py:59
  147.7 5.5 %collective-permute-start.37 = (bf16[16,5504]{1,0:T(8,128)(2,1)S(1)}, bf16[16,5504]{1,0:T(8,128)(2,1)S(1)}, u32[]{:S(2)}, u32[]{:S(2)}) collective-permute-start(bf16[16,5504]{1,0:T(8,128)(2,1)S(1)} %get-tuple-element.196), channel_id=1, source_target_pairs={{0,1},{1,0},{2,3},{3,2},{4,5},{5,4},{6,7},{7,6},{8,9},{9,8},{10,11... | collective-permute-start | bytes 528392 | tf_op jit(solution)/shard_map/ppermute | solution.py:59
  153.2 7.8 %collective-permute-start.40 = (bf16[16,5504]{1,0:T(8,128)(2,1)S(1)}, bf16[16,5504]{1,0:T(8,128)(2,1)S(1)}, u32[]{:S(2)}, u32[]{:S(2)}) collective-permute-start(bf16[16,5504]{1,0:T(8,128)(2,1)S(1)} %add_convert_fusion), channel_id=1, source_target_pairs={{0,4},{1,5},{2,6},{3,7},{4,0},{5,1},{6,2},{7,3},{8,12},{9,13},{10,... | collective-permute-start | bytes 528392 | tf_op jit(solution)/shard_map/ppermute | solution.py:59
  155.7 8.3 %collective-permute-start.38 = (bf16[16,5504]{1,0:T(8,128)(2,1)S(1)}, bf16[16,5504]{1,0:T(8,128)(2,1)S(1)}, u32[]{:S(2)}, u32[]{:S(2)}) collective-permute-start(bf16[16,5504]{1,0:T(8,128)(2,1)S(1)} %get-tuple-element.197), channel_id=1, source_target_pairs={{0,2},{1,3},{2,0},{3,1},{4,6},{5,7},{6,4},{7,5},{8,10},{9,11},{10,... | collective-permute-start | bytes 528392 | tf_op jit(solution)/shard_map/ppermute | solution.py:59
  156.0 8.0 %collective-permute-start.39 = (bf16[16,5504]{1,0:T(8,128)(2,1)S(1)}, bf16[16,5504]{1,0:T(8,128)(2,1)S(1)}, u32[]{:S(2)}, u32[]{:S(2)}) collective-permute-start(bf16[16,5504]{1,0:T(8,128)(2,1)S(1)} %get-tuple-element.198), channel_id=1, source_target_pairs={{0,1},{1,0},{2,3},{3,2},{4,5},{5,4},{6,7},{7,6},{8,9},{9,8},{10,11... | collective-permute-start | bytes 528392 | tf_op jit(solution)/shard_map/ppermute | solution.py:59
  157.2 8.8 %collective-permute-start.41 = (bf16[16,5504]{1,0:T(8,128)(2,1)S(1)}, bf16[16,5504]{1,0:T(8,128)(2,1)S(1)}, u32[]{:S(2)}, u32[]{:S(2)}) collective-permute-start(bf16[16,5504]{1,0:T(8,128)(2,1)S(1)} %get-tuple-element.201.refs_11_), channel_id=1, source_target_pairs={{0,2},{1,3},{2,0},{3,1},{4,6},{5,7},{6,4},{7,5},{8,10},{9,11},{10,... | collective-permute-start | bytes 528392 | tf_op jit(solution)/shard_map/ppermute | solution.py:59
  158.9 7.0 %collective-permute-start.42 = (bf16[16,5504]{1,0:T(8,128)(2,1)S(1)}, bf16[16,5504]{1,0:T(8,128)(2,1)S(1)}, u32[]{:S(2)}, u32[]{:S(2)}) collective-permute-start(bf16[16,5504]{1,0:T(8,128)(2,1)S(1)} %get-tuple-element.202), channel_id=1, source_target_pairs={{0,1},{1,0},{2,3},{3,2},{4,5},{5,4},{6,7},{7,6},{8,9},{9,8},{10,11... | collective-permute-start | bytes 528392 | tf_op jit(solution)/shard_map/ppermute | solution.py:59
  (1 other events, 2.3 us)

commit v5 on v4

--- a/solution.py
+++ b/solution.py
@@ -599,6 +599,7 @@
         *fin_back,
         *fin_own,
         scratch=[picked],
+        after=[g0],
     )
     return (final[None], g0[None])
 

time: 168 us -> 168 us (level)
  transfers between devices with their start and end apart: 43 -> 43, of which waited for: 29 -> 28; matrix products, arithmetic and copies ran while one was open for 1% -> 1% of each run, Pallas kernels for 8% -> 8%
where the time goes in v5:
time: 168 us
  waiting for transfers between devices  91.9 us (55%)
  starting transfers between devices  46.2 us (28%)
  Pallas kernels  23 us (14%)
  local copies, waits for them, and re-layouts  5.5 us (3%)
    ppermute x43, waiting for transfers between devices, shift(): return lax.ppermute(value, ('section', 'expert'), pairs)  91.9 us
    ppermute x43, starting transfers between devices, shift(): return lax.ppermute(value, ('section', 'expert'), pairs)  46.2 us
    pallas_call x15, Pallas kernels, call(): pl.pallas_call(reading, out_shape=list(outs), in_specs=[vmem] * read + [p...  23 us
  transfers between devices with their start and end apart: 43, of which 28 were waited for; matrix products, arithmetic and copies ran while one was open for 1% of the time, Pallas kernels for 8%

profile of v5, /device:TPU:0, one launch (start us, length us, event | category | flops | bytes accessed | tf_op | source)
XLA Modules:
  0.0 168.0 jit_solution(13917201076205321281)
XLA Ops:
  0.6 1.2 slice.40
  1.8 1.1 slice.41
  3.1 3.0 %collective-permute-start = (bf16[336,2560]{1,0:T(8,128)(2,1)S(1)}, bf16[336,2560]{1,0:T(8,128)(2,1)S(1)}, u32[]{:S(2)}, u32[]{:S(2)}) collective-permute-start(bf16[336,2560]{1,0:T(8,128)(2,1)S(1)} %pad_maximum_fusion.refs_5_.refs_0_), channel_id=1, source_target_pairs={{0,1},{1,0},{2,3},{3,2},{4,5},{5,4},{6,7},{7,6},{8,9},{9,8},{10,11... | collective-permute-start | bytes 5160968 | tf_op jit(solution)/shard_map/ppermute | solution.py:59
  6.1 1.0 slice.42
  7.2 1.1 slice.43
  8.4 1.6 collective-permute-start.1
  10.9 2.6 %collective-permute-start.2 = (bf16[32,5504]{1,0:T(8,128)(2,1)S(1)}, bf16[32,5504]{1,0:T(8,128)(2,1)S(1)}, u32[]{:S(2)}, u32[]{:S(2)}) collective-permute-start(bf16[32,5504]{1,0:T(8,128)(2,1)S(1)} %get-tuple-element.103), channel_id=1, source_target_pairs={{0,4},{1,5},{2,6},{3,7},{4,0},{5,1},{6,2},{7,3},{8,12},{9,13},{10,... | collective-permute-start | bytes 1056776 | tf_op jit(solution)/shard_map/ppermute | solution.py:59
  14.5 32.9 %collective-permute-done.4.refs_6_ = bf16[16,5504]{1,0:T(8,128)(2,1)S(1)} collective-permute-done((bf16[16,5504]{1,0:T(8,128)(2,1)S(1)}, bf16[16,5504]{1,0:T(8,128)(2,1)S(1)}, u32[]{:S(2)}, u32[]{:S(2)}) %collective-permute-start.4) | collective-permute-done | bytes 176160 | tf_op jit(solution)/shard_map/ppermute | solution.py:59
  49.3 1.6 collective-permute-start.5
  50.9 2.9 %collective-permute-done.6.refs_6_ = bf16[16,5504]{1,0:T(8,128)(2,1)S(1)} collective-permute-done((bf16[16,5504]{1,0:T(8,128)(2,1)S(1)}, bf16[16,5504]{1,0:T(8,128)(2,1)S(1)}, u32[]{:S(2)}, u32[]{:S(2)}) %collective-permute-start.6) | collective-permute-done | bytes 176160 | tf_op jit(solution)/shard_map/ppermute | solution.py:59
  54.8 2.5 %shard_map.96 = (bf16[16,5504]{1,0:T(8,128)(2,1)S(1)}, bf16[16,5504]{1,0:T(8,128)(2,1)S(1)}, bf16[16,5504]{1,0:T(8,128)(2,1)S(1)}, f32[96,224]{1,0:T(8,128)S(1)}...) custom-call(bf16[336,2560]{1,0:T(8,128)(2,1)S(1)} %pad_maximum_fusion.refs_5_.refs_0_, ...), custom_call_target="tpu_custom_call" | custom-call | flops 566231040 | bytes 7249920 | tf_op jit(solution)/shard_map/pallas_call | solution.py:71
  57.2 1.6 collective-permute-start.8
  58.9 1.1 collective-permute-start.9
  61.3 2.5 %shard_map.97 = (bf16[16,5504]{1,0:T(8,128)(2,1)S(1)}, bf16[16,5504]{1,0:T(8,128)(2,1)S(1)}, bf16[16,5504]{1,0:T(8,128)(2,1)S(1)}, f32[96,224]{1,0:T(8,128)S(1)}...) custom-call(bf16[336,2560]{1,0:T(8,128)(2,1)S(1)} %pad_maximum_fusion.refs_5_.refs_0_, ...), custom_call_target="tpu_custom_call" | custom-call | flops 566231040 | bytes 7249920 | tf_op jit(solution)/shard_map/pallas_call | solution.py:71
  64.5 1.7 %collective-permute-done.9 = bf16[16,5504]{1,0:T(8,128)(2,1)S(1)} collective-permute-done((bf16[16,5504]{1,0:T(8,128)(2,1)S(1)}, bf16[16,5504]{1,0:T(8,128)(2,1)S(1)}, u32[]{:S(2)}, u32[]{:S(2)}) %collective-permute-start.9) | collective-permute-done | bytes 176160 | tf_op jit(solution)/shard_map/ppermute | solution.py:59
  66.3 1.5 collective-permute-start.10
  67.8 2.5 %collective-permute-done.12.refs_6_ = bf16[32,5504]{1,0:T(8,128)(2,1)S(1)} collective-permute-done((bf16[32,5504]{1,0:T(8,128)(2,1)S(1)}, bf16[32,5504]{1,0:T(8,128)(2,1)S(1)}, u32[]{:S(2)}, u32[]{:S(2)}) %collective-permute-start.12) | collective-permute-done | bytes 352288 | tf_op jit(solution)/shard_map/ppermute | solution.py:59
  70.3 1.9 %collective-permute-start.14 = (bf16[16,5504]{1,0:T(8,128)(2,1)S(1)}, bf16[16,5504]{1,0:T(8,128)(2,1)S(1)}, u32[]{:S(2)}, u32[]{:S(2)}) collective-permute-start(bf16[16,5504]{1,0:T(8,128)(2,1)S(1)} %get-tuple-element.131), channel_id=1, source_target_pairs={{0,9},{1,8},{2,11},{3,10},{4,13},{5,12},{6,15},{7,14},{8,17},{9,16... | collective-permute-start | bytes 528392 | tf_op jit(solution)/shard_map/ppermute | solution.py:59
  72.3 6.4 %collective-permute-done.10.refs_4_ = bf16[16,5504]{1,0:T(8,128)(2,1)S(1)} collective-permute-done((bf16[16,5504]{1,0:T(8,128)(2,1)S(1)}, bf16[16,5504]{1,0:T(8,128)(2,1)S(1)}, u32[]{:S(2)}, u32[]{:S(2)}) %collective-permute-start.10) | collective-permute-done | bytes 176160 | tf_op jit(solution)/shard_map/ppermute | solution.py:59
  78.6 1.2 collective-permute-done.13.refs_5_
  79.8 1.1 collective-permute-done.15.refs_7_
  81.9 1.9 %collective-permute-start.17 = (bf16[16,5504]{1,0:T(8,128)(2,1)S(1)}, bf16[16,5504]{1,0:T(8,128)(2,1)S(1)}, u32[]{:S(2)}, u32[]{:S(2)}) collective-permute-start(bf16[16,5504]{1,0:T(8,128)(2,1)S(1)} %get-tuple-element.143), channel_id=1, source_target_pairs={{0,4},{1,5},{2,6},{3,7},{4,0},{5,1},{6,2},{7,3},{8,12},{9,13},{10,... | collective-permute-start | bytes 528392 | tf_op jit(solution)/shard_map/ppermute | solution.py:59
  84.3 2.5 %collective-permute-start.18 = (bf16[16,5504]{1,0:T(8,128)(2,1)S(1)}, bf16[16,5504]{1,0:T(8,128)(2,1)S(1)}, u32[]{:S(2)}, u32[]{:S(2)}) collective-permute-start(bf16[16,5504]{1,0:T(8,128)(2,1)S(1)} %get-tuple-element.144.refs_9_), channel_id=1, source_target_pairs={{0,2},{1,3},{2,0},{3,1},{4,6},{5,7},{6,4},{7,5},{8,10},{9,11},{10,... | collective-permute-start | bytes 528392 | tf_op jit(solution)/shard_map/ppermute | solution.py:59
  86.8 5.8 %collective-permute-done.17.refs_9_ = bf16[16,5504]{1,0:T(8,128)(2,1)S(1)} collective-permute-done((bf16[16,5504]{1,0:T(8,128)(2,1)S(1)}, bf16[16,5504]{1,0:T(8,128)(2,1)S(1)}, u32[]{:S(2)}, u32[]{:S(2)}) %collective-permute-start.17) | collective-permute-done | bytes 176160 | tf_op jit(solution)/shard_map/ppermute | solution.py:59
  96.4 2.7 %shard_map.101 = (bf16[16,5504]{1,0:T(8,128)(2,1)S(1)}, bf16[16,5504]{1,0:T(8,128)(2,1)S(1)}, bf16[16,5504]{1,0:T(8,128)(2,1)S(1)}, f32[96,224]{1,0:T(8,128)S(1)...) custom-call(bf16[336,2560]{1,0:T(8,128)(2,1)S(1)} %pad_maximum_fusion.refs_5_.refs_0_, ...), custom_call_target="tpu_custom_call" | custom-call | flops 566231040 | bytes 7397376 | tf_op jit(solution)/shard_map/pallas_call | solution.py:71
  99.8 2.6 %shard_map.102 = (bf16[16,5504]{1,0:T(8,128)(2,1)S(1)}, bf16[16,5504]{1,0:T(8,128)(2,1)S(1)}, bf16[16,5504]{1,0:T(8,128)(2,1)S(1)}, f32[96,224]{1,0:T(8,128)S(1)...) custom-call(bf16[336,2560]{1,0:T(8,128)(2,1)S(1)} %pad_maximum_fusion.refs_5_.refs_0_, ...), custom_call_target="tpu_custom_call" | custom-call | flops 566231040 | bytes 7397376 | tf_op jit(solution)/shard_map/pallas_call | solution.py:71
  102.5 1.0 collective-permute-start.22
  103.5 1.0 collective-permute-start.23
  105.4 1.0 collective-permute-start.25
  108.0 1.0 collective-permute-done.23
  109.5 2.7 %collective-permute-start.27 = (bf16[16,5504]{1,0:T(8,128)(2,1)S(1)}, bf16[16,5504]{1,0:T(8,128)(2,1)S(1)}, u32[]{:S(2)}, u32[]{:S(2)}) collective-permute-start(bf16[16,5504]{1,0:T(8,128)(2,1)S(1)} %get-tuple-element.166.refs_11_), channel_id=1, source_target_pairs={{0,26},{1,27},{2,24},{3,25},{4,30},{5,31},{6,28},{7,29},{8,2},{9,3... | collective-permute-start | bytes 528392 | tf_op jit(solution)/shard_map/ppermute | solution.py:59
  113.1 1.0 collective-permute-start.29
  114.2 6.4 %collective-permute-done.24.refs_2_ = bf16[16,5504]{1,0:T(8,128)(2,1)S(1)} collective-permute-done((bf16[16,5504]{1,0:T(8,128)(2,1)S(1)}, bf16[16,5504]{1,0:T(8,128)(2,1)S(1)}, u32[]{:S(2)}, u32[]{:S(2)}) %collective-permute-start.24) | collective-permute-done | bytes 176160 | tf_op jit(solution)/shard_map/ppermute | solution.py:59
  122.1 2.4 %collective-permute-start.30 = (bf16[16,5504]{1,0:T(8,128)(2,1)S(1)}, bf16[16,5504]{1,0:T(8,128)(2,1)S(1)}, u32[]{:S(2)}, u32[]{:S(2)}) collective-permute-start(bf16[16,5504]{1,0:T(8,128)(2,1)S(1)} %get-tuple-element.169), channel_id=1, source_target_pairs={{0,4},{1,5},{2,6},{3,7},{4,0},{5,1},{6,2},{7,3},{8,12},{9,13},{10,... | collective-permute-start | bytes 528392 | tf_op jit(solution)/shard_map/ppermute | solution.py:59
  126.2 8.6 %collective-permute-done.33.refs_2_ = bf16[16,5504]{1,0:T(8,128)(2,1)S(1)} collective-permute-done((bf16[16,5504]{1,0:T(8,128)(2,1)S(1)}, bf16[16,5504]{1,0:T(8,128)(2,1)S(1)}, u32[]{:S(2)}, u32[]{:S(2)}) %collective-permute-start.33) | collective-permute-done | bytes 176160 | tf_op jit(solution)/shard_map/ppermute | solution.py:59
  134.8 3.7 %collective-permute-done.30.refs_9_ = bf16[16,5504]{1,0:T(8,128)(2,1)S(1)} collective-permute-done((bf16[16,5504]{1,0:T(8,128)(2,1)S(1)}, bf16[16,5504]{1,0:T(8,128)(2,1)S(1)}, u32[]{:S(2)}, u32[]{:S(2)}) %collective-permute-start.30) | collective-permute-done | bytes 176160 | tf_op jit(solution)/shard_map/ppermute | solution.py:59
  139.8 2.0 %shard_map.105 = (bf16[16,5504]{1,0:T(8,128)(2,1)S(1)}, bf16[16,5504]{1,0:T(8,128)(2,1)S(1)}, bf16[16,5504]{1,0:T(8,128)(2,1)S(1)}) custom-call(bf16[336,2560]{1,0:T(8,128)(2,1)S(1)} %pad_maximum_fusion.refs_5_.refs_0_, bf16[336,2560]{1,0:T(8,128)(2,1)S(1)} %collective-permute-done.refs_1_, bf16[240,2560]{1,0:T(8,128)(2,1)S(1)} %pad_maximum_fusion.1.refs_6_.refs_2_, ...), custom_call_target="tpu_custom_call" | custom-call | flops 566231040 | bytes 7249920 | tf_op jit(solution)/shard_map/pallas_call | solution.py:71
  141.8 3.5 %collective-permute-done.35.refs_10_ = bf16[16,5504]{1,0:T(8,128)(2,1)S(1)} collective-permute-done((bf16[16,5504]{1,0:T(8,128)(2,1)S(1)}, bf16[16,5504]{1,0:T(8,128)(2,1)S(1)}, u32[]{:S(2)}, u32[]{:S(2)}) %collective-permute-start.35) | collective-permute-done | bytes 176160 | tf_op jit(solution)/shard_map/ppermute | solution.py:59
  145.4 2.0 %shard_map.107 = (bf16[16,5504]{1,0:T(8,128)(2,1)S(1)}, bf16[16,5504]{1,0:T(8,128)(2,1)S(1)}, bf16[16,5504]{1,0:T(8,128)(2,1)S(1)}) custom-call(bf16[336,2560]{1,0:T(8,128)(2,1)S(1)} %pad_maximum_fusion.refs_5_.refs_0_, bf16[336,2560]{1,0:T(8,128)(2,1)S(1)} %collective-permute-done.refs_1_, bf16[240,2560]{1,0:T(8,128)(2,1)S(1)} %pad_maximum_fusion.1.refs_6_.refs_2_, ...), custom_call_target="tpu_custom_call" | custom-call | flops 566231040 | bytes 7249920 | tf_op jit(solution)/shard_map/pallas_call | solution.py:71
  147.7 1.8 %collective-permute-start.37 = (bf16[16,5504]{1,0:T(8,128)(2,1)S(1)}, bf16[16,5504]{1,0:T(8,128)(2,1)S(1)}, u32[]{:S(2)}, u32[]{:S(2)}) collective-permute-start(bf16[16,5504]{1,0:T(8,128)(2,1)S(1)} %get-tuple-element.196), channel_id=1, source_target_pairs={{0,1},{1,0},{2,3},{3,2},{4,5},{5,4},{6,7},{7,6},{8,9},{9,8},{10,11... | collective-permute-start | bytes 528392 | tf_op jit(solution)/shard_map/ppermute | solution.py:59
  150.3 2.5 %collective-permute-done.36 = bf16[16,5504]{1,0:T(8,128)(2,1)S(1)} collective-permute-done((bf16[16,5504]{1,0:T(8,128)(2,1)S(1)}, bf16[16,5504]{1,0:T(8,128)(2,1)S(1)}, u32[]{:S(2)}, u32[]{:S(2)}) %collective-permute-start.36) | collective-permute-done | bytes 176160 | tf_op jit(solution)/shard_map/ppermute | solution.py:59
  153.2 2.5 %collective-permute-start.40 = (bf16[16,5504]{1,0:T(8,128)(2,1)S(1)}, bf16[16,5504]{1,0:T(8,128)(2,1)S(1)}, u32[]{:S(2)}, u32[]{:S(2)}) collective-permute-start(bf16[16,5504]{1,0:T(8,128)(2,1)S(1)} %add_convert_fusion), channel_id=1, source_target_pairs={{0,4},{1,5},{2,6},{3,7},{4,0},{5,1},{6,2},{7,3},{8,12},{9,13},{10,... | collective-permute-start | bytes 528392 | tf_op jit(solution)/shard_map/ppermute | solution.py:59
  156.0 1.2 collective-permute-start.42
  157.2 1.7 %collective-permute-start.38 = (bf16[16,5504]{1,0:T(8,128)(2,1)S(1)}, bf16[16,5504]{1,0:T(8,128)(2,1)S(1)}, u32[]{:S(2)}, u32[]{:S(2)}) collective-permute-start(bf16[16,5504]{1,0:T(8,128)(2,1)S(1)} %get-tuple-element.197), channel_id=1, source_target_pairs={{0,2},{1,3},{2,0},{3,1},{4,6},{5,7},{6,4},{7,5},{8,10},{9,11},{10,... | collective-permute-start | bytes 528392 | tf_op jit(solution)/shard_map/ppermute | solution.py:59
  159.8 1.3 collective-permute-done.40
  161.1 2.9 %collective-permute-done.41.refs_5_ = bf16[16,5504]{1,0:T(8,128)(2,1)S(1)} collective-permute-done((bf16[16,5504]{1,0:T(8,128)(2,1)S(1)}, bf16[16,5504]{1,0:T(8,128)(2,1)S(1)}, u32[]{:S(2)}, u32[]{:S(2)}) %collective-permute-start.41) | collective-permute-done | bytes 176160 | tf_op jit(solution)/shard_map/ppermute | solution.py:59
  164.0 1.3 shard_map.108.refs_6_
  166.9 1.1 shard_map.109
  (82 shorter events, 25.7 us)
Async XLA Ops:
  3.1 45.2 %collective-permute-start = (bf16[336,2560]{1,0:T(8,128)(2,1)S(1)}, bf16[336,2560]{1,0:T(8,128)(2,1)S(1)}, u32[]{:S(2)}, u32[]{:S(2)}) collective-permute-start(bf16[336,2560]{1,0:T(8,128)(2,1)S(1)} %pad_maximum_fusion.refs_5_.refs_0_), channel_id=1, source_target_pairs={{0,1},{1,0},{2,3},{3,2},{4,5},{5,4},{6,7},{7,6},{8,9},{9,8},{10,11... | collective-permute-start | bytes 5160968 | tf_op jit(solution)/shard_map/ppermute | solution.py:59
  7.2 2.9 %copy-start.1 = (bf16[1,64,2560]{2,1,0:T(8,128)(2,1)S(1)}, bf16[1,64,2560]{2,1,0:T(8,128)(2,1)}, u32[]{:S(2)}) copy-start(bf16[1,64,2560]{2,1,0:T(8,128)(2,1)} %param.15) | copy-start | bytes 983044
  7.2 2.9 %copy-start.2 = (bf16[1,64,2560]{2,1,0:T(8,128)(2,1)S(1)}, bf16[1,64,2560]{2,1,0:T(8,128)(2,1)}, u32[]{:S(2)}) copy-start(bf16[1,64,2560]{2,1,0:T(8,128)(2,1)} %param.8) | copy-start | bytes 983044
  7.2 2.9 %copy-start.3 = (f32[1,2560]{1,0:T(1,128)S(1)}, f32[1,2560]{1,0:T(1,128)}, u32[]{:S(2)}) copy-start(f32[1,2560]{1,0:T(1,128)} %refs_3_.3) | copy-start | bytes 30724
  7.2 2.9 %copy-start.4 = (s32[1,2,64,1]{2,3,1,0:T(1,128)S(1)}, s32[1,2,64,1]{2,3,1,0:T(1,128)}, u32[]{:S(2)}) copy-start(s32[1,2,64,1]{2,3,1,0:T(1,128)} %param.13) | copy-start | bytes 1540
  7.2 2.8 %copy-start.5 = (f32[1,2,64,1]{2,3,1,0:T(1,128)S(1)}, f32[1,2,64,1]{2,3,1,0:T(1,128)}, u32[]{:S(2)}) copy-start(f32[1,2,64,1]{2,3,1,0:T(1,128)} %param.14) | copy-start | bytes 1540
  8.4 39.9 %collective-permute-start.1 = (bf16[240,2560]{1,0:T(8,128)(2,1)S(1)}, bf16[240,2560]{1,0:T(8,128)(2,1)S(1)}, u32[]{:S(2)}, u32[]{:S(2)}) collective-permute-start(bf16[240,2560]{1,0:T(8,128)(2,1)S(1)} %pad_maximum_fusion.1.refs_6_.refs_2_), channel_id=1, source_target_pairs={{0,2},{1,3},{2,0},{3,1},{4,6},{5,7},{6,4},{7,5},{8,10},{9,11},{10,... | collective-permute-start | bytes 3686408 | tf_op jit(solution)/shard_map/ppermute | solution.py:59
  10.9 37.4 %collective-permute-start.2 = (bf16[32,5504]{1,0:T(8,128)(2,1)S(1)}, bf16[32,5504]{1,0:T(8,128)(2,1)S(1)}, u32[]{:S(2)}, u32[]{:S(2)}) collective-permute-start(bf16[32,5504]{1,0:T(8,128)(2,1)S(1)} %get-tuple-element.103), channel_id=1, source_target_pairs={{0,4},{1,5},{2,6},{3,7},{4,0},{5,1},{6,2},{7,3},{8,12},{9,13},{10,... | collective-permute-start | bytes 1056776 | tf_op jit(solution)/shard_map/ppermute | solution.py:59
  13.6 33.9 %collective-permute-start.4 = (bf16[16,5504]{1,0:T(8,128)(2,1)S(1)}, bf16[16,5504]{1,0:T(8,128)(2,1)S(1)}, u32[]{:S(2)}, u32[]{:S(2)}) collective-permute-start(bf16[16,5504]{1,0:T(8,128)(2,1)S(1)} %get-tuple-element.124.refs_5_), channel_id=1, source_target_pairs={{0,1},{1,0},{2,3},{3,2},{4,5},{5,4},{6,7},{7,6},{8,9},{9,8},{10,11... | collective-permute-start | bytes 528392 | tf_op jit(solution)/shard_map/ppermute | solution.py:59
  14.1 34.2 %collective-permute-start.3 = (bf16[16,5504]{1,0:T(8,128)(2,1)S(1)}, bf16[16,5504]{1,0:T(8,128)(2,1)S(1)}, u32[]{:S(2)}, u32[]{:S(2)}) collective-permute-start(bf16[16,5504]{1,0:T(8,128)(2,1)S(1)} %get-tuple-element.124.refs_5_), channel_id=1, source_target_pairs={{0,2},{1,3},{2,0},{3,1},{4,6},{5,7},{6,4},{7,5},{8,10},{9,11},{10,... | collective-permute-start | bytes 528392 | tf_op jit(solution)/shard_map/ppermute | solution.py:59
  48.3 5.5 %collective-permute-start.6 = (bf16[16,5504]{1,0:T(8,128)(2,1)S(1)}, bf16[16,5504]{1,0:T(8,128)(2,1)S(1)}, u32[]{:S(2)}, u32[]{:S(2)}) collective-permute-start(bf16[16,5504]{1,0:T(8,128)(2,1)S(1)} %get-tuple-element.112.refs_5_), channel_id=1, source_target_pairs={{0,1},{1,0},{2,3},{3,2},{4,5},{5,4},{6,7},{7,6},{8,9},{9,8},{10,11... | collective-permute-start | bytes 528392 | tf_op jit(solution)/shard_map/ppermute | solution.py:59
  49.3 5.5 %collective-permute-start.5 = (bf16[16,5504]{1,0:T(8,128)(2,1)S(1)}, bf16[16,5504]{1,0:T(8,128)(2,1)S(1)}, u32[]{:S(2)}, u32[]{:S(2)}) collective-permute-start(bf16[16,5504]{1,0:T(8,128)(2,1)S(1)} %get-tuple-element.112.refs_5_), channel_id=1, source_target_pairs={{0,2},{1,3},{2,0},{3,1},{4,6},{5,7},{6,4},{7,5},{8,10},{9,11},{10,... | collective-permute-start | bytes 528392 | tf_op jit(solution)/shard_map/ppermute | solution.py:59
  57.2 7.3 %collective-permute-start.8 = (bf16[16,5504]{1,0:T(8,128)(2,1)S(1)}, bf16[16,5504]{1,0:T(8,128)(2,1)S(1)}, u32[]{:S(2)}, u32[]{:S(2)}) collective-permute-start(bf16[16,5504]{1,0:T(8,128)(2,1)S(1)} %get-tuple-element.121.refs_7_), channel_id=1, source_target_pairs={{0,2},{1,3},{2,0},{3,1},{4,6},{5,7},{6,4},{7,5},{8,10},{9,11},{10,... | collective-permute-start | bytes 528392 | tf_op jit(solution)/shard_map/ppermute | solution.py:59
  58.9 7.4 %collective-permute-start.9 = (bf16[16,5504]{1,0:T(8,128)(2,1)S(1)}, bf16[16,5504]{1,0:T(8,128)(2,1)S(1)}, u32[]{:S(2)}, u32[]{:S(2)}) collective-permute-start(bf16[16,5504]{1,0:T(8,128)(2,1)S(1)} %get-tuple-element.122), channel_id=1, source_target_pairs={{0,1},{1,0},{2,3},{3,2},{4,5},{5,4},{6,7},{7,6},{8,9},{9,8},{10,11... | collective-permute-start | bytes 528392 | tf_op jit(solution)/shard_map/ppermute | solution.py:59
  60.0 10.3 %collective-permute-start.12 = (bf16[32,5504]{1,0:T(8,128)(2,1)S(1)}, bf16[32,5504]{1,0:T(8,128)(2,1)S(1)}, u32[]{:S(2)}, u32[]{:S(2)}) collective-permute-start(bf16[32,5504]{1,0:T(8,128)(2,1)S(1)} %pad_maximum_fusion.2.refs_5_), channel_id=1, source_target_pairs={{0,1},{1,0},{2,3},{3,2},{4,5},{5,4},{6,7},{7,6},{8,9},{9,8},{10,11... | collective-permute-start | bytes 1056776 | tf_op jit(solution)/shard_map/ppermute | solution.py:59
  60.9 9.4 %collective-permute-start.11 = (bf16[32,5504]{1,0:T(8,128)(2,1)S(1)}, bf16[32,5504]{1,0:T(8,128)(2,1)S(1)}, u32[]{:S(2)}, u32[]{:S(2)}) collective-permute-start(bf16[32,5504]{1,0:T(8,128)(2,1)S(1)} %pad_maximum_fusion.2.refs_5_), channel_id=1, source_target_pairs={{0,2},{1,3},{2,0},{3,1},{4,6},{5,7},{6,4},{7,5},{8,10},{9,11},{10,... | collective-permute-start | bytes 1056776 | tf_op jit(solution)/shard_map/ppermute | solution.py:59
  61.3 17.3 %collective-permute-start.7 = (bf16[80,2560]{1,0:T(8,128)(2,1)S(1)}, bf16[80,2560]{1,0:T(8,128)(2,1)S(1)}, u32[]{:S(2)}, u32[]{:S(2)}) collective-permute-start(bf16[80,2560]{1,0:T(8,128)(2,1)S(1)} %get-tuple-element.118), channel_id=1, source_target_pairs={{0,8},{1,9},{2,10},{3,11},{4,12},{5,13},{6,14},{7,15},{8,16},{9,17... | collective-permute-start | bytes 1228808 | tf_op jit(solution)/shard_map/ppermute | solution.py:59
  66.3 12.3 %collective-permute-start.10 = (bf16[16,5504]{1,0:T(8,128)(2,1)S(1)}, bf16[16,5504]{1,0:T(8,128)(2,1)S(1)}, u32[]{:S(2)}, u32[]{:S(2)}) collective-permute-start(bf16[16,5504]{1,0:T(8,128)(2,1)S(1)} %add_convert_fusion.3), channel_id=1, source_target_pairs={{0,12},{1,13},{2,14},{3,15},{4,8},{5,9},{6,10},{7,11},{8,20},{9,21... | collective-permute-start | bytes 528392 | tf_op jit(solution)/shard_map/ppermute | solution.py:59
  70.3 9.5 %collective-permute-start.13 = (bf16[16,5504]{1,0:T(8,128)(2,1)S(1)}, bf16[16,5504]{1,0:T(8,128)(2,1)S(1)}, u32[]{:S(2)}, u32[]{:S(2)}) collective-permute-start(bf16[16,5504]{1,0:T(8,128)(2,1)S(1)} %get-tuple-element.130), channel_id=1, source_target_pairs={{0,10},{1,11},{2,8},{3,9},{4,14},{5,15},{6,12},{7,13},{8,18},{9,19... | collective-permute-start | bytes 528392 | tf_op jit(solution)/shard_map/ppermute | solution.py:59
  70.3 9.5 %collective-permute-start.14 = (bf16[16,5504]{1,0:T(8,128)(2,1)S(1)}, bf16[16,5504]{1,0:T(8,128)(2,1)S(1)}, u32[]{:S(2)}, u32[]{:S(2)}) collective-permute-start(bf16[16,5504]{1,0:T(8,128)(2,1)S(1)} %get-tuple-element.131), channel_id=1, source_target_pairs={{0,9},{1,8},{2,11},{3,10},{4,13},{5,12},{6,15},{7,14},{8,17},{9,16... | collective-permute-start | bytes 528392 | tf_op jit(solution)/shard_map/ppermute | solution.py:59
  72.3 8.7 %collective-permute-start.15 = (bf16[16,5504]{1,0:T(8,128)(2,1)S(1)}, bf16[16,5504]{1,0:T(8,128)(2,1)S(1)}, u32[]{:S(2)}, u32[]{:S(2)}) collective-permute-start(bf16[16,5504]{1,0:T(8,128)(2,1)S(1)} %get-tuple-element.132), channel_id=1, source_target_pairs={{0,8},{1,9},{2,10},{3,11},{4,12},{5,13},{6,14},{7,15},{8,16},{9,17... | collective-permute-start | bytes 528392 | tf_op jit(solution)/shard_map/ppermute | solution.py:59
  81.9 10.8 %collective-permute-start.17 = (bf16[16,5504]{1,0:T(8,128)(2,1)S(1)}, bf16[16,5504]{1,0:T(8,128)(2,1)S(1)}, u32[]{:S(2)}, u32[]{:S(2)}) collective-permute-start(bf16[16,5504]{1,0:T(8,128)(2,1)S(1)} %get-tuple-element.143), channel_id=1, source_target_pairs={{0,4},{1,5},{2,6},{3,7},{4,0},{5,1},{6,2},{7,3},{8,12},{9,13},{10,... | collective-permute-start | bytes 528392 | tf_op jit(solution)/shard_map/ppermute | solution.py:59
  83.8 8.9 %collective-permute-start.19 = (bf16[16,5504]{1,0:T(8,128)(2,1)S(1)}, bf16[16,5504]{1,0:T(8,128)(2,1)S(1)}, u32[]{:S(2)}, u32[]{:S(2)}) collective-permute-start(bf16[16,5504]{1,0:T(8,128)(2,1)S(1)} %get-tuple-element.144.refs_9_), channel_id=1, source_target_pairs={{0,1},{1,0},{2,3},{3,2},{4,5},{5,4},{6,7},{7,6},{8,9},{9,8},{10,11... | collective-permute-start | bytes 528392 | tf_op jit(solution)/shard_map/ppermute | solution.py:59
  84.3 9.1 %collective-permute-start.18 = (bf16[16,5504]{1,0:T(8,128)(2,1)S(1)}, bf16[16,5504]{1,0:T(8,128)(2,1)S(1)}, u32[]{:S(2)}, u32[]{:S(2)}) collective-permute-start(bf16[16,5504]{1,0:T(8,128)(2,1)S(1)} %get-tuple-element.144.refs_9_), channel_id=1, source_target_pairs={{0,2},{1,3},{2,0},{3,1},{4,6},{5,7},{6,4},{7,5},{8,10},{9,11},{10,... | collective-permute-start | bytes 528392 | tf_op jit(solution)/shard_map/ppermute | solution.py:59
  93.4 5.7 %collective-permute-start.21 = (bf16[16,5504]{1,0:T(8,128)(2,1)S(1)}, bf16[16,5504]{1,0:T(8,128)(2,1)S(1)}, u32[]{:S(2)}, u32[]{:S(2)}) collective-permute-start(bf16[16,5504]{1,0:T(8,128)(2,1)S(1)} %collective-permute-done.17.refs_9_), channel_id=1, source_target_pairs={{0,1},{1,0},{2,3},{3,2},{4,5},{5,4},{6,7},{7,6},{8,9},{9,8},{10,11... | collective-permute-start | bytes 528392 | tf_op jit(solution)/shard_map/ppermute | solution.py:59
  94.4 5.5 %collective-permute-start.20 = (bf16[16,5504]{1,0:T(8,128)(2,1)S(1)}, bf16[16,5504]{1,0:T(8,128)(2,1)S(1)}, u32[]{:S(2)}, u32[]{:S(2)}) collective-permute-start(bf16[16,5504]{1,0:T(8,128)(2,1)S(1)} %collective-permute-done.17.refs_9_), channel_id=1, source_target_pairs={{0,2},{1,3},{2,0},{3,1},{4,6},{5,7},{6,4},{7,5},{8,10},{9,11},{10,... | collective-permute-start | bytes 528392 | tf_op jit(solution)/shard_map/ppermute | solution.py:59
  102.5 5.5 %collective-permute-start.22 = (bf16[16,5504]{1,0:T(8,128)(2,1)S(1)}, bf16[16,5504]{1,0:T(8,128)(2,1)S(1)}, u32[]{:S(2)}, u32[]{:S(2)}) collective-permute-start(bf16[16,5504]{1,0:T(8,128)(2,1)S(1)} %get-tuple-element.154), channel_id=1, source_target_pairs={{0,2},{1,3},{2,0},{3,1},{4,6},{5,7},{6,4},{7,5},{8,10},{9,11},{10,... | collective-permute-start | bytes 528392 | tf_op jit(solution)/shard_map/ppermute | solution.py:59
  103.5 5.5 %collective-permute-start.23 = (bf16[16,5504]{1,0:T(8,128)(2,1)S(1)}, bf16[16,5504]{1,0:T(8,128)(2,1)S(1)}, u32[]{:S(2)}, u32[]{:S(2)}) collective-permute-start(bf16[16,5504]{1,0:T(8,128)(2,1)S(1)} %get-tuple-element.155), channel_id=1, source_target_pairs={{0,1},{1,0},{2,3},{3,2},{4,5},{5,4},{6,7},{7,6},{8,9},{9,8},{10,11... | collective-permute-start | bytes 528392 | tf_op jit(solution)/shard_map/ppermute | solution.py:59
  104.6 16.5 %collective-permute-start.16 = (bf16[144,2560]{1,0:T(8,128)(2,1)S(1)}, bf16[144,2560]{1,0:T(8,128)(2,1)S(1)}, u32[]{:S(2)}, u32[]{:S(2)}) collective-permute-start(bf16[144,2560]{1,0:T(8,128)(2,1)S(1)} %get-tuple-element.134), channel_id=1, source_target_pairs={{0,24},{1,25},{2,26},{3,27},{4,28},{5,29},{6,30},{7,31},{8,0},{9,1... | collective-permute-start | bytes 2211848 | tf_op jit(solution)/shard_map/ppermute | solution.py:59
  105.4 6.9 %collective-permute-start.25 = (bf16[16,5504]{1,0:T(8,128)(2,1)S(1)}, bf16[16,5504]{1,0:T(8,128)(2,1)S(1)}, u32[]{:S(2)}, u32[]{:S(2)}) collective-permute-start(bf16[16,5504]{1,0:T(8,128)(2,1)S(1)} %get-tuple-element.161), channel_id=1, source_target_pairs={{0,2},{1,3},{2,0},{3,1},{4,6},{5,7},{6,4},{7,5},{8,10},{9,11},{10,... | collective-permute-start | bytes 528392 | tf_op jit(solution)/shard_map/ppermute | solution.py:59
  106.5 6.6 %collective-permute-start.26 = (bf16[16,5504]{1,0:T(8,128)(2,1)S(1)}, bf16[16,5504]{1,0:T(8,128)(2,1)S(1)}, u32[]{:S(2)}, u32[]{:S(2)}) collective-permute-start(bf16[16,5504]{1,0:T(8,128)(2,1)S(1)} %get-tuple-element.162), channel_id=1, source_target_pairs={{0,1},{1,0},{2,3},{3,2},{4,5},{5,4},{6,7},{7,6},{8,9},{9,8},{10,11... | collective-permute-start | bytes 528392 | tf_op jit(solution)/shard_map/ppermute | solution.py:59
  109.1 11.5 %collective-permute-start.24 = (bf16[16,5504]{1,0:T(8,128)(2,1)S(1)}, bf16[16,5504]{1,0:T(8,128)(2,1)S(1)}, u32[]{:S(2)}, u32[]{:S(2)}) collective-permute-start(bf16[16,5504]{1,0:T(8,128)(2,1)S(1)} %add_convert_fusion.2), channel_id=1, source_target_pairs={{0,28},{1,29},{2,30},{3,31},{4,24},{5,25},{6,26},{7,27},{8,4},{9,5... | collective-permute-start | bytes 528392 | tf_op jit(solution)/shard_map/ppermute | solution.py:59
  109.5 11.1 %collective-permute-start.27 = (bf16[16,5504]{1,0:T(8,128)(2,1)S(1)}, bf16[16,5504]{1,0:T(8,128)(2,1)S(1)}, u32[]{:S(2)}, u32[]{:S(2)}) collective-permute-start(bf16[16,5504]{1,0:T(8,128)(2,1)S(1)} %get-tuple-element.166.refs_11_), channel_id=1, source_target_pairs={{0,26},{1,27},{2,24},{3,25},{4,30},{5,31},{6,28},{7,29},{8,2},{9,3... | collective-permute-start | bytes 528392 | tf_op jit(solution)/shard_map/ppermute | solution.py:59
  112.3 8.2 %collective-permute-start.28 = (bf16[16,5504]{1,0:T(8,128)(2,1)S(1)}, bf16[16,5504]{1,0:T(8,128)(2,1)S(1)}, u32[]{:S(2)}, u32[]{:S(2)}) collective-permute-start(bf16[16,5504]{1,0:T(8,128)(2,1)S(1)} %get-tuple-element.167), channel_id=1, source_target_pairs={{0,25},{1,24},{2,27},{3,26},{4,29},{5,28},{6,31},{7,30},{8,1},{9,0... | collective-permute-start | bytes 528392 | tf_op jit(solution)/shard_map/ppermute | solution.py:59
  113.1 8.0 %collective-permute-start.29 = (bf16[16,5504]{1,0:T(8,128)(2,1)S(1)}, bf16[16,5504]{1,0:T(8,128)(2,1)S(1)}, u32[]{:S(2)}, u32[]{:S(2)}) collective-permute-start(bf16[16,5504]{1,0:T(8,128)(2,1)S(1)} %get-tuple-element.168), channel_id=1, source_target_pairs={{0,24},{1,25},{2,26},{3,27},{4,28},{5,29},{6,30},{7,31},{8,0},{9,1... | collective-permute-start | bytes 528392 | tf_op jit(solution)/shard_map/ppermute | solution.py:59
  120.5 14.2 %collective-permute-start.33 = (bf16[16,5504]{1,0:T(8,128)(2,1)S(1)}, bf16[16,5504]{1,0:T(8,128)(2,1)S(1)}, u32[]{:S(2)}, u32[]{:S(2)}) collective-permute-start(bf16[16,5504]{1,0:T(8,128)(2,1)S(1)} %add_convert_fusion.1), channel_id=1, source_target_pairs={{0,4},{1,5},{2,6},{3,7},{4,0},{5,1},{6,2},{7,3},{8,12},{9,13},{10,... | collective-permute-start | bytes 528392 | tf_op jit(solution)/shard_map/ppermute | solution.py:59
  122.1 16.4 %collective-permute-start.30 = (bf16[16,5504]{1,0:T(8,128)(2,1)S(1)}, bf16[16,5504]{1,0:T(8,128)(2,1)S(1)}, u32[]{:S(2)}, u32[]{:S(2)}) collective-permute-start(bf16[16,5504]{1,0:T(8,128)(2,1)S(1)} %get-tuple-element.169), channel_id=1, source_target_pairs={{0,4},{1,5},{2,6},{3,7},{4,0},{5,1},{6,2},{7,3},{8,12},{9,13},{10,... | collective-permute-start | bytes 528392 | tf_op jit(solution)/shard_map/ppermute | solution.py:59
  124.5 14.0 %collective-permute-start.32 = (bf16[16,5504]{1,0:T(8,128)(2,1)S(1)}, bf16[16,5504]{1,0:T(8,128)(2,1)S(1)}, u32[]{:S(2)}, u32[]{:S(2)}) collective-permute-start(bf16[16,5504]{1,0:T(8,128)(2,1)S(1)} %get-tuple-element.170.refs_9_), channel_id=1, source_target_pairs={{0,1},{1,0},{2,3},{3,2},{4,5},{5,4},{6,7},{7,6},{8,9},{9,8},{10,11... | collective-permute-start | bytes 528392 | tf_op jit(solution)/shard_map/ppermute | solution.py:59
  125.4 14.1 %collective-permute-start.31 = (bf16[16,5504]{1,0:T(8,128)(2,1)S(1)}, bf16[16,5504]{1,0:T(8,128)(2,1)S(1)}, u32[]{:S(2)}, u32[]{:S(2)}) collective-permute-start(bf16[16,5504]{1,0:T(8,128)(2,1)S(1)} %get-tuple-element.170.refs_9_), channel_id=1, source_target_pairs={{0,2},{1,3},{2,0},{3,1},{4,6},{5,7},{6,4},{7,5},{8,10},{9,11},{10,... | collective-permute-start | bytes 528392 | tf_op jit(solution)/shard_map/ppermute | solution.py:59
  139.5 5.9 %collective-permute-start.35 = (bf16[16,5504]{1,0:T(8,128)(2,1)S(1)}, bf16[16,5504]{1,0:T(8,128)(2,1)S(1)}, u32[]{:S(2)}, u32[]{:S(2)}) collective-permute-start(bf16[16,5504]{1,0:T(8,128)(2,1)S(1)} %collective-permute-done.30.refs_9_), channel_id=1, source_target_pairs={{0,1},{1,0},{2,3},{3,2},{4,5},{5,4},{6,7},{7,6},{8,9},{9,8},{10,11... | collective-permute-start | bytes 528392 | tf_op jit(solution)/shard_map/ppermute | solution.py:59
  139.8 5.5 %collective-permute-start.34 = (bf16[16,5504]{1,0:T(8,128)(2,1)S(1)}, bf16[16,5504]{1,0:T(8,128)(2,1)S(1)}, u32[]{:S(2)}, u32[]{:S(2)}) collective-permute-start(bf16[16,5504]{1,0:T(8,128)(2,1)S(1)} %collective-permute-done.30.refs_9_), channel_id=1, source_target_pairs={{0,2},{1,3},{2,0},{3,1},{4,6},{5,7},{6,4},{7,5},{8,10},{9,11},{10,... | collective-permute-start | bytes 528392 | tf_op jit(solution)/shard_map/ppermute | solution.py:59
  147.4 5.5 %collective-permute-start.36 = (bf16[16,5504]{1,0:T(8,128)(2,1)S(1)}, bf16[16,5504]{1,0:T(8,128)(2,1)S(1)}, u32[]{:S(2)}, u32[]{:S(2)}) collective-permute-start(bf16[16,5504]{1,0:T(8,128)(2,1)S(1)} %get-tuple-element.195), channel_id=1, source_target_pairs={{0,2},{1,3},{2,0},{3,1},{4,6},{5,7},{6,4},{7,5},{8,10},{9,11},{10,... | collective-permute-start | bytes 528392 | tf_op jit(solution)/shard_map/ppermute | solution.py:59
  147.7 5.5 %collective-permute-start.37 = (bf16[16,5504]{1,0:T(8,128)(2,1)S(1)}, bf16[16,5504]{1,0:T(8,128)(2,1)S(1)}, u32[]{:S(2)}, u32[]{:S(2)}) collective-permute-start(bf16[16,5504]{1,0:T(8,128)(2,1)S(1)} %get-tuple-element.196), channel_id=1, source_target_pairs={{0,1},{1,0},{2,3},{3,2},{4,5},{5,4},{6,7},{7,6},{8,9},{9,8},{10,11... | collective-permute-start | bytes 528392 | tf_op jit(solution)/shard_map/ppermute | solution.py:59
  153.2 7.8 %collective-permute-start.40 = (bf16[16,5504]{1,0:T(8,128)(2,1)S(1)}, bf16[16,5504]{1,0:T(8,128)(2,1)S(1)}, u32[]{:S(2)}, u32[]{:S(2)}) collective-permute-start(bf16[16,5504]{1,0:T(8,128)(2,1)S(1)} %add_convert_fusion), channel_id=1, source_target_pairs={{0,4},{1,5},{2,6},{3,7},{4,0},{5,1},{6,2},{7,3},{8,12},{9,13},{10,... | collective-permute-start | bytes 528392 | tf_op jit(solution)/shard_map/ppermute | solution.py:59
  155.7 8.3 %collective-permute-start.41 = (bf16[16,5504]{1,0:T(8,128)(2,1)S(1)}, bf16[16,5504]{1,0:T(8,128)(2,1)S(1)}, u32[]{:S(2)}, u32[]{:S(2)}) collective-permute-start(bf16[16,5504]{1,0:T(8,128)(2,1)S(1)} %get-tuple-element.201.refs_11_), channel_id=1, source_target_pairs={{0,2},{1,3},{2,0},{3,1},{4,6},{5,7},{6,4},{7,5},{8,10},{9,11},{10,... | collective-permute-start | bytes 528392 | tf_op jit(solution)/shard_map/ppermute | solution.py:59
  156.0 8.0 %collective-permute-start.42 = (bf16[16,5504]{1,0:T(8,128)(2,1)S(1)}, bf16[16,5504]{1,0:T(8,128)(2,1)S(1)}, u32[]{:S(2)}, u32[]{:S(2)}) collective-permute-start(bf16[16,5504]{1,0:T(8,128)(2,1)S(1)} %get-tuple-element.202), channel_id=1, source_target_pairs={{0,1},{1,0},{2,3},{3,2},{4,5},{5,4},{6,7},{7,6},{8,9},{9,8},{10,11... | collective-permute-start | bytes 528392 | tf_op jit(solution)/shard_map/ppermute | solution.py:59
  157.2 8.7 %collective-permute-start.38 = (bf16[16,5504]{1,0:T(8,128)(2,1)S(1)}, bf16[16,5504]{1,0:T(8,128)(2,1)S(1)}, u32[]{:S(2)}, u32[]{:S(2)}) collective-permute-start(bf16[16,5504]{1,0:T(8,128)(2,1)S(1)} %get-tuple-element.197), channel_id=1, source_target_pairs={{0,2},{1,3},{2,0},{3,1},{4,6},{5,7},{6,4},{7,5},{8,10},{9,11},{10,... | collective-permute-start | bytes 528392 | tf_op jit(solution)/shard_map/ppermute | solution.py:59
  158.9 6.9 %collective-permute-start.39 = (bf16[16,5504]{1,0:T(8,128)(2,1)S(1)}, bf16[16,5504]{1,0:T(8,128)(2,1)S(1)}, u32[]{:S(2)}, u32[]{:S(2)}) collective-permute-start(bf16[16,5504]{1,0:T(8,128)(2,1)S(1)} %get-tuple-element.198), channel_id=1, source_target_pairs={{0,1},{1,0},{2,3},{3,2},{4,5},{5,4},{6,7},{7,6},{8,9},{9,8},{10,11... | collective-permute-start | bytes 528392 | tf_op jit(solution)/shard_map/ppermute | solution.py:59
  (2 other events, 3.3 us)
